TPU v7x, 128 devices: a whole 4x4x4 slice. The times are simulated.
128 devices in a mesh: row: 8 (over x, y_lo), col: 16 (over y_hi, z, core).
Axes of the slice: x: 4, y: 4 (y_hi: 2, y_lo: 2; y = y_hi * 2 + y_lo), z: 4, core: 2. Of those that a mesh axis runs over, the one named last changes fastest.
Arguments:
- tokens: bfloat16 [1024, 6144], P('row', 'col'), may hold values from -6 to 6
- w_in: bfloat16 [6144, 24576], P('col', 'row'), may hold values from -0.078125 to 0.078125
- w_out: bfloat16 [24576, 6144], P('row', 'col'), may hold values from -0.0390625 to 0.0390625
- out_grad: bfloat16 [1024, 6144], P('row', 'col'), may hold values from -6 to 6
Outputs:
- in_grad: bfloat16 [1024, 6144], P('row', 'col')
- w_in_grad: float32 [6144, 24576], P('col', 'row')
- w_out_grad: float32 [24576, 6144], P('row', 'col')
All inputs are finite; a program needn't handle non-finite values.
Results may differ from a plain program's by a relative error of at most 0.028.
Values may be sent and summed in bfloat16 or wider, within the bound.
No kernel may reach another device: no remote copies, remote signals or barrier semaphores. Data moves between devices by JAX's collectives and lax.ppermute only.
A program may use at most 128 MiB of HBM per device.

v0:
```python
import jax
import jax.numpy as jnp
from jax import lax
from jax.sharding import PartitionSpec as P

inv_root_two = 0.7071067811865476
inv_root_two_pi = 0.3989422804014327


def gelu_value(values):
    return 0.5 * values * (1.0 + jax.scipy.special.erf(values * inv_root_two))


def gelu_slope(values):
    return (
        0.5 * (1.0 + jax.scipy.special.erf(values * inv_root_two))
        + values * jnp.exp(-0.5 * values * values) * inv_root_two_pi
    )


def body(tokens, w_in, w_out, out_grad):
    tok_panel, grad_panel = (
        lax.all_gather(tokens, "row", axis=0, tiled=True),
        lax.all_gather(out_grad, "row", axis=0, tiled=True),
    )
    part_rows = tok_panel
    hidden = lax.psum_scatter(
        jnp.dot(part_rows, w_in, preferred_element_type=jnp.float32).astype(jnp.bfloat16),
        "col",
        scatter_dimension=0,
        tiled=True,
    ).astype(jnp.float32)
    gelu_share = gelu_value(hidden).astype(jnp.bfloat16)
    gelu_out = lax.all_gather(gelu_share, "col", axis=0, tiled=True)
    w_out_grad = lax.dot_general(
        gelu_out, grad_panel, (((0,), (0,)), ((), ())), preferred_element_type=jnp.float32
    )
    part_rows = grad_panel
    hidden_grad = lax.psum_scatter(
        lax.dot_general(
            part_rows, w_out, (((1,), (1,)), ((), ())), preferred_element_type=jnp.float32
        ).astype(jnp.bfloat16),
        "col",
        scatter_dimension=0,
        tiled=True,
    ).astype(jnp.float32)
    pre_share = (hidden_grad * gelu_slope(hidden)).astype(jnp.bfloat16)
    pre_grad = lax.all_gather(pre_share, "col", axis=0, tiled=True)
    w_in_grad = lax.dot_general(
        tok_panel, pre_grad, (((0,), (0,)), ((), ())), preferred_element_type=jnp.float32
    )
    part_rows = pre_grad
    in_grad = lax.psum_scatter(
        lax.dot_general(
            part_rows, w_in, (((1,), (1,)), ((), ())), preferred_element_type=jnp.float32
        ).astype(jnp.bfloat16),
        "row",
        scatter_dimension=0,
        tiled=True,
    )
    return (in_grad, w_in_grad, w_out_grad)


def solution(mesh):
    in_specs = (P("row", "col"), P("col", "row"), P("row", "col"), P("row", "col"))
    out_specs = (P("row", "col"), P("col", "row"), P("row", "col"))
    return jax.shard_map(body, mesh=mesh, in_specs=in_specs, out_specs=out_specs, check_vma=False)
```

profile of v0, /device:TPU:1, one launch (start us, length us, event | category | flops | bytes accessed | tf_op | source)
XLA Modules:
  0.0 399.8 jit_solution(6518281266809792072)
XLA Ops:
  7.2 0.0 copy-start
  7.2 0.0 reduce-scatter.6.cloned.1.call-start
  7.2 25.9 %all_gather.13 = bf16[1024,384]{1,0:T(8,128)(2,1)S(1)} all-gather(bf16[128,384]{1,0:T(8,128)(2,1)} %param.4), channel_id=1, replica_groups=mesh['row'=8,'col'=16] {'row'}, dimensions={0}, use_global_device_ids=true | all-gather | bytes 884736 | tf_op jit(solution)/shard_map/all_gather | solution.py:23
  33.1 0.0 copy-done
  33.1 0.0 copy-start.3
  33.1 5.3 %convolution_convert_fusion = bf16[1024,3072]{1,0:T(8,128)(2,1)} fusion(bf16[1024,384]{1,0:T(8,128)(2,1)S(1)} %all_gather.13, bf16[384,3072]{1,0:T(8,128)(2,1)S(1)} %copy-done), kind=kOutput, calls=%fused_computation | convolution fusion | flops 2419064832 | bytes 9437184 | tf_op jit(solution)/shard_map/dot_general | solution.py:28
  38.4 0.0 reduce-scatter.6.cloned.1.call-update
  38.5 0.0 reduce-scatter.4.cloned.1.call-start
  38.5 0.0 copy-done.3
  38.5 24.0 %all_gather.12 = bf16[1024,384]{1,0:T(8,128)(2,1)S(1)} all-gather(bf16[128,384]{1,0:T(8,128)(2,1)S(1)} %copy-done.3), channel_id=1, replica_groups=mesh['row'=8,'col'=16] {'row'}, dimensions={0}, use_global_device_ids=true | all-gather | bytes 884736 | tf_op jit(solution)/shard_map/all_gather | solution.py:24
  62.5 0.0 copy-start.1
  62.5 0.9 copy-done.1
  63.5 7.2 %convolution_convert_fusion.1 = bf16[1024,3072]{1,0:T(8,128)(2,1)} fusion(bf16[1024,384]{1,0:T(8,128)(2,1)S(1)} %all_gather.12, bf16[3072,384]{1,0:T(8,128)(2,1)} %param.6), kind=kOutput, calls=%fused_computation.1 | convolution fusion | flops 2419064832 | bytes 9437184 | tf_op jit(solution)/shard_map/dot_general | solution.py:40
  70.7 0.0 reduce-scatter.4.cloned.1.call-update
  70.7 0.0 all-gather.3.cloned.1.call-start
  70.7 63.6 %reduce-scatter.6.cloned.1.call-done = bf16[64,3072]{1,0:T(8,128)(2,1)} async-done(((bf16[1024,3072]{1,0:T(8,128)(2,1)}), bf16[64,3072]{1,0:T(8,128)(2,1)}) %reduce-scatter.6.cloned.1.call-update) | async-done | bytes 393232 | tf_op jit(solution)/shard_map/reduce_scatter | solution.py:27
  134.3 93.3 %reduce-scatter.4.cloned.1.call-done = bf16[64,3072]{1,0:T(8,128)(2,1)} async-done(((bf16[1024,3072]{1,0:T(8,128)(2,1)}), bf16[64,3072]{1,0:T(8,128)(2,1)}) %reduce-scatter.4.cloned.1.call-update) | async-done | bytes 393232 | tf_op jit(solution)/shard_map/reduce_scatter | solution.py:39
  227.6 2.4 fusion.8
  230.1 0.0 all-gather.3.cloned.1.call-update
  230.1 0.0 all-gather.5.cloned.1.call-start
  230.1 0.5 all-gather.5.cloned.1.call-update
  230.7 0.2 reduce-scatter.8.cloned.1.call-start
  230.9 64.4 %all-gather.3.cloned.1.call-done = bf16[1024,3072]{1,0:T(8,128)(2,1)} async-done(((bf16[64,3072]{1,0:T(8,128)(2,1)}), bf16[1024,3072]{1,0:T(8,128)(2,1)}) %all-gather.3.cloned.1.call-update) | async-done | bytes 6291472 | tf_op jit(solution)/shard_map/all_gather | solution.py:48
  295.3 6.5 %convolution_convert_fusion.2 = bf16[1024,384]{1,0:T(8,128)(2,1)} fusion(bf16[1024,3072]{1,0:T(8,128)(2,1)} %all-gather.3.cloned.1.call-done, bf16[384,3072]{1,0:T(8,128)(2,1)S(1)} %copy-done), kind=kOutput, calls=%fused_computation.8 | convolution fusion | flops 2416312320 | bytes 9437184 | tf_op jit(solution)/shard_map/dot_general | solution.py:54
  301.8 0.0 reduce-scatter.8.cloned.1.call-update
  301.8 8.5 %convolution_bitcast_fusion = f32[384,3072]{0,1:T(8,128)} fusion(bf16[1024,3072]{1,0:T(8,128)(2,1)} %all-gather.3.cloned.1.call-done, bf16[1024,384]{1,0:T(8,128)(2,1)S(1)} %all_gather.13), kind=kOutput, calls=%fused_computation.2 | convolution fusion | flops 2415919104 | bytes 11796480 | tf_op jit(solution)/shard_map/dot_general | solution.py:49
  310.3 0.0 copy-start.2
  310.3 6.1 %copy.7 = f32[384,3072]{1,0:T(8,128)} copy(f32[384,3072]{0,1:T(8,128)} %convolution_bitcast_fusion) | data formatting | bytes 9437184
  316.5 43.2 %all-gather.5.cloned.1.call-done = bf16[1024,3072]{1,0:T(8,128)(2,1)} async-done(((bf16[64,3072]{1,0:T(8,128)(2,1)}), bf16[1024,3072]{1,0:T(8,128)(2,1)}) %all-gather.5.cloned.1.call-update) | async-done | bytes 6291472 | tf_op jit(solution)/shard_map/all_gather | solution.py:34
  359.6 0.0 copy-done.2
  359.6 8.4 %fusion.9 = f32[3072,384]{1,0:T(8,128)} fusion(bf16[1024,3072]{1,0:T(8,128)(2,1)} %all-gather.5.cloned.1.call-done, bf16[1024,384]{1,0:T(8,128)(2,1)S(1)} %copy-done.2), kind=kOutput, calls=%fused_computation.18 | convolution fusion | flops 2415919104 | bytes 11796480 | tf_op jit(solution)/shard_map/dot_general | solution.py:35
  368.1 25.2 %reduce-scatter.8.cloned.1.call-done = bf16[128,384]{1,0:T(8,128)(2,1)} async-done(((bf16[1024,384]{1,0:T(8,128)(2,1)}), bf16[128,384]{1,0:T(8,128)(2,1)}) %reduce-scatter.8.cloned.1.call-update) | async-done | bytes 98320 | tf_op jit(solution)/shard_map/reduce_scatter | solution.py:53
Async XLA Ops:
  7.2 25.9 %copy-start = (bf16[384,3072]{1,0:T(8,128)(2,1)S(1)}, bf16[384,3072]{1,0:T(8,128)(2,1)}, u32[]{:S(2)}) copy-start(bf16[384,3072]{1,0:T(8,128)(2,1)} %param.5) | copy-start | bytes 7077892
  7.2 127.1 %reduce-scatter.6.cloned.1.call-start = ((), (), s32[]{:S(2)}) async-start(), calls=%async_computation.4 | async-start | bytes 6684672 | tf_op jit(solution)/shard_map/reduce_scatter | solution.py:27
  33.1 5.4 %copy-start.3 = (bf16[128,384]{1,0:T(8,128)(2,1)S(1)}, bf16[128,384]{1,0:T(8,128)(2,1)}, u32[]{:S(2)}) copy-start(bf16[128,384]{1,0:T(8,128)(2,1)} %param.7) | copy-start | bytes 294916
  38.5 189.2 %reduce-scatter.4.cloned.1.call-start = ((), (), s32[]{:S(2)}) async-start(), calls=%async_computation.3 | async-start | bytes 6684672 | tf_op jit(solution)/shard_map/reduce_scatter | solution.py:39
  62.5 0.9 copy-start.1
  70.7 224.6 %all-gather.3.cloned.1.call-start = ((), (), s32[]{:S(2)}) async-start(), calls=%async_computation.5 | async-start | bytes 6684672 | tf_op jit(solution)/shard_map/all_gather | solution.py:48
  230.1 129.5 %all-gather.5.cloned.1.call-start = ((), (), s32[]{:S(2)}) async-start(), calls=%async_computation.7 | async-start | bytes 6684672 | tf_op jit(solution)/shard_map/all_gather | solution.py:34
  230.7 162.6 %reduce-scatter.8.cloned.1.call-start = ((), (), s32[]{:S(2)}) async-start(), calls=%async_computation.6 | async-start | bytes 884736 | tf_op jit(solution)/shard_map/reduce_scatter | solution.py:53
  310.3 49.3 %copy-start.2 = (bf16[1024,384]{1,0:T(8,128)(2,1)S(1)}, bf16[1024,384]{1,0:T(8,128)(2,1)}, u32[]{:S(2)}) copy-start(bf16[1024,384]{1,0:T(8,128)(2,1)} %copy-done.1) | copy-start | bytes 2359300
Sparse Core Ops, SparseCore 0:
  38.6 95.6 reduce-scatter.5
  139.1 88.5 reduce-scatter.3
  230.7 64.5 all-gather.2
  297.7 61.9 all-gather.4
  362.4 30.8 reduce-scatter.7
where the time goes:
time: 404 us; the launch traced here: 400 us
  waiting for transfers between devices  290 us (72%)
  blocking collectives  49.9 us (12%)
  matrix products  36 us (9%)
  between operations  13.8 us (3%)
  local copies, waits for them, and re-layouts  7.1 us (2%)
    reduce_scatter x1, waiting for transfers between devices, body(): lax.psum_scatter(lax.dot_general(part_rows, w_out, (((1,), (1,)), ((), ()...  93.3 us
    all_gather x1, waiting for transfers between devices, body(): pre_grad = lax.all_gather(pre_share, 'col', axis=0, tiled=True)  64.4 us
    reduce_scatter x1, waiting for transfers between devices, body(): lax.psum_scatter(jnp.dot(part_rows, w_in, preferred_element_type=jnp.floa...  63.6 us
    all_gather x1, waiting for transfers between devices, body(): gelu_out = lax.all_gather(gelu_share, 'col', axis=0, tiled=True)  43.2 us
    all_gather x1, blocking collectives, body(): lax.all_gather(tokens, 'row', axis=0, tiled=True)  25.9 us
    reduce_scatter x1, waiting for transfers between devices, body(): lax.psum_scatter(lax.dot_general(part_rows, w_in, (((1,), (1,)), ((), ())...  25.2 us
    all_gather x1, blocking collectives, body(): lax.all_gather(out_grad, 'row', axis=0, tiled=True)  24 us
    dot_general x1, matrix products, body(): lax.dot_general(tok_panel, pre_grad, (((0,), (0,)), ((), ())), preferred_...  8.5 us
  transfers between devices with their start and end apart: 5, of which 5 were waited for; matrix products, arithmetic and copies ran while one was open for 9% of the time, Pallas kernels for 0%

commit v1 on v0

v1 whole, which is shorter than its diff:
```python
import jax
import jax.numpy as jnp
from jax import lax
from jax.experimental import pallas as pl
from jax.experimental.pallas import tpu as pltpu
from jax.sharding import PartitionSpec as P

inv_root_two = 0.7071067811865476
inv_root_two_pi = 0.3989422804014327
AXES = ("row", "col")


def gelu_value(values):
    return 0.5 * values * (1.0 + jax.scipy.special.erf(values * inv_root_two))


def gelu_slope(values):
    return (
        0.5 * (1.0 + jax.scipy.special.erf(values * inv_root_two))
        + values * jnp.exp(-0.5 * values * values) * inv_root_two_pi
    )


def device_index(x, y, z, core):
    return (x * 2 + y % 2) * 16 + (y // 2) * 8 + z * 2 + core


def flip_pairs(x_flip=0, y_flip=0, z_flip=0, core_flip=0):
    return [
        (
            device_index(x, y, z, core),
            device_index(x ^ x_flip, y ^ y_flip, z ^ z_flip, core ^ core_flip),
        )
        for x in range(4)
        for y in range(4)
        for z in range(4)
        for core in range(2)
    ]


FLIPS = {
    "a": flip_pairs(z_flip=1),
    "b": flip_pairs(z_flip=3),
    "y": flip_pairs(y_flip=2),
    "core": flip_pairs(core_flip=1),
    "xa": flip_pairs(x_flip=1),
    "xb": flip_pairs(x_flip=3),
    "yl": flip_pairs(y_flip=1),
}
TOKEN_ORDERS = ("aby", "bay")
Z_GROUPS = [[y * 8 + z * 2 + core for z in range(4)] for y in range(2) for core in range(2)]


def swap(values, name):
    return lax.ppermute(values, AXES, FLIPS[name])


def after(first, then):
    return lax.optimization_barrier((first, then))[1]


def f32(values):
    return values.astype(jnp.float32)


def b16(values):
    return values.astype(jnp.bfloat16)


TILE = 512
VMEM_LIMIT = 16 * 1024 * 1024
CORE, Z, Y_HI, ROW = range(4)
IN_VMEM = pl.BlockSpec(memory_space=pltpu.VMEM)


def kernel_call(kernel, place, args, out_specs, out_shape, scratch=()):
    return pl.pallas_call(
        kernel,
        in_specs=[pl.BlockSpec(memory_space=pltpu.SMEM)] + [IN_VMEM] * len(args),
        out_specs=out_specs,
        out_shape=out_shape,
        scratch_shapes=scratch,
        compiler_params=pltpu.CompilerParams(vmem_limit_bytes=VMEM_LIMIT),
        cost_estimate=pl.CostEstimate(flops=0, bytes_accessed=0, transcendentals=0),
    )(place, *args)


def copies_for_row(place, out_grad, tokens):
    rows, depth = tokens.shape
    own = rows // 8

    def kernel(place_ref, grad_ref, tok_ref, out_ref):
        z, y_hi = place_ref[Z], place_ref[Y_HI]
        for i in range(8):
            first, second, third = i >> 2, (i >> 1) & 1, i & 1
            grad = grad_ref[(i & 3) * 2 + (y_hi ^ first)]
            tok = tok_ref[(z ^ first ^ (3 * second)) * 2 + (y_hi ^ third)]
            for to in range(8):
                out_ref[to, 0, i * own : (i + 1) * own] = grad
                out_ref[to, 1, i * own : (i + 1) * own] = tok

    pieces = (8, own, depth)
    out = (8, 2, rows, depth)
    return kernel_call(
        kernel,
        place,
        (out_grad.reshape(pieces), tokens.reshape(pieces)),
        IN_VMEM,
        jax.ShapeDtypeStruct(out, tokens.dtype),
    )


def grad_pieces(block):
    return [(block + r, 4 * y + z) for y in range(2) for z in range(4) for r in range(4)]


def token_pieces(chunk, block):
    return [
        (block + r, (first * 4 + second * 2 if chunk == 0 else second * 4 + first * 2) + y)
        for first in range(2)
        for second in range(2)
        for y in range(2)
        for r in range(4)
    ]


def partial_sums(place, raw, raw_other, kind, pieces, weight, weight_other, hidden_axis):
    rows, depth = raw.shape[2:]
    own = rows // 8
    total_rows = own * len(pieces)
    half = total_rows // 2
    width = weight_other.shape[hidden_axis]
    tile = min(TILE, width)
    dims = (((1,), (1 - hidden_axis,)), ((), ()))

    def kernel(place_ref, l_ref, lo_ref, w_ref, wo_ref, keep_ref, send_ref, left):
        for i, (block, piece) in enumerate(pieces):
            left[i * own : (i + 1) * own, :depth] = l_ref[block, kind, piece * own : (piece + 1) * own]
            left[i * own : (i + 1) * own, depth:] = lo_ref[block, kind, piece * own : (piece + 1) * own]
        for start in range(0, width, tile):
            mine = pl.ds(pl.multiple_of(place_ref[CORE] * width + start, tile), tile)
            if hidden_axis == 1:
                right = jnp.concatenate([w_ref[:, mine], wo_ref[:, start : start + tile]])
            else:
                right = jnp.concatenate([w_ref[mine, :], wo_ref[start : start + tile, :]], axis=1)
            total = lax.dot_general(left[...], right, dims, preferred_element_type=jnp.float32)
            total = total.astype(jnp.bfloat16)
            keep_ref[:, start : start + tile] = total[:half]
            send_ref[:, start : start + tile] = total[half:]

    out = jax.ShapeDtypeStruct((half, width), jnp.bfloat16)
    return kernel_call(
        kernel,
        place,
        (raw, raw_other, weight, weight_other),
        [IN_VMEM, IN_VMEM],
        [out, out],
        [pltpu.VMEM((total_rows, 2 * depth), jnp.bfloat16)],
    )


def input_total(place, parts):
    count, rows, depth = parts.shape
    own = rows // 8

    def kernel(place_ref, parts_ref, out_ref):
        z, y_hi = place_ref[Z], place_ref[Y_HI]
        swapped = place_ref[ROW] >= 4
        for i in range(8):
            first, second, y = i >> 2, (i >> 1) & 1, i & 1
            total = parts_ref[0, i * own : (i + 1) * own].astype(jnp.float32)
            for device in range(1, count):
                total += parts_ref[device, i * own : (i + 1) * own].astype(jnp.float32)
            a = jnp.where(swapped, second, first)
            b = jnp.where(swapped, first, second)
            out_ref[(z ^ a ^ (3 * b)) * 2 + (y_hi ^ y)] = total.astype(jnp.bfloat16)

    out = jax.ShapeDtypeStruct((8, own, depth), jnp.bfloat16)
    return kernel_call(kernel, place, (parts,), IN_VMEM, out).reshape(8 * own, depth)


def for_tiles(width, step):
    tile = min(128, width)

    @pl.loop(0, width // tile)
    def _(i):
        step(pl.ds(pl.multiple_of(i * tile, tile), tile))


def fold(place, kept, got, second):
    count = len(kept)
    rows, width = second[0].shape
    half = rows // 2

    def kernel(place_ref, *refs):
        own_ref, send_ref = refs[3 * count :]

        def step(at):
            for i in range(count):
                k, g, s = refs[i], refs[count + i], refs[2 * count + i]
                total = k[:rows, at].astype(jnp.float32) + g[:rows, at].astype(jnp.float32)
                total += s[:, at].astype(jnp.float32)
                own_ref[i * half : (i + 1) * half, at] = total[:half]
                send_ref[i * half : (i + 1) * half, at] = total[half:].astype(jnp.bfloat16)

        for_tiles(width, step)

    out = (count * half, width)
    return kernel_call(
        kernel,
        place,
        (*kept, *got, *second),
        [IN_VMEM, IN_VMEM],
        [jax.ShapeDtypeStruct(out, jnp.float32), jax.ShapeDtypeStruct(out, jnp.bfloat16)],
    )


def activate(place, own_sums, far):
    rows, width = own_sums.shape

    def kernel(place_ref, own_ref, far_ref, out_ref, slope_ref):
        def step(at):
            hidden = own_ref[:, at] + far_ref[:, at].astype(jnp.float32)
            gelu = gelu_value(hidden).astype(jnp.bfloat16)
            for chip in range(4):
                out_ref[chip * rows : (chip + 1) * rows, at] = gelu
            slope_ref[:, at] = gelu_slope(hidden)

        for_tiles(width, step)

    return kernel_call(
        kernel,
        place,
        (own_sums, far),
        [IN_VMEM, IN_VMEM],
        [
            jax.ShapeDtypeStruct((4 * rows, width), jnp.bfloat16),
            jax.ShapeDtypeStruct((rows, width), jnp.float32),
        ],
    )


def chain_slope(place, parts, slope):
    rows, width = slope.shape
    half = rows // len(parts)

    def kernel(place_ref, *refs):
        slope_ref, out_ref = refs[len(parts) :]

        def step(at):
            for i, part in enumerate(refs[: len(parts)]):
                total = part[:half, at].astype(jnp.float32)
                for chip in range(1, 4):
                    total += part[chip * half : (chip + 1) * half, at].astype(jnp.float32)
                here = slice(i * half, (i + 1) * half)
                out_ref[here, at] = (total * slope_ref[here, at]).astype(jnp.bfloat16)

        for_tiles(width, step)

    return kernel_call(kernel, place, (*parts, slope), IN_VMEM, jax.ShapeDtypeStruct((rows, width), jnp.bfloat16))


def features_of(place, raw, kind, pieces):
    rows, depth = raw.shape[2:]
    own = rows // 8

    def kernel(place_ref, raw_ref, out_ref):
        for g in range(0, len(pieces), 8):
            block = [raw_ref[b, kind, p * own : (p + 1) * own] for b, p in pieces[g : g + 8]]
            out_ref[:, g * own : (g + 8) * own] = jnp.concatenate(block).T

    return kernel_call(
        kernel, place, (raw,), IN_VMEM, jax.ShapeDtypeStruct((depth, own * len(pieces)), raw.dtype)
    )


def grad_scratch(tile_shape):
    return [pltpu.VMEM((2, *tile_shape), jnp.float32), pltpu.SemaphoreType.DMA((2,))]


def write_grad(core, parts_of, features, hidden_axis, out_ref, tiles, sems):
    width = parts_of[0][0].shape[1]
    tile = min(TILE, width)
    stores = [None, None]
    step = 0
    for parts, place_of in zip(parts_of, (core, 1 - core)):
        for start in range(0, width, tile):
            units = jnp.concatenate([p[:, start : start + tile] for p in parts])
            total = jnp.dot(features[...], units, preferred_element_type=jnp.float32)
            slot = step % 2
            if stores[slot] is not None:
                stores[slot].wait()
            tiles[slot] = total if hidden_axis == 1 else total.T
            to = pl.ds(pl.multiple_of(place_of * width + start, tile), tile)
            stores[slot] = pltpu.make_async_copy(
                tiles.at[slot], out_ref.at[:, to] if hidden_axis == 1 else out_ref.at[to, :], sems.at[slot]
            )
            stores[slot].start()
            step += 1
    for store in stores:
        store.wait()


def write_input_sums(core, parts_of, w_ref, out_ref, offset):
    rows, width = parts_of[0][0].shape
    own = rows // 16
    dims = (((1,), (1,)), ((), ()))
    for i in range(len(parts_of[0])):
        total = None
        for parts, place_of in zip(parts_of, (core, 1 - core)):
            units = pl.ds(pl.multiple_of(place_of * width, width), width)
            part = lax.dot_general(parts[i][...], w_ref[:, units], dims, preferred_element_type=jnp.float32)
            total = part if total is None else total + part
        total = total.astype(jnp.bfloat16)
        for k in range(16):
            at, block = offset + (k // 4) * own, 4 * i + k % 4
            out_ref[block, at : at + own] = total[k * own : (k + 1) * own]


def input_sums(place, mine, other, weight):
    count = len(mine)
    own = mine[0].shape[0] // 16

    def kernel(place_ref, *refs):
        write_input_sums(place_ref[CORE], (refs[:count], refs[count : 2 * count]), refs[-2], refs[-1], 0)

    out = jax.ShapeDtypeStruct((4 * count, 4 * own, weight.shape[0]), jnp.bfloat16)
    return kernel_call(kernel, place, (*mine, *other, weight), IN_VMEM, out)


def input_sums_and_grad(place, mine, other, weight, kept, features):
    count = len(mine)
    half = count // 2
    blocks, rows, depth = kept.shape
    width = mine[0].shape[1]

    def kernel(place_ref, *refs):
        core = place_ref[CORE]
        parts_of = (refs[:count], refs[count : 2 * count])
        w_ref, kept_ref, features_ref, sums_ref, grad_ref, *scratch = refs[2 * count :]
        sums_ref[:, :rows] = kept_ref[...]
        write_input_sums(core, [parts[half:] for parts in parts_of], w_ref, sums_ref, rows)
        write_grad(core, parts_of, features_ref, 1, grad_ref, *scratch)

    return kernel_call(
        kernel,
        place,
        (*mine, *other, weight, kept, features),
        [IN_VMEM, pl.BlockSpec(memory_space=pl.ANY)],
        [
            jax.ShapeDtypeStruct((blocks, 2 * rows, depth), jnp.bfloat16),
            jax.ShapeDtypeStruct((depth, 2 * width), jnp.float32),
        ],
        grad_scratch((depth, min(TILE, width))),
    )


def weight_grad(place, mine, other, features):
    count = len(mine)
    width = mine[0].shape[1]
    depth = features.shape[0]

    def kernel(place_ref, *refs):
        features_ref, out_ref, *scratch = refs[2 * count :]
        parts_of = (refs[:count], refs[count : 2 * count])
        write_grad(place_ref[CORE], parts_of, features_ref, 0, out_ref, *scratch)

    return kernel_call(
        kernel,
        place,
        (*mine, *other, features),
        pl.BlockSpec(memory_space=pl.ANY),
        jax.ShapeDtypeStruct((2 * width, depth), jnp.float32),
        grad_scratch((min(TILE, width), depth)),
    )


def body(tokens, w_in, w_out, out_grad):
    column, row = lax.axis_index("col"), lax.axis_index("row")
    core, z, y_hi = column % 2, (column // 2) % 4, column // 8
    place = jnp.stack([core, z, y_hi, row]).astype(jnp.int32)
    rows, depth = tokens.shape
    own = rows // 8
    width = w_in.shape[1] // 2
    half = 4 * rows
    quarter = half // 2

    copies = copies_for_row(place, out_grad, tokens)
    raw = lax.all_to_all(copies, "row", 0, 0, tiled=True)
    raw_other = swap(raw, "core")

    w_out_other = swap(lax.dynamic_slice_in_dim(w_out, (1 - core) * width, width, 0), "core")
    w_in_other = swap(lax.dynamic_slice_in_dim(w_in, (1 - core) * width, width, 1), "core")

    def grad_sums(raw, raw_other, chunk):
        return partial_sums(place, raw, raw_other, 0, grad_pieces(4 * chunk), w_out, w_out_other, 0)

    def token_sums(raw, raw_other, chunk):
        return partial_sums(place, raw, raw_other, 1, token_pieces(chunk, 4 * chunk), w_in, w_in_other, 1)

    grad_kept_1, sent_1 = grad_sums(raw, raw_other, 0)
    grad_got_1 = swap(sent_1, "y")
    then = after(sent_1, (raw, raw_other))
    tok_kept, tok_sent = zip(*[token_sums(*then, chunk) for chunk in range(2)])
    tok_got = [swap(sent, order[0]) for sent, order in zip(tok_sent, TOKEN_ORDERS)]
    grad_kept_2, sent_2 = grad_sums(*after(tok_sent, then), 1)
    grad_got_2 = swap(sent_2, "y")

    def z_terms(kept, got):
        parts = b16(f32(kept) + f32(got))
        return lax.all_to_all(parts, "col", 0, 0, axis_index_groups=Z_GROUPS, tiled=True)

    q = quarter // 2
    terms = [z_terms(grad_kept_1, grad_got_1)]
    tok_got = after((grad_got_1, sent_2), tok_got)
    second = [
        swap(b16(f32(k[q:]) + f32(g[q:])), order[1]) for k, g, order in zip(tok_kept, tok_got, TOKEN_ORDERS)
    ]
    second = after((grad_got_2, terms[0]), second)
    own_sums, to_send = fold(place, tok_kept, tok_got, second)
    far = swap(to_send, "y")
    terms.append(z_terms(grad_kept_2, grad_got_2))
    q = quarter // 4

    keep_pieces = token_pieces(0, 0)[:16] + token_pieces(1, 4)[:16]
    first_pieces = token_pieces(0, 0)[16:] + token_pieces(1, 4)[16:]
    grad_order = [(r, 4 * y + z) for y in range(2) for z in range(4) for r in range(8)]
    raw = after(to_send, raw)
    tok_features = features_of(place, raw, 1, keep_pieces + first_pieces)
    grad_features = features_of(place, raw, 0, grad_order)
    far = after((tok_features, grad_features), far)

    spread, slope = activate(place, own_sums, far)
    gelu_keep = lax.all_to_all(spread, "col", 0, 0, axis_index_groups=Z_GROUPS, tiled=True)
    pre_share = chain_slope(place, terms, slope)
    far = swap(pre_share, "y")
    two = [jnp.concatenate([pre_share[i : i + q], far[i : i + q]]) for i in (0, q)]

    gelu_keep, two = lax.optimization_barrier((gelu_keep, two))
    cuts = (0, quarter // 2, 11 * quarter // 8)
    gelu_far = [swap(gelu_keep[: cuts[1]], "y")]
    pre_keep = [jnp.concatenate([t, swap(t, order[1])]) for t, order in zip(two, TOKEN_ORDERS)]

    gelu_far[0], pre_keep, gelu_keep = lax.optimization_barrier((gelu_far[0], pre_keep, gelu_keep))
    gelu_far.append(swap(gelu_keep[cuts[1] : cuts[2]], "y"))
    pre_first = [swap(k, order[0]) for k, order in zip(pre_keep, TOKEN_ORDERS)]
    pre_keep_other = [swap(k, "core") for k in pre_keep]
    kept = input_sums(place, pre_keep, pre_keep_other, w_in)

    gelu_far[1], pre_first, kept, gelu_keep = lax.optimization_barrier((gelu_far[1], pre_first, kept, gelu_keep))
    gelu_far.append(swap(gelu_keep[cuts[2] :], "y"))
    pre_first_other = [swap(f, "core") for f in pre_first]
    sums, w_in_grad = input_sums_and_grad(
        place,
        (*pre_keep, *pre_first),
        (*pre_keep_other, *pre_first_other),
        w_in,
        kept,
        tok_features,
    )
    parts = lax.all_to_all(sums, "row", 0, 0, tiled=True)
    gelu_far[2] = after(sums, gelu_far[2])
    gelu_mine = (gelu_keep, *gelu_far)
    gelu_other = [swap(g, "core") for g in gelu_mine]
    w_out_grad = weight_grad(place, gelu_mine, gelu_other, grad_features)
    parts = after(w_out_grad, parts)
    in_grad = input_total(place, parts)
    return (in_grad, w_in_grad, w_out_grad)


def solution(mesh):
    in_specs = (P("row", "col"), P("col", "row"), P("row", "col"), P("row", "col"))
    out_specs = (P("row", "col"), P("col", "row"), P("row", "col"))
    return jax.shard_map(body, mesh=mesh, in_specs=in_specs, out_specs=out_specs, check_vma=False)
```

time: 404 us -> 209 us (0.52)
  waiting for transfers between devices: 290 us -> 96.2 us
  starting transfers between devices: 0.38 us -> 57.7 us
  blocking collectives: 49.9 us -> 0 us
  matrix products: 36 us -> 0 us
  Pallas kernels: 0 us -> 33.2 us
  between operations: 13.8 us -> 0.96 us
  other arithmetic: 2.42 us -> 9.42 us
    reduce_scatter x3 -> x0, waiting for transfers between devices: 182 us -> none  [the longest x1 93.3 us: body(): lax.psum_scatter(lax.dot_general(part_rows, w_out, (((1,), (1,)), ((), ()...]
    all_gather x2 -> x0, waiting for transfers between devices: 108 us -> none  [the longest x1 64.4 us: body(): pre_grad = lax.all_gather(pre_share, 'col', axis=0, tiled=True)]
    ppermute x0 -> x26, waiting for transfers between devices: none -> 58.2 us  [swap(): return lax.ppermute(values, AXES, FLIPS[name])]
    all_gather x2 -> x0, blocking collectives: 49.9 us -> none  [the longest x1 25.9 us: body(): lax.all_gather(tokens, 'row', axis=0, tiled=True)]
    all_to_all x0 -> x5, waiting for transfers between devices: none -> 37.9 us  [the longest x1 23 us: body(): raw = lax.all_to_all(copies, 'row', 0, 0, tiled=True)]
    dot_general x5 -> x0, matrix products: 36 us -> none  [the longest x1 8.5 us: body(): lax.dot_general(tok_panel, pre_grad, (((0,), (0,)), ((), ())), preferred_...]
    ppermute x0 -> x26, starting transfers between devices: none -> 35.7 us  [swap(): return lax.ppermute(values, AXES, FLIPS[name])]
    pallas_call x0 -> x14, Pallas kernels: none -> 33.2 us  [kernel_call(): pl.pallas_call(kernel, in_specs=[pl.BlockSpec(memory_space=pltpu.SMEM)] +...]
  transfers between devices with their start and end apart: 5 -> 31, of which waited for: 5 -> 18; matrix products, arithmetic and copies ran while one was open for 9% -> 6% of each run, Pallas kernels for 0% -> 13%
where the time goes in v1:
time: 209 us; the launch traced here: 208 us
  waiting for transfers between devices  96.2 us (46%)
  starting transfers between devices  57.7 us (28%)
  Pallas kernels  33.2 us (16%)
  local copies, waits for them, and re-layouts  10.7 us (5%)
  other arithmetic  9.42 us (5%)
    ppermute x26, waiting for transfers between devices, swap(): return lax.ppermute(values, AXES, FLIPS[name])  58.2 us
    ppermute x26, starting transfers between devices, swap(): return lax.ppermute(values, AXES, FLIPS[name])  35.7 us
    pallas_call x14, Pallas kernels, kernel_call(): pl.pallas_call(kernel, in_specs=[pl.BlockSpec(memory_space=pltpu.SMEM)] +...  33.2 us
    all_to_all x1, waiting for transfers between devices, body(): raw = lax.all_to_all(copies, 'row', 0, 0, tiled=True)  23 us
    all_to_all x1, waiting for transfers between devices, body(): lax.all_to_all(spread, 'col', 0, 0, axis_index_groups=Z_GROUPS, tiled=True)  11.9 us
    all_to_all x2, starting transfers between devices, z_terms(): lax.all_to_all(parts, 'col', 0, 0, axis_index_groups=Z_GROUPS, tiled=True)  7.69 us
    unnamed x34, local copies, waits for them, and re-layouts  7.25 us
    convert_element_type x4, other arithmetic, b16(): return values.astype(jnp.bfloat16)  6.17 us
  transfers between devices with their start and end apart: 31, of which 18 were waited for; matrix products, arithmetic and copies ran while one was open for 6% of the time, Pallas kernels for 13%

profile of v1, /device:TPU:1, one launch (start us, length us, event | category | flops | bytes accessed | tf_op | source)
XLA Modules:
  0.0 208.2 jit_solution(4624647191549298733)
XLA Ops:
  4.4 5.9 %all-to-all-start = ((bf16[8,2,128,384]{3,2,1,0:T(8,128)(2,1)}), bf16[8,2,128,384]{3,2,1,0:T(8,128)(2,1)S(1)}, u32[]{:S(2)}, u32[]{:S(2)}) async-start(bf16[8,2,128,384]{3,2,1,0:T(8,128)(2,1)} %shard_map.67), calls=%async_computation | async-start | bytes 3145728 | tf_op jit(solution)/shard_map/all_to_all | solution.py:389
  10.2 23.0 %all-to-all-done.l_ref.raw_ref = bf16[8,2,128,384]{3,2,1,0:T(8,128)(2,1)S(1)} async-done(((bf16[8,2,128,384]{3,2,1,0:T(8,128)(2,1)}), bf16[8,2,128,384]{3,2,1,0:T(8,128)(2,1)S(1)}, u32[]{:S(2)}, u32[]{:S(2)}) %all-to-all-start) | async-done | bytes 1572896 | tf_op jit(solution)/shard_map/all_to_all | solution.py:389
  37.1 2.5 %collective-permute-done.1.wo_ref = bf16[1536,384]{1,0:T(8,128)(2,1)S(1)} collective-permute-done((bf16[1536,384]{1,0:T(8,128)(2,1)S(1)}, bf16[1536,384]{1,0:T(8,128)(2,1)S(1)}, u32[]{:S(2)}, u32[]{:S(2)}) %collective-permute-start.1) | collective-permute-done | bytes 1179680 | tf_op jit(solution)/shard_map/ppermute | solution.py:55
  39.6 2.0 shard_map.68
  41.6 2.0 shard_map.70
  43.6 3.8 %collective-permute-start.5 = (bf16[256,1536]{1,0:T(8,128)(2,1)S(1)}, bf16[256,1536]{1,0:T(8,128)(2,1)S(1)}, u32[]{:S(2)}, u32[]{:S(2)}) collective-permute-start(bf16[256,1536]{1,0:T(8,128)(2,1)S(1)} %get-tuple-element.47), channel_id=1, source_target_pairs={{0,6},{1,7},{2,4},{3,5},{4,2},{5,3},{6,0},{7,1},{16,22},{17,23},{1... | collective-permute-start | bytes 2359304 | tf_op jit(solution)/shard_map/ppermute | solution.py:55
  47.4 2.0 shard_map.69
  49.5 2.7 %collective-permute-start.3 = (bf16[256,1536]{1,0:T(8,128)(2,1)S(1)}, bf16[256,1536]{1,0:T(8,128)(2,1)S(1)}, u32[]{:S(2)}, u32[]{:S(2)}) collective-permute-start(bf16[256,1536]{1,0:T(8,128)(2,1)S(1)} %get-tuple-element.41), channel_id=1, source_target_pairs={{0,8},{1,9},{2,10},{3,11},{4,12},{5,13},{6,14},{7,15},{16,24},{17,... | collective-permute-start | bytes 2359304 | tf_op jit(solution)/shard_map/ppermute | solution.py:55
  52.2 2.9 %shard_map.71 = (bf16[256,1536]{1,0:T(8,128)(2,1)S(1)}, bf16[256,1536]{1,0:T(8,128)(2,1)}) custom-call(s32[4]{0:T(128)S(1)} %pad_add_fusion.place_ref, bf16[8,2,128,384]{3,2,1,0:T(8,128)(2,1)S(1)} %all-to-all-done.l_ref.raw_ref, bf16[8,2,128,384]{3,2,1,0:T(8,128)(2,1)S(1)} %collective-permute-done.lo_ref, bf16[3072,384]{1,0:T(8,128)(2,1)S(1)} %copy-done.2, ...), custom_call_target="tpu_custom_call" | custom-call | tf_op jit(solution)/shard_map/pallas_call | solution.py:77
  55.4 9.6 %collective-permute-done.5.refs_3_ = bf16[256,1536]{1,0:T(8,128)(2,1)S(1)} collective-permute-done((bf16[256,1536]{1,0:T(8,128)(2,1)S(1)}, bf16[256,1536]{1,0:T(8,128)(2,1)S(1)}, u32[]{:S(2)}, u32[]{:S(2)}) %collective-permute-start.5) | collective-permute-done | bytes 786464 | tf_op jit(solution)/shard_map/ppermute | solution.py:55
  65.0 2.9 %collective-permute-done.4.refs_2_ = bf16[256,1536]{1,0:T(8,128)(2,1)S(1)} collective-permute-done((bf16[256,1536]{1,0:T(8,128)(2,1)S(1)}, bf16[256,1536]{1,0:T(8,128)(2,1)S(1)}, u32[]{:S(2)}, u32[]{:S(2)}) %collective-permute-start.4) | collective-permute-done | bytes 786464 | tf_op jit(solution)/shard_map/ppermute | solution.py:55
  72.5 3.5 %all-to-all-start.1 = ((bf16[4,64,1536]{2,1,0:T(8,128)(2,1)}), bf16[4,64,1536]{2,1,0:T(8,128)(2,1)S(1)}, u32[]{:S(2)}, u32[]{:S(2)}) async-start(bf16[4,64,1536]{2,1,0:T(8,128)(2,1)} %bitcast.23), calls=%async_computation.1 | async-start | bytes 1572864 | tf_op jit(solution)/shard_map/all_to_all | solution.py:411
  76.0 2.0 add_convert_fusion.3
  78.1 2.6 %collective-permute-start.7 = (bf16[128,1536]{1,0:T(8,128)(2,1)}, bf16[128,1536]{1,0:T(8,128)(2,1)}, u32[]{:S(2)}, u32[]{:S(2)}) collective-permute-start(bf16[128,1536]{1,0:T(8,128)(2,1)} %add_convert_fusion.3), channel_id=1, source_target_pairs={{0,6},{1,7},{2,4},{3,5},{4,2},{5,3},{6,0},{7,1},{16,22},{17,23},{1... | collective-permute-start | bytes 1179656 | tf_op jit(solution)/shard_map/ppermute | solution.py:55
  80.7 5.8 %collective-permute-done.6 = bf16[256,1536]{1,0:T(8,128)(2,1)} collective-permute-done((bf16[256,1536]{1,0:T(8,128)(2,1)}, bf16[256,1536]{1,0:T(8,128)(2,1)}, u32[]{:S(2)}, u32[]{:S(2)}) %collective-permute-start.6) | collective-permute-done | bytes 786464 | tf_op jit(solution)/shard_map/ppermute | solution.py:55
  86.5 2.2 %add_convert_fusion = bf16[256,1536]{1,0:T(8,128)(2,1)} fusion(bf16[256,1536]{1,0:T(8,128)(2,1)} %collective-permute-done.6, bf16[256,1536]{1,0:T(8,128)(2,1)S(1)} %copy-done.14), kind=kLoop, calls=%fused_computation | loop fusion | flops 1572864 | bytes 2359296 | tf_op jit(solution)/shard_map/convert_element_type | solution.py:67
  88.7 4.2 %all-to-all-start.3 = ((bf16[4,64,1536]{2,1,0:T(8,128)(2,1)}), bf16[4,64,1536]{2,1,0:T(8,128)(2,1)}, u32[]{:S(2)}, u32[]{:S(2)}) async-start(bf16[4,64,1536]{2,1,0:T(8,128)(2,1)} %bitcast.22), calls=%async_computation.3 | async-start | bytes 1572864 | tf_op jit(solution)/shard_map/all_to_all | solution.py:411
  98.7 2.7 %collective-permute-start.9 = (bf16[128,1536]{1,0:T(8,128)(2,1)S(1)}, bf16[128,1536]{1,0:T(8,128)(2,1)S(1)}, u32[]{:S(2)}, u32[]{:S(2)}) collective-permute-start(bf16[128,1536]{1,0:T(8,128)(2,1)S(1)} %get-tuple-element.57), channel_id=1, source_target_pairs={{0,8},{1,9},{2,10},{3,11},{4,12},{5,13},{6,14},{7,15},{16,24},{17,... | collective-permute-start | bytes 1179656 | tf_op jit(solution)/shard_map/ppermute | solution.py:55
  103.0 4.3 %collective-permute-done.9.far_ref = bf16[128,1536]{1,0:T(8,128)(2,1)S(1)} collective-permute-done((bf16[128,1536]{1,0:T(8,128)(2,1)S(1)}, bf16[128,1536]{1,0:T(8,128)(2,1)S(1)}, u32[]{:S(2)}, u32[]{:S(2)}) %collective-permute-start.9) | collective-permute-done | bytes 393248 | tf_op jit(solution)/shard_map/ppermute | solution.py:55
  111.1 2.7 %collective-permute-start.10 = (bf16[128,1536]{1,0:T(8,128)(2,1)S(1)}, bf16[128,1536]{1,0:T(8,128)(2,1)}, u32[]{:S(2)}, u32[]{:S(2)}) collective-permute-start(bf16[128,1536]{1,0:T(8,128)(2,1)S(1)} %shard_map.76), channel_id=1, source_target_pairs={{0,8},{1,9},{2,10},{3,11},{4,12},{5,13},{6,14},{7,15},{16,24},{17,... | collective-permute-start | bytes 1179656 | tf_op jit(solution)/shard_map/ppermute | solution.py:55
  113.8 5.0 %all-to-all-start.2 = ((bf16[4,128,1536]{2,1,0:T(8,128)(2,1)}), bf16[4,128,1536]{2,1,0:T(8,128)(2,1)S(1)}, u32[]{:S(2)}, u32[]{:S(2)}) async-start(bf16[4,128,1536]{2,1,0:T(8,128)(2,1)} %bitcast.19), calls=%async_computation.2 | async-start | bytes 3145728 | tf_op jit(solution)/shard_map/all_to_all | solution.py:434
  121.4 11.9 %all-to-all-done.2 = bf16[4,128,1536]{2,1,0:T(8,128)(2,1)S(1)} async-done(((bf16[4,128,1536]{2,1,0:T(8,128)(2,1)}), bf16[4,128,1536]{2,1,0:T(8,128)(2,1)S(1)}, u32[]{:S(2)}, u32[]{:S(2)}) %all-to-all-start.2) | async-done | bytes 1572896 | tf_op jit(solution)/shard_map/all_to_all | solution.py:434
  134.7 8.1 %collective-permute-done.13 = bf16[128,1536]{1,0:T(8,128)(2,1)S(1)} collective-permute-done((bf16[128,1536]{1,0:T(8,128)(2,1)}, bf16[128,1536]{1,0:T(8,128)(2,1)S(1)}, u32[]{:S(2)}, u32[]{:S(2)}) %collective-permute-start.13) | collective-permute-done | bytes 393248 | tf_op jit(solution)/shard_map/ppermute | solution.py:55
  145.6 9.8 %collective-permute-start.17 = (bf16[256,1536]{1,0:T(8,128)(2,1)S(1)}, bf16[256,1536]{1,0:T(8,128)(2,1)S(1)}, u32[]{:S(2)}, u32[]{:S(2)}) collective-permute-start(bf16[256,1536]{1,0:T(8,128)(2,1)S(1)} %pad_maximum_fusion.refs_0_), channel_id=1, source_target_pairs={{0,1},{1,0},{2,3},{3,2},{4,5},{5,4},{6,7},{7,6},{16,17},{17,16},{1... | collective-permute-start | bytes 2359304 | tf_op jit(solution)/shard_map/ppermute | solution.py:55
  158.5 2.3 %shard_map.77.refs_9_ = bf16[8,64,384]{2,1,0:T(8,128)(2,1)S(1)} custom-call(s32[4]{0:T(128)S(1)} %pad_add_fusion.place_ref, bf16[256,1536]{1,0:T(8,128)(2,1)S(1)} %pad_maximum_fusion.refs_0_, bf16[256,1536]{1,0:T(8,128)(2,1)S(1)} %pad_maximum_fusion.1.refs_1_, bf16[256,1536]{1,0:T(8,128)(2,1)S(1)} %collective-permute-done.17.refs_2_.refs_4_, ...), custom_call_target="tpu_custom_call" | custom-call | tf_op jit(solution)/shard_map/pallas_call | solution.py:77
  160.8 14.7 %collective-permute-done.14.refs_2_ = bf16[224,1536]{1,0:T(8,128)(2,1)} collective-permute-done((bf16[224,1536]{1,0:T(8,128)(2,1)S(1)}, bf16[224,1536]{1,0:T(8,128)(2,1)}, u32[]{:S(2)}, u32[]{:S(2)}) %collective-permute-start.14) | collective-permute-done | bytes 688160 | tf_op jit(solution)/shard_map/ppermute | solution.py:55
  179.3 3.0 %collective-permute-done.19.refs_6_ = bf16[256,1536]{1,0:T(8,128)(2,1)S(1)} collective-permute-done((bf16[256,1536]{1,0:T(8,128)(2,1)S(1)}, bf16[256,1536]{1,0:T(8,128)(2,1)S(1)}, u32[]{:S(2)}, u32[]{:S(2)}) %collective-permute-start.19) | collective-permute-done | bytes 786464 | tf_op jit(solution)/shard_map/ppermute | solution.py:55
  183.5 6.5 %shard_map.78 = (bf16[8,128,384]{2,1,0:T(8,128)(2,1)S(1)}, f32[384,3072]{1,0:T(8,128)}) custom-call(s32[4]{0:T(128)S(1)} %pad_add_fusion.place_ref, bf16[256,1536]{1,0:T(8,128)(2,1)S(1)} %pad_maximum_fusion.refs_0_, bf16[256,1536]{1,0:T(8,128)(2,1)S(1)} %pad_maximum_fusion.1.refs_1_, bf16[256,1536]{1,0:T(8,128)(2,1)S(1)} %collective-permute-done.15.refs_2_, ...), custom_call_target="tpu_custom_call" | custom-call | tf_op jit(solution)/shard_map/pallas_call | solution.py:77
  191.0 3.5 %all-to-all-start.4 = ((bf16[8,128,384]{2,1,0:T(8,128)(2,1)}), bf16[8,128,384]{2,1,0:T(8,128)(2,1)S(1)}, u32[]{:S(2)}, u32[]{:S(2)}) async-start(bf16[8,128,384]{2,1,0:T(8,128)(2,1)} %copy-done.12), calls=%async_computation.4 | async-start | bytes 1572864 | tf_op jit(solution)/shard_map/all_to_all | solution.py:461
  195.1 1.9 collective-permute-done.23.refs_5_
  197.0 6.9 %shard_map.79 = f32[3072,384]{1,0:T(8,128)} custom-call(s32[4]{0:T(128)S(1)} %pad_add_fusion.place_ref, bf16[512,1536]{1,0:T(8,128)(2,1)S(1)} %bitcast.17, bf16[128,1536]{1,0:T(8,128)(2,1)S(1)} %collective-permute-done.11.refs_1_, bf16[224,1536]{1,0:T(8,128)(2,1)} %collective-permute-done.14.refs_2_, bf16[160,1536]{1,0:T(8,128)(2,1)} %collective-permute-done.21.refs_3_, ...), custom_call_target="tpu_custom_call" | custom-call | tf_op jit(solution)/shard_map/pallas_call | solution.py:77
  203.9 3.0 %all-to-all-done.4.parts_ref = bf16[8,128,384]{2,1,0:T(8,128)(2,1)S(1)} async-done(((bf16[8,128,384]{2,1,0:T(8,128)(2,1)}), bf16[8,128,384]{2,1,0:T(8,128)(2,1)S(1)}, u32[]{:S(2)}, u32[]{:S(2)}) %all-to-all-start.4) | async-done | bytes 786464 | tf_op jit(solution)/shard_map/all_to_all | solution.py:461
  (93 shorter events, 41.2 us)
Async XLA Ops:
  4.4 28.9 %all-to-all-start = ((bf16[8,2,128,384]{3,2,1,0:T(8,128)(2,1)}), bf16[8,2,128,384]{3,2,1,0:T(8,128)(2,1)S(1)}, u32[]{:S(2)}, u32[]{:S(2)}) async-start(bf16[8,2,128,384]{3,2,1,0:T(8,128)(2,1)} %shard_map.67), calls=%async_computation | async-start | bytes 3145728 | tf_op jit(solution)/shard_map/all_to_all | solution.py:389
  33.3 6.4 %collective-permute-start = (bf16[8,2,128,384]{3,2,1,0:T(8,128)(2,1)S(1)}, bf16[8,2,128,384]{3,2,1,0:T(8,128)(2,1)S(1)}, u32[]{:S(2)}, u32[]{:S(2)}) collective-permute-start(bf16[8,2,128,384]{3,2,1,0:T(8,128)(2,1)S(1)} %all-to-all-done.l_ref.raw_ref), channel_id=1, source_target_pairs={{0,1},{1,0},{2,3},{3,2},{4,5},{5,4},{6,7},{7,6},{16,17},{17,16},{1... | collective-permute-start | bytes 4718600 | tf_op jit(solution)/shard_map/ppermute | solution.py:55
  36.3 3.3 %collective-permute-start.1 = (bf16[1536,384]{1,0:T(8,128)(2,1)S(1)}, bf16[1536,384]{1,0:T(8,128)(2,1)S(1)}, u32[]{:S(2)}, u32[]{:S(2)}) collective-permute-start(bf16[1536,384]{1,0:T(8,128)(2,1)S(1)} %constant_dynamic-slice_fusion.1), channel_id=1, source_target_pairs={{0,1},{1,0},{2,3},{3,2},{4,5},{5,4},{6,7},{7,6},{16,17},{17,16},{1... | collective-permute-start | bytes 3538952 | tf_op jit(solution)/shard_map/ppermute | solution.py:55
  36.6 5.0 %collective-permute-start.2 = (bf16[384,1536]{1,0:T(8,128)(2,1)S(1)}, bf16[384,1536]{1,0:T(8,128)(2,1)S(1)}, u32[]{:S(2)}, u32[]{:S(2)}) collective-permute-start(bf16[384,1536]{1,0:T(8,128)(2,1)S(1)} %constant_dynamic-slice_fusion), channel_id=1, source_target_pairs={{0,1},{1,0},{2,3},{3,2},{4,5},{5,4},{6,7},{7,6},{16,17},{17,16},{1... | collective-permute-start | bytes 3538952 | tf_op jit(solution)/shard_map/ppermute | solution.py:55
  43.6 21.4 %collective-permute-start.5 = (bf16[256,1536]{1,0:T(8,128)(2,1)S(1)}, bf16[256,1536]{1,0:T(8,128)(2,1)S(1)}, u32[]{:S(2)}, u32[]{:S(2)}) collective-permute-start(bf16[256,1536]{1,0:T(8,128)(2,1)S(1)} %get-tuple-element.47), channel_id=1, source_target_pairs={{0,6},{1,7},{2,4},{3,5},{4,2},{5,3},{6,0},{7,1},{16,22},{17,23},{1... | collective-permute-start | bytes 2359304 | tf_op jit(solution)/shard_map/ppermute | solution.py:55
  49.4 18.5 %collective-permute-start.4 = (bf16[256,1536]{1,0:T(8,128)(2,1)S(1)}, bf16[256,1536]{1,0:T(8,128)(2,1)S(1)}, u32[]{:S(2)}, u32[]{:S(2)}) collective-permute-start(bf16[256,1536]{1,0:T(8,128)(2,1)S(1)} %get-tuple-element.46), channel_id=1, source_target_pairs={{0,2},{1,3},{2,0},{3,1},{4,6},{5,7},{6,4},{7,5},{16,18},{17,19},{1... | collective-permute-start | bytes 2359304 | tf_op jit(solution)/shard_map/ppermute | solution.py:55
  49.5 20.0 %collective-permute-start.3 = (bf16[256,1536]{1,0:T(8,128)(2,1)S(1)}, bf16[256,1536]{1,0:T(8,128)(2,1)S(1)}, u32[]{:S(2)}, u32[]{:S(2)}) collective-permute-start(bf16[256,1536]{1,0:T(8,128)(2,1)S(1)} %get-tuple-element.41), channel_id=1, source_target_pairs={{0,8},{1,9},{2,10},{3,11},{4,12},{5,13},{6,14},{7,15},{16,24},{17,... | collective-permute-start | bytes 2359304 | tf_op jit(solution)/shard_map/ppermute | solution.py:55
  55.1 17.4 %copy-start.13 = (bf16[256,1536]{1,0:T(8,128)(2,1)}, bf16[256,1536]{1,0:T(8,128)(2,1)S(1)}, u32[]{:S(2)}) copy-start(bf16[256,1536]{1,0:T(8,128)(2,1)S(1)} %get-tuple-element.61) | copy-start | bytes 2359300
  55.1 31.4 %collective-permute-start.6 = (bf16[256,1536]{1,0:T(8,128)(2,1)}, bf16[256,1536]{1,0:T(8,128)(2,1)}, u32[]{:S(2)}, u32[]{:S(2)}) collective-permute-start(bf16[256,1536]{1,0:T(8,128)(2,1)} %get-tuple-element.50), channel_id=1, source_target_pairs={{0,8},{1,9},{2,10},{3,11},{4,12},{5,13},{6,14},{7,15},{16,24},{17,... | collective-permute-start | bytes 2359304 | tf_op jit(solution)/shard_map/ppermute | solution.py:55
  70.4 22.5 %collective-permute-start.8 = (bf16[128,1536]{1,0:T(8,128)(2,1)}, bf16[128,1536]{1,0:T(8,128)(2,1)S(1)}, u32[]{:S(2)}, u32[]{:S(2)}) collective-permute-start(bf16[128,1536]{1,0:T(8,128)(2,1)} %add_convert_fusion.2), channel_id=1, source_target_pairs={{0,2},{1,3},{2,0},{3,1},{4,6},{5,7},{6,4},{7,5},{16,18},{17,19},{1... | collective-permute-start | bytes 1179656 | tf_op jit(solution)/shard_map/ppermute | solution.py:55
  72.5 16.2 %all-to-all-start.1 = ((bf16[4,64,1536]{2,1,0:T(8,128)(2,1)}), bf16[4,64,1536]{2,1,0:T(8,128)(2,1)S(1)}, u32[]{:S(2)}, u32[]{:S(2)}) async-start(bf16[4,64,1536]{2,1,0:T(8,128)(2,1)} %bitcast.23), calls=%async_computation.1 | async-start | bytes 1572864 | tf_op jit(solution)/shard_map/all_to_all | solution.py:411
  78.1 15.8 %collective-permute-start.7 = (bf16[128,1536]{1,0:T(8,128)(2,1)}, bf16[128,1536]{1,0:T(8,128)(2,1)}, u32[]{:S(2)}, u32[]{:S(2)}) collective-permute-start(bf16[128,1536]{1,0:T(8,128)(2,1)} %add_convert_fusion.3), channel_id=1, source_target_pairs={{0,6},{1,7},{2,4},{3,5},{4,2},{5,3},{6,0},{7,1},{16,22},{17,23},{1... | collective-permute-start | bytes 1179656 | tf_op jit(solution)/shard_map/ppermute | solution.py:55
  88.7 20.9 %all-to-all-start.3 = ((bf16[4,64,1536]{2,1,0:T(8,128)(2,1)}), bf16[4,64,1536]{2,1,0:T(8,128)(2,1)}, u32[]{:S(2)}, u32[]{:S(2)}) async-start(bf16[4,64,1536]{2,1,0:T(8,128)(2,1)} %bitcast.22), calls=%async_computation.3 | async-start | bytes 1572864 | tf_op jit(solution)/shard_map/all_to_all | solution.py:411
  98.7 8.6 %collective-permute-start.9 = (bf16[128,1536]{1,0:T(8,128)(2,1)S(1)}, bf16[128,1536]{1,0:T(8,128)(2,1)S(1)}, u32[]{:S(2)}, u32[]{:S(2)}) collective-permute-start(bf16[128,1536]{1,0:T(8,128)(2,1)S(1)} %get-tuple-element.57), channel_id=1, source_target_pairs={{0,8},{1,9},{2,10},{3,11},{4,12},{5,13},{6,14},{7,15},{16,24},{17,... | collective-permute-start | bytes 1179656 | tf_op jit(solution)/shard_map/ppermute | solution.py:55
  111.1 8.3 %collective-permute-start.10 = (bf16[128,1536]{1,0:T(8,128)(2,1)S(1)}, bf16[128,1536]{1,0:T(8,128)(2,1)}, u32[]{:S(2)}, u32[]{:S(2)}) collective-permute-start(bf16[128,1536]{1,0:T(8,128)(2,1)S(1)} %shard_map.76), channel_id=1, source_target_pairs={{0,8},{1,9},{2,10},{3,11},{4,12},{5,13},{6,14},{7,15},{16,24},{17,... | collective-permute-start | bytes 1179656 | tf_op jit(solution)/shard_map/ppermute | solution.py:55
  113.8 19.5 %all-to-all-start.2 = ((bf16[4,128,1536]{2,1,0:T(8,128)(2,1)}), bf16[4,128,1536]{2,1,0:T(8,128)(2,1)S(1)}, u32[]{:S(2)}, u32[]{:S(2)}) async-start(bf16[4,128,1536]{2,1,0:T(8,128)(2,1)} %bitcast.19), calls=%async_computation.2 | async-start | bytes 3145728 | tf_op jit(solution)/shard_map/all_to_all | solution.py:434
  133.3 9.5 %collective-permute-start.13 = (bf16[128,1536]{1,0:T(8,128)(2,1)}, bf16[128,1536]{1,0:T(8,128)(2,1)S(1)}, u32[]{:S(2)}, u32[]{:S(2)}) collective-permute-start(bf16[128,1536]{1,0:T(8,128)(2,1)} %get-tuple-element.65), channel_id=1, source_target_pairs={{0,2},{1,3},{2,0},{3,1},{4,6},{5,7},{6,4},{7,5},{16,18},{17,19},{1... | collective-permute-start | bytes 1179656 | tf_op jit(solution)/shard_map/ppermute | solution.py:55
  133.6 10.8 %collective-permute-start.12 = (bf16[128,1536]{1,0:T(8,128)(2,1)}, bf16[128,1536]{1,0:T(8,128)(2,1)S(1)}, u32[]{:S(2)}, u32[]{:S(2)}) collective-permute-start(bf16[128,1536]{1,0:T(8,128)(2,1)} %get-tuple-element.64), channel_id=1, source_target_pairs={{0,6},{1,7},{2,4},{3,5},{4,2},{5,3},{6,0},{7,1},{16,22},{17,23},{1... | collective-permute-start | bytes 1179656 | tf_op jit(solution)/shard_map/ppermute | solution.py:55
  134.2 11.4 %collective-permute-start.11 = (bf16[128,1536]{1,0:T(8,128)(2,1)S(1)}, bf16[128,1536]{1,0:T(8,128)(2,1)S(1)}, u32[]{:S(2)}, u32[]{:S(2)}) collective-permute-start(bf16[128,1536]{1,0:T(8,128)(2,1)S(1)} %slice.41), channel_id=1, source_target_pairs={{0,8},{1,9},{2,10},{3,11},{4,12},{5,13},{6,14},{7,15},{16,24},{17,... | collective-permute-start | bytes 1179656 | tf_op jit(solution)/shard_map/ppermute | solution.py:55
  145.6 12.5 %collective-permute-start.17 = (bf16[256,1536]{1,0:T(8,128)(2,1)S(1)}, bf16[256,1536]{1,0:T(8,128)(2,1)S(1)}, u32[]{:S(2)}, u32[]{:S(2)}) collective-permute-start(bf16[256,1536]{1,0:T(8,128)(2,1)S(1)} %pad_maximum_fusion.refs_0_), channel_id=1, source_target_pairs={{0,1},{1,0},{2,3},{3,2},{4,5},{5,4},{6,7},{7,6},{16,17},{17,16},{1... | collective-permute-start | bytes 2359304 | tf_op jit(solution)/shard_map/ppermute | solution.py:55
  155.5 3.0 %collective-permute-start.18 = (bf16[256,1536]{1,0:T(8,128)(2,1)S(1)}, bf16[256,1536]{1,0:T(8,128)(2,1)S(1)}, u32[]{:S(2)}, u32[]{:S(2)}) collective-permute-start(bf16[256,1536]{1,0:T(8,128)(2,1)S(1)} %pad_maximum_fusion.1.refs_1_), channel_id=1, source_target_pairs={{0,1},{1,0},{2,3},{3,2},{4,5},{5,4},{6,7},{7,6},{16,17},{17,16},{1... | collective-permute-start | bytes 2359304 | tf_op jit(solution)/shard_map/ppermute | solution.py:55
  155.5 20.0 %collective-permute-start.15 = (bf16[256,1536]{1,0:T(8,128)(2,1)S(1)}, bf16[256,1536]{1,0:T(8,128)(2,1)S(1)}, u32[]{:S(2)}, u32[]{:S(2)}) collective-permute-start(bf16[256,1536]{1,0:T(8,128)(2,1)S(1)} %pad_maximum_fusion.refs_0_), channel_id=1, source_target_pairs={{0,2},{1,3},{2,0},{3,1},{4,6},{5,7},{6,4},{7,5},{16,18},{17,19},{1... | collective-permute-start | bytes 2359304 | tf_op jit(solution)/shard_map/ppermute | solution.py:55
  155.6 20.0 %collective-permute-start.16 = (bf16[256,1536]{1,0:T(8,128)(2,1)S(1)}, bf16[256,1536]{1,0:T(8,128)(2,1)S(1)}, u32[]{:S(2)}, u32[]{:S(2)}) collective-permute-start(bf16[256,1536]{1,0:T(8,128)(2,1)S(1)} %pad_maximum_fusion.1.refs_1_), channel_id=1, source_target_pairs={{0,6},{1,7},{2,4},{3,5},{4,2},{5,3},{6,0},{7,1},{16,22},{17,23},{1... | collective-permute-start | bytes 2359304 | tf_op jit(solution)/shard_map/ppermute | solution.py:55
  157.5 18.0 %collective-permute-start.14 = (bf16[224,1536]{1,0:T(8,128)(2,1)S(1)}, bf16[224,1536]{1,0:T(8,128)(2,1)}, u32[]{:S(2)}, u32[]{:S(2)}) collective-permute-start(bf16[224,1536]{1,0:T(8,128)(2,1)S(1)} %slice.42), channel_id=1, source_target_pairs={{0,8},{1,9},{2,10},{3,11},{4,12},{5,13},{6,14},{7,15},{16,24},{17,... | collective-permute-start | bytes 2064392 | tf_op jit(solution)/shard_map/ppermute | solution.py:55
  175.6 21.5 %collective-permute-start.22 = (bf16[512,1536]{1,0:T(8,128)(2,1)S(1)}, bf16[512,1536]{1,0:T(8,128)(2,1)}, u32[]{:S(2)}, u32[]{:S(2)}) collective-permute-start(bf16[512,1536]{1,0:T(8,128)(2,1)S(1)} %bitcast.15), channel_id=1, source_target_pairs={{0,1},{1,0},{2,3},{3,2},{4,5},{5,4},{6,7},{7,6},{16,17},{17,16},{1... | collective-permute-start | bytes 4718600 | tf_op jit(solution)/shard_map/ppermute | solution.py:55
  177.2 5.0 %collective-permute-start.19 = (bf16[256,1536]{1,0:T(8,128)(2,1)S(1)}, bf16[256,1536]{1,0:T(8,128)(2,1)S(1)}, u32[]{:S(2)}, u32[]{:S(2)}) collective-permute-start(bf16[256,1536]{1,0:T(8,128)(2,1)S(1)} %collective-permute-done.15.refs_2_), channel_id=1, source_target_pairs={{0,1},{1,0},{2,3},{3,2},{4,5},{5,4},{6,7},{7,6},{16,17},{17,16},{1... | collective-permute-start | bytes 2359304 | tf_op jit(solution)/shard_map/ppermute | solution.py:55
  177.3 6.2 %collective-permute-start.20 = (bf16[256,1536]{1,0:T(8,128)(2,1)S(1)}, bf16[256,1536]{1,0:T(8,128)(2,1)S(1)}, u32[]{:S(2)}, u32[]{:S(2)}) collective-permute-start(bf16[256,1536]{1,0:T(8,128)(2,1)S(1)} %collective-permute-done.16.refs_3_), channel_id=1, source_target_pairs={{0,1},{1,0},{2,3},{3,2},{4,5},{5,4},{6,7},{7,6},{16,17},{17,16},{1... | collective-permute-start | bytes 2359304 | tf_op jit(solution)/shard_map/ppermute | solution.py:55
  178.6 15.9 %collective-permute-start.21 = (bf16[160,1536]{1,0:T(8,128)(2,1)}, bf16[160,1536]{1,0:T(8,128)(2,1)}, u32[]{:S(2)}, u32[]{:S(2)}) collective-permute-start(bf16[160,1536]{1,0:T(8,128)(2,1)} %slice.43), channel_id=1, source_target_pairs={{0,8},{1,9},{2,10},{3,11},{4,12},{5,13},{6,14},{7,15},{16,24},{17,... | collective-permute-start | bytes 1474568 | tf_op jit(solution)/shard_map/ppermute | solution.py:55
  178.9 18.1 %collective-permute-start.24 = (bf16[224,1536]{1,0:T(8,128)(2,1)}, bf16[224,1536]{1,0:T(8,128)(2,1)}, u32[]{:S(2)}, u32[]{:S(2)}) collective-permute-start(bf16[224,1536]{1,0:T(8,128)(2,1)} %collective-permute-done.14.refs_2_), channel_id=1, source_target_pairs={{0,1},{1,0},{2,3},{3,2},{4,5},{5,4},{6,7},{7,6},{16,17},{17,16},{1... | collective-permute-start | bytes 2064392 | tf_op jit(solution)/shard_map/ppermute | solution.py:55
  191.0 16.0 %all-to-all-start.4 = ((bf16[8,128,384]{2,1,0:T(8,128)(2,1)}), bf16[8,128,384]{2,1,0:T(8,128)(2,1)S(1)}, u32[]{:S(2)}, u32[]{:S(2)}) async-start(bf16[8,128,384]{2,1,0:T(8,128)(2,1)} %copy-done.12), calls=%async_computation.4 | async-start | bytes 1572864 | tf_op jit(solution)/shard_map/all_to_all | solution.py:461
  194.5 2.5 %collective-permute-start.25 = (bf16[160,1536]{1,0:T(8,128)(2,1)}, bf16[160,1536]{1,0:T(8,128)(2,1)S(1)}, u32[]{:S(2)}, u32[]{:S(2)}) collective-permute-start(bf16[160,1536]{1,0:T(8,128)(2,1)} %collective-permute-done.21.refs_3_), channel_id=1, source_target_pairs={{0,1},{1,0},{2,3},{3,2},{4,5},{5,4},{6,7},{7,6},{16,17},{17,16},{1... | collective-permute-start | bytes 1474568 | tf_op jit(solution)/shard_map/ppermute | solution.py:55
  195.0 2.1 collective-permute-start.23
  (16 other events, 73.2 us)

commit v2 on v1

--- a/solution.py
+++ b/solution.py
@@ -48,6 +48,7 @@
     "yl": flip_pairs(y_flip=1),
 }
 TOKEN_ORDERS = ("aby", "bay")
+GRAD_PARTS = (range(5), range(5, 8))
 Z_GROUPS = [[y * 8 + z * 2 + core for z in range(4)] for y in range(2) for core in range(2)]
 
 
@@ -55,8 +56,8 @@
     return lax.ppermute(values, AXES, FLIPS[name])
 
 
-def after(first, then):
-    return lax.optimization_barrier((first, then))[1]
+def together(*values):
+    return lax.optimization_barrier(values)
 
 
 def f32(values):
@@ -81,7 +82,6 @@
         out_shape=out_shape,
         scratch_shapes=scratch,
         compiler_params=pltpu.CompilerParams(vmem_limit_bytes=VMEM_LIMIT),
-        cost_estimate=pl.CostEstimate(flops=0, bytes_accessed=0, transcendentals=0),
     )(place, *args)
 
 
@@ -110,8 +110,8 @@
     )
 
 
-def grad_pieces(block):
-    return [(block + r, 4 * y + z) for y in range(2) for z in range(4) for r in range(4)]
+def grad_pieces(blocks):
+    return [(r, 4 * y + z) for y in range(2) for z in range(4) for r in blocks]
 
 
 def token_pieces(chunk, block):
@@ -124,16 +124,18 @@
     ]
 
 
-def partial_sums(place, raw, raw_other, kind, pieces, weight, weight_other, hidden_axis):
-    rows, depth = raw.shape[2:]
+def partial_sums(place, raws, kind, pieces, weights, hidden_axis, got=None, split=False, earlier=()):
+    rows, depth = raws[0].shape[2:]
     own = rows // 8
     total_rows = own * len(pieces)
-    half = total_rows // 2
-    width = weight_other.shape[hidden_axis]
+    half = total_rows // 2 if split else 0
+    width = weights[1].shape[hidden_axis]
     tile = min(TILE, width)
     dims = (((1,), (1 - hidden_axis,)), ((), ()))
-
-    def kernel(place_ref, l_ref, lo_ref, w_ref, wo_ref, keep_ref, send_ref, left):
+    outs = 2 if split else 1
+
+    def kernel(place_ref, l_ref, lo_ref, w_ref, wo_ref, *refs):
+        out_refs, left = refs[-1 - outs : -1], refs[-1]
         for i, (block, piece) in enumerate(pieces):
             left[i * own : (i + 1) * own, :depth] = l_ref[block, kind, piece * own : (piece + 1) * own]
             left[i * own : (i + 1) * own, depth:] = lo_ref[block, kind, piece * own : (piece + 1) * own]
@@ -144,19 +146,24 @@
             else:
                 right = jnp.concatenate([w_ref[mine, :], wo_ref[start : start + tile, :]], axis=1)
             total = lax.dot_general(left[...], right, dims, preferred_element_type=jnp.float32)
-            total = total.astype(jnp.bfloat16)
-            keep_ref[:, start : start + tile] = total[:half]
-            send_ref[:, start : start + tile] = total[half:]
-
-    out = jax.ShapeDtypeStruct((half, width), jnp.bfloat16)
-    return kernel_call(
-        kernel,
-        place,
-        (raw, raw_other, weight, weight_other),
-        [IN_VMEM, IN_VMEM],
-        [out, out],
+            if got is not None:
+                total += refs[0][:, start : start + tile].astype(jnp.float32)
+            if split:
+                out_refs[0][:, start : start + tile] = total[:half].astype(jnp.bfloat16)
+            out_refs[-1][:, start : start + tile] = total[half:].astype(jnp.bfloat16)
+
+    shapes = [jax.ShapeDtypeStruct((total_rows - half, width), jnp.bfloat16)]
+    if split:
+        shapes = [jax.ShapeDtypeStruct((half, width), jnp.bfloat16)] + shapes
+    result = kernel_call(
+        kernel,
+        place,
+        (*raws, *weights) + (() if got is None else (got,)) + tuple(earlier),
+        [IN_VMEM] * outs,
+        shapes,
         [pltpu.VMEM((total_rows, 2 * depth), jnp.bfloat16)],
     )
+    return result if split else result[0]
 
 
 def input_total(place, parts):
@@ -187,19 +194,17 @@
         step(pl.ds(pl.multiple_of(i * tile, tile), tile))
 
 
-def fold(place, kept, got, second):
-    count = len(kept)
-    rows, width = second[0].shape
+def fold(place, held, second):
+    count = len(held)
+    rows, width = held[0].shape
     half = rows // 2
 
     def kernel(place_ref, *refs):
-        own_ref, send_ref = refs[3 * count :]
+        own_ref, send_ref = refs[2 * count :]
 
         def step(at):
             for i in range(count):
-                k, g, s = refs[i], refs[count + i], refs[2 * count + i]
-                total = k[:rows, at].astype(jnp.float32) + g[:rows, at].astype(jnp.float32)
-                total += s[:, at].astype(jnp.float32)
+                total = refs[i][:, at].astype(jnp.float32) + refs[count + i][:, at].astype(jnp.float32)
                 own_ref[i * half : (i + 1) * half, at] = total[:half]
                 send_ref[i * half : (i + 1) * half, at] = total[half:].astype(jnp.bfloat16)
 
@@ -209,55 +214,46 @@
     return kernel_call(
         kernel,
         place,
-        (*kept, *got, *second),
+        (*held, *second),
         [IN_VMEM, IN_VMEM],
         [jax.ShapeDtypeStruct(out, jnp.float32), jax.ShapeDtypeStruct(out, jnp.bfloat16)],
     )
 
 
 def activate(place, own_sums, far):
-    rows, width = own_sums.shape
-
-    def kernel(place_ref, own_ref, far_ref, out_ref, slope_ref):
+    shape = jax.ShapeDtypeStruct(own_sums.shape, jnp.bfloat16)
+
+    def kernel(place_ref, own_ref, far_ref, gelu_ref, slope_ref):
         def step(at):
             hidden = own_ref[:, at] + far_ref[:, at].astype(jnp.float32)
-            gelu = gelu_value(hidden).astype(jnp.bfloat16)
-            for chip in range(4):
-                out_ref[chip * rows : (chip + 1) * rows, at] = gelu
-            slope_ref[:, at] = gelu_slope(hidden)
+            gelu_ref[:, at] = gelu_value(hidden).astype(jnp.bfloat16)
+            slope_ref[:, at] = gelu_slope(hidden).astype(jnp.bfloat16)
+
+        for_tiles(shape.shape[1], step)
+
+    return kernel_call(kernel, place, (own_sums, far), [IN_VMEM, IN_VMEM], [shape, shape])
+
+
+def chain_slope(place, parts, slope, earlier):
+    rows, width = slope.shape
+
+    def kernel(place_ref, *refs):
+        slope_ref, out_ref = refs[len(parts)], refs[-1]
+
+        def step(at):
+            start = 0
+            for part in refs[: len(parts)]:
+                size = part.shape[0] // 4
+                total = part[:size, at].astype(jnp.float32)
+                for chip in range(1, 4):
+                    total += part[chip * size : (chip + 1) * size, at].astype(jnp.float32)
+                here = slice(start, start + size)
+                out_ref[here, at] = (total * slope_ref[here, at].astype(jnp.float32)).astype(jnp.bfloat16)
+                start += size
 
         for_tiles(width, step)
 
-    return kernel_call(
-        kernel,
-        place,
-        (own_sums, far),
-        [IN_VMEM, IN_VMEM],
-        [
-            jax.ShapeDtypeStruct((4 * rows, width), jnp.bfloat16),
-            jax.ShapeDtypeStruct((rows, width), jnp.float32),
-        ],
-    )
-
-
-def chain_slope(place, parts, slope):
-    rows, width = slope.shape
-    half = rows // len(parts)
-
-    def kernel(place_ref, *refs):
-        slope_ref, out_ref = refs[len(parts) :]
-
-        def step(at):
-            for i, part in enumerate(refs[: len(parts)]):
-                total = part[:half, at].astype(jnp.float32)
-                for chip in range(1, 4):
-                    total += part[chip * half : (chip + 1) * half, at].astype(jnp.float32)
-                here = slice(i * half, (i + 1) * half)
-                out_ref[here, at] = (total * slope_ref[here, at]).astype(jnp.bfloat16)
-
-        for_tiles(width, step)
-
-    return kernel_call(kernel, place, (*parts, slope), IN_VMEM, jax.ShapeDtypeStruct((rows, width), jnp.bfloat16))
+    return kernel_call(kernel, place, (*parts, slope, *earlier), IN_VMEM, jax.ShapeDtypeStruct((rows, width), jnp.bfloat16))
 
 
 def features_of(place, raw, kind, pieces):
@@ -265,8 +261,15 @@
     own = rows // 8
 
     def kernel(place_ref, raw_ref, out_ref):
+        def rows_of(block, piece):
+            if isinstance(piece, tuple):
+                y, flip = piece
+                piece = 4 * y + (place_ref[Z] ^ flip)
+                return raw_ref[block, kind, pl.ds(pl.multiple_of(piece * own, own), own)]
+            return raw_ref[block, kind, piece * own : (piece + 1) * own]
+
         for g in range(0, len(pieces), 8):
-            block = [raw_ref[b, kind, p * own : (p + 1) * own] for b, p in pieces[g : g + 8]]
+            block = [rows_of(*at) for at in pieces[g : g + 8]]
             out_ref[:, g * own : (g + 8) * own] = jnp.concatenate(block).T
 
     return kernel_call(
@@ -274,29 +277,30 @@
     )
 
 
-def grad_scratch(tile_shape):
-    return [pltpu.VMEM((2, *tile_shape), jnp.float32), pltpu.SemaphoreType.DMA((2,))]
+def grad_scratch(depth, width, hidden_axis):
+    tile = min(TILE, width)
+    steps = 2 * width // tile
+    tile_shape = (depth, tile) if hidden_axis == 1 else (tile, depth)
+    return [pltpu.VMEM((steps, *tile_shape), jnp.float32), pltpu.SemaphoreType.DMA((steps,))]
 
 
 def write_grad(core, parts_of, features, hidden_axis, out_ref, tiles, sems):
     width = parts_of[0][0].shape[1]
     tile = min(TILE, width)
-    stores = [None, None]
-    step = 0
+    stores = []
     for parts, place_of in zip(parts_of, (core, 1 - core)):
         for start in range(0, width, tile):
             units = jnp.concatenate([p[:, start : start + tile] for p in parts])
             total = jnp.dot(features[...], units, preferred_element_type=jnp.float32)
-            slot = step % 2
-            if stores[slot] is not None:
-                stores[slot].wait()
-            tiles[slot] = total if hidden_axis == 1 else total.T
+            step = len(stores)
+            tiles[step] = total if hidden_axis == 1 else total.T
             to = pl.ds(pl.multiple_of(place_of * width + start, tile), tile)
-            stores[slot] = pltpu.make_async_copy(
-                tiles.at[slot], out_ref.at[:, to] if hidden_axis == 1 else out_ref.at[to, :], sems.at[slot]
+            stores.append(
+                pltpu.make_async_copy(
+                    tiles.at[step], out_ref.at[:, to] if hidden_axis == 1 else out_ref.at[to, :], sems.at[step]
+                )
             )
-            stores[slot].start()
-            step += 1
+            stores[step].start()
     for store in stores:
         store.wait()
 
@@ -351,7 +355,7 @@
             jax.ShapeDtypeStruct((blocks, 2 * rows, depth), jnp.bfloat16),
             jax.ShapeDtypeStruct((depth, 2 * width), jnp.float32),
         ],
-        grad_scratch((depth, min(TILE, width))),
+        grad_scratch(depth, width, 1),
     )
 
 
@@ -371,7 +375,7 @@
         (*mine, *other, features),
         pl.BlockSpec(memory_space=pl.ANY),
         jax.ShapeDtypeStruct((2 * width, depth), jnp.float32),
-        grad_scratch((min(TILE, width), depth)),
+        grad_scratch(depth, width, 0),
     )
 
 
@@ -387,57 +391,70 @@
 
     copies = copies_for_row(place, out_grad, tokens)
     raw = lax.all_to_all(copies, "row", 0, 0, tiled=True)
-    raw_other = swap(raw, "core")
 
     w_out_other = swap(lax.dynamic_slice_in_dim(w_out, (1 - core) * width, width, 0), "core")
     w_in_other = swap(lax.dynamic_slice_in_dim(w_in, (1 - core) * width, width, 1), "core")
-
-    def grad_sums(raw, raw_other, chunk):
-        return partial_sums(place, raw, raw_other, 0, grad_pieces(4 * chunk), w_out, w_out_other, 0)
-
-    def token_sums(raw, raw_other, chunk):
-        return partial_sums(place, raw, raw_other, 1, token_pieces(chunk, 4 * chunk), w_in, w_in_other, 1)
-
-    grad_kept_1, sent_1 = grad_sums(raw, raw_other, 0)
-    grad_got_1 = swap(sent_1, "y")
-    then = after(sent_1, (raw, raw_other))
-    tok_kept, tok_sent = zip(*[token_sums(*then, chunk) for chunk in range(2)])
-    tok_got = [swap(sent, order[0]) for sent, order in zip(tok_sent, TOKEN_ORDERS)]
-    grad_kept_2, sent_2 = grad_sums(*after(tok_sent, then), 1)
-    grad_got_2 = swap(sent_2, "y")
-
-    def z_terms(kept, got):
-        parts = b16(f32(kept) + f32(got))
-        return lax.all_to_all(parts, "col", 0, 0, axis_index_groups=Z_GROUPS, tiled=True)
-
-    q = quarter // 2
-    terms = [z_terms(grad_kept_1, grad_got_1)]
-    tok_got = after((grad_got_1, sent_2), tok_got)
-    second = [
-        swap(b16(f32(k[q:]) + f32(g[q:])), order[1]) for k, g, order in zip(tok_kept, tok_got, TOKEN_ORDERS)
-    ]
-    second = after((grad_got_2, terms[0]), second)
-    own_sums, to_send = fold(place, tok_kept, tok_got, second)
-    far = swap(to_send, "y")
-    terms.append(z_terms(grad_kept_2, grad_got_2))
-    q = quarter // 4
+    raw, w_out_other, w_in_other = together(raw, w_out_other, w_in_other)
+    raw_other = swap(raw, "core")
+
+    raws = (raw, raw_other)
+
+    pieces = [token_pieces(chunk, 4 * chunk) for chunk in range(2)]
+    half_of = [(p[:16], p[16:]) for p in pieces]
+    w_in_both, w_out_both = (w_in, w_in_other), (w_out, w_out_other)
+    first = []
+    for _, far_half in half_of:
+        first.append(partial_sums(place, raws, 1, far_half, w_in_both, 1))
+    tok_got = [swap(f, order[0]) for f, order in zip(first, TOKEN_ORDERS)]
+    grad_half_of, sent, grad_got = [], [first[1]], []
+    for blocks in GRAD_PARTS:
+        pieces = grad_pieces(blocks)
+        grad_half_of.append(pieces[: len(pieces) // 2])
+        far_half = pieces[len(pieces) // 2 :]
+        sent.append(partial_sums(place, raws, 0, far_half, w_out_both, 0))
+        grad_got.append(swap(sent[-1], "y"))
 
     keep_pieces = token_pieces(0, 0)[:16] + token_pieces(1, 4)[:16]
     first_pieces = token_pieces(0, 0)[16:] + token_pieces(1, 4)[16:]
-    grad_order = [(r, 4 * y + z) for y in range(2) for z in range(4) for r in range(8)]
-    raw = after(to_send, raw)
     tok_features = features_of(place, raw, 1, keep_pieces + first_pieces)
+    flips = {"a": 1, "b": 3}
+    grad_order = [
+        (4 * chunk + r, (y, (flips[order[0]] * late) ^ (flips[order[1]] * early)))
+        for y in range(2)
+        for chunk, order in enumerate(TOKEN_ORDERS)
+        for late in range(2)
+        for early in range(2)
+        for r in range(4)
+    ]
     grad_features = features_of(place, raw, 0, grad_order)
-    far = after((tok_features, grad_features), far)
-
-    spread, slope = activate(place, own_sums, far)
-    gelu_keep = lax.all_to_all(spread, "col", 0, 0, axis_index_groups=Z_GROUPS, tiled=True)
-    pre_share = chain_slope(place, terms, slope)
+
+    held, sent = [], []
+    for (near_half, _), got in zip(half_of, tok_got):
+        hold, send = partial_sums(place, raws, 1, near_half, w_in_both, 1, got, split=True, earlier=sent or (tok_features, grad_features))
+        held.append(hold)
+        sent.append(send)
+    second = [swap(s, order[1]) for s, order in zip(sent, TOKEN_ORDERS)]
+    terms, earlier = [], sent[1:]
+    for near_half, got in zip(grad_half_of, grad_got):
+        sums = partial_sums(place, raws, 0, near_half, w_out_both, 0, got, earlier=earlier)
+        earlier = ()
+        terms.append(lax.all_to_all(sums, "col", 0, 0, axis_index_groups=Z_GROUPS, tiled=True))
+    own_sums, to_send = fold(place, held, second)
+    far = swap(to_send, "y")
+    q = quarter // 4
+
+    gelu_share, slope = activate(place, own_sums, far)
+    gelu_near = []
+    for start, order in zip((0, q), TOKEN_ORDERS):
+        two = jnp.concatenate([gelu_share[start : start + q], swap(gelu_share[start : start + q], order[1])])
+        gelu_near += [two, swap(two, order[0])]
+    gelu_keep = jnp.concatenate(gelu_near)
+    pre_share = chain_slope(place, terms, slope, ())
     far = swap(pre_share, "y")
     two = [jnp.concatenate([pre_share[i : i + q], far[i : i + q]]) for i in (0, q)]
 
     gelu_keep, two = lax.optimization_barrier((gelu_keep, two))
-    cuts = (0, quarter // 2, 11 * quarter // 8)
+    cuts = (0, quarter // 4, 11 * quarter // 8)
     gelu_far = [swap(gelu_keep[: cuts[1]], "y")]
     pre_keep = [jnp.concatenate([t, swap(t, order[1])]) for t, order in zip(two, TOKEN_ORDERS)]
 
@@ -459,11 +476,11 @@
         tok_features,
     )
     parts = lax.all_to_all(sums, "row", 0, 0, tiled=True)
-    gelu_far[2] = after(sums, gelu_far[2])
+    w_in_grad, gelu_far[2] = together(w_in_grad, gelu_far[2])
     gelu_mine = (gelu_keep, *gelu_far)
     gelu_other = [swap(g, "core") for g in gelu_mine]
     w_out_grad = weight_grad(place, gelu_mine, gelu_other, grad_features)
-    parts = after(w_out_grad, parts)
+    w_out_grad, parts = together(w_out_grad, parts)
     in_grad = input_total(place, parts)
     return (in_grad, w_in_grad, w_out_grad)
 

time: 209 us -> 197 us (0.943)
  waiting for transfers between devices: 96.2 us -> 67.7 us
  local copies, waits for them, and re-layouts: 10.7 us -> 20 us
  starting transfers between devices: 57.7 us -> 67 us
  other arithmetic: 9.42 us -> 2.24 us
  Pallas kernels: 33.2 us -> 37.2 us
    ppermute x26 -> x30, waiting for transfers between devices: 58.2 us -> 41.5 us  [swap(): return lax.ppermute(values, AXES, FLIPS[name])]
    ppermute x26 -> x30, starting transfers between devices: 35.7 us -> 50.4 us  [swap(): return lax.ppermute(values, AXES, FLIPS[name])]
    all_to_all x3 -> x2, waiting for transfers between devices: 11.9 us -> 4.12 us  [body(): lax.all_to_all(sums, 'col', 0, 0, axis_index_groups=Z_GROUPS, tiled=True)]
    unnamed x34 -> x58, local copies, waits for them, and re-layouts: 7.25 us -> 14.4 us
    convert_element_type x4 -> x0, other arithmetic: 6.17 us -> none  [b16(): return values.astype(jnp.bfloat16)]
    all_to_all x3 -> x2, starting transfers between devices: 12.7 us -> 7.8 us  [body(): lax.all_to_all(sums, 'col', 0, 0, axis_index_groups=Z_GROUPS, tiled=True)]
    all_to_all x1, waiting for transfers between devices: 23 us -> 18.8 us  [body(): raw = lax.all_to_all(copies, 'row', 0, 0, tiled=True)]
    pallas_call x14 -> x18, Pallas kernels: 33.2 us -> 37.2 us  [kernel_call(): pl.pallas_call(kernel, in_specs=[pl.BlockSpec(memory_space=pltpu.SMEM)] +...]
  transfers between devices with their start and end apart: 31 -> 34, of which waited for: 18 -> 19; matrix products, arithmetic and copies ran while one was open for 6% -> 3% of each run, Pallas kernels for 13% -> 18%
where the time goes in v2:
time: 197 us; the launch traced here: 195 us
  waiting for transfers between devices  67.7 us (34%)
  starting transfers between devices  67 us (34%)
  Pallas kernels  37.2 us (19%)
  local copies, waits for them, and re-layouts  20 us (10%)
  other arithmetic  2.24 us (1%)
    ppermute x30, starting transfers between devices, swap(): return lax.ppermute(values, AXES, FLIPS[name])  50.4 us
    ppermute x30, waiting for transfers between devices, swap(): return lax.ppermute(values, AXES, FLIPS[name])  41.5 us
    pallas_call x18, Pallas kernels, kernel_call(): pl.pallas_call(kernel, in_specs=[pl.BlockSpec(memory_space=pltpu.SMEM)] +...  37.2 us
    all_to_all x1, waiting for transfers between devices, body(): raw = lax.all_to_all(copies, 'row', 0, 0, tiled=True)  18.8 us
    unnamed x58, local copies, waits for them, and re-layouts  14.4 us
    all_to_all x2, starting transfers between devices, body(): lax.all_to_all(sums, 'col', 0, 0, axis_index_groups=Z_GROUPS, tiled=True)  7.8 us
    all_to_all x1, starting transfers between devices, body(): raw = lax.all_to_all(copies, 'row', 0, 0, tiled=True)  5.12 us
    all_to_all x2, waiting for transfers between devices, body(): lax.all_to_all(sums, 'col', 0, 0, axis_index_groups=Z_GROUPS, tiled=True)  4.12 us
  transfers between devices with their start and end apart: 34, of which 19 were waited for; matrix products, arithmetic and copies ran while one was open for 3% of the time, Pallas kernels for 18%

profile of v2, /device:TPU:1, one launch (start us, length us, event | category | flops | bytes accessed | tf_op | source)
XLA Modules:
  0.0 195.2 jit_solution(13148155807278746602)
XLA Ops:
  0.7 2.4 %constant_dynamic-slice_fusion = bf16[384,1536]{1,0:T(8,128)(2,1)} fusion(bf16[384,3072]{1,0:T(8,128)(2,1)} %refs_8_.1, s32[]{:T(128)S(6)} %select_n.26), kind=kLoop, calls=%fused_computation.13 | loop fusion | bytes 2359300 | tf_op jit(solution)/shard_map/dynamic_slice | solution.py:396
  6.4 5.1 %all-to-all-start = ((bf16[8,2,128,384]{3,2,1,0:T(8,128)(2,1)}), bf16[8,2,128,384]{3,2,1,0:T(8,128)(2,1)S(1)}, u32[]{:S(2)}, u32[]{:S(2)}) async-start(bf16[8,2,128,384]{3,2,1,0:T(8,128)(2,1)} %copy-done.15), calls=%async_computation | async-start | bytes 3145728 | tf_op jit(solution)/shard_map/all_to_all | solution.py:393
  16.9 18.8 %all-to-all-done.l_ref.raw_ref = bf16[8,2,128,384]{3,2,1,0:T(8,128)(2,1)S(1)} async-done(((bf16[8,2,128,384]{3,2,1,0:T(8,128)(2,1)}), bf16[8,2,128,384]{3,2,1,0:T(8,128)(2,1)S(1)}, u32[]{:S(2)}, u32[]{:S(2)}) %all-to-all-start) | async-done | bytes 1572896 | tf_op jit(solution)/shard_map/all_to_all | solution.py:393
  36.8 3.0 %collective-permute-done.2.lo_ref = bf16[8,2,128,384]{3,2,1,0:T(8,128)(2,1)S(1)} collective-permute-done((bf16[8,2,128,384]{3,2,1,0:T(8,128)(2,1)S(1)}, bf16[8,2,128,384]{3,2,1,0:T(8,128)(2,1)S(1)}, u32[]{:S(2)}, u32[]{:S(2)}) %collective-permute-start.2) | collective-permute-done | bytes 1572896 | tf_op jit(solution)/shard_map/ppermute | solution.py:56
  47.1 2.3 %collective-permute-start.4 = (bf16[256,1536]{1,0:T(8,128)(2,1)S(1)}, bf16[256,1536]{1,0:T(8,128)(2,1)S(1)}, u32[]{:S(2)}, u32[]{:S(2)}) collective-permute-start(bf16[256,1536]{1,0:T(8,128)(2,1)S(1)} %shard_map.72), channel_id=1, source_target_pairs={{0,6},{1,7},{2,4},{3,5},{4,2},{5,3},{6,0},{7,1},{16,22},{17,23},{1... | collective-permute-start | bytes 2359304 | tf_op jit(solution)/shard_map/ppermute | solution.py:56
  51.0 2.7 %collective-permute-start.13 = (bf16[192,1536]{1,0:T(8,128)(2,1)S(1)}, bf16[192,1536]{1,0:T(8,128)(2,1)S(1)}, u32[]{:S(2)}, u32[]{:S(2)}) collective-permute-start(bf16[192,1536]{1,0:T(8,128)(2,1)S(1)} %shard_map.78), channel_id=1, source_target_pairs={{0,8},{1,9},{2,10},{3,11},{4,12},{5,13},{6,14},{7,15},{16,24},{17,... | collective-permute-start | bytes 1769480 | tf_op jit(solution)/shard_map/ppermute | solution.py:56
  53.7 2.5 %shard_map.76 = bf16[320,1536]{1,0:T(8,128)(2,1)} custom-call(s32[4]{0:T(128)S(1)} %pad_add_fusion.place_ref, bf16[8,2,128,384]{3,2,1,0:T(8,128)(2,1)S(1)} %all-to-all-done.l_ref.raw_ref, bf16[8,2,128,384]{3,2,1,0:T(8,128)(2,1)S(1)} %collective-permute-done.2.lo_ref, bf16[3072,384]{1,0:T(8,128)(2,1)S(1)} %copy-done.3, bf16[1536,384]{1,0:T(8,128)(2,1)S(1)} %copy-done.6), custom_call_target="tpu_custom_call" | custom-call | tf_op jit(solution)/shard_map/pallas_call | solution.py:78
  58.2 5.1 %collective-permute-done.3.refs_0_ = bf16[256,1536]{1,0:T(8,128)(2,1)S(1)} collective-permute-done((bf16[256,1536]{1,0:T(8,128)(2,1)S(1)}, bf16[256,1536]{1,0:T(8,128)(2,1)S(1)}, u32[]{:S(2)}, u32[]{:S(2)}) %collective-permute-start.3) | collective-permute-done | bytes 786464 | tf_op jit(solution)/shard_map/ppermute | solution.py:56
  63.3 2.1 %shard_map.71 = (bf16[128,1536]{1,0:T(8,128)(2,1)S(1)}, bf16[128,1536]{1,0:T(8,128)(2,1)}) custom-call(s32[4]{0:T(128)S(1)} %pad_add_fusion.place_ref, bf16[8,2,128,384]{3,2,1,0:T(8,128)(2,1)S(1)} %all-to-all-done.l_ref.raw_ref, bf16[8,2,128,384]{3,2,1,0:T(8,128)(2,1)S(1)} %collective-permute-done.2.lo_ref, bf16[384,3072]{1,0:T(8,128)(2,1)S(1)} %copy-done.1, ...), custom_call_target="tpu_custom_call" | custom-call | tf_op jit(solution)/shard_map/pallas_call | solution.py:78
  65.4 3.5 %collective-permute-start.5 = (bf16[128,1536]{1,0:T(8,128)(2,1)}, bf16[128,1536]{1,0:T(8,128)(2,1)}, u32[]{:S(2)}, u32[]{:S(2)}) collective-permute-start(bf16[128,1536]{1,0:T(8,128)(2,1)} %get-tuple-element.35.refs_1_), channel_id=1, source_target_pairs={{0,6},{1,7},{2,4},{3,5},{4,2},{5,3},{6,0},{7,1},{16,22},{17,23},{1... | collective-permute-start | bytes 1179656 | tf_op jit(solution)/shard_map/ppermute | solution.py:56
  68.9 1.8 shard_map.73
  73.2 4.2 %all-to-all-start.2 = ((bf16[4,48,1536]{2,1,0:T(8,128)(2,1)}), bf16[4,48,1536]{2,1,0:T(8,128)(2,1)}, u32[]{:S(2)}, u32[]{:S(2)}) async-start(bf16[4,48,1536]{2,1,0:T(8,128)(2,1)} %bitcast.13), calls=%async_computation.2 | async-start | bytes 1179648 | tf_op jit(solution)/shard_map/all_to_all | solution.py:441
  77.5 2.6 %collective-permute-done.6.refs_3_ = bf16[128,1536]{1,0:T(8,128)(2,1)} collective-permute-done((bf16[128,1536]{1,0:T(8,128)(2,1)S(1)}, bf16[128,1536]{1,0:T(8,128)(2,1)}, u32[]{:S(2)}, u32[]{:S(2)}) %collective-permute-start.6) | collective-permute-done | bytes 393248 | tf_op jit(solution)/shard_map/ppermute | solution.py:56
  82.1 2.2 %shard_map.74 = (f32[128,1536]{1,0:T(8,128)S(1)}, bf16[128,1536]{1,0:T(8,128)(2,1)}) custom-call(s32[4]{0:T(128)S(1)} %pad_add_fusion.place_ref, bf16[128,1536]{1,0:T(8,128)(2,1)S(1)} %copy-done.22, bf16[128,1536]{1,0:T(8,128)(2,1)S(1)} %copy-done.24, bf16[128,1536]{1,0:T(8,128)(2,1)} %collective-permute-done.5.refs_2_, ...), custom_call_target="tpu_custom_call" | custom-call | tf_op jit(solution)/shard_map/pallas_call | solution.py:78
  85.2 2.6 %collective-permute-start.7 = (bf16[128,1536]{1,0:T(8,128)(2,1)}, bf16[128,1536]{1,0:T(8,128)(2,1)}, u32[]{:S(2)}, u32[]{:S(2)}) collective-permute-start(bf16[128,1536]{1,0:T(8,128)(2,1)} %get-tuple-element.39), channel_id=1, source_target_pairs={{0,8},{1,9},{2,10},{3,11},{4,12},{5,13},{6,14},{7,15},{16,24},{17,... | collective-permute-start | bytes 1179656 | tf_op jit(solution)/shard_map/ppermute | solution.py:56
  89.5 2.2 %shard_map.77 = bf16[320,1536]{1,0:T(8,128)(2,1)S(1)} custom-call(s32[4]{0:T(128)S(1)} %pad_add_fusion.place_ref, bf16[8,2,128,384]{3,2,1,0:T(8,128)(2,1)S(1)} %all-to-all-done.l_ref.raw_ref, bf16[8,2,128,384]{3,2,1,0:T(8,128)(2,1)S(1)} %collective-permute-done.2.lo_ref, bf16[3072,384]{1,0:T(8,128)(2,1)S(1)} %copy-done.4, bf16[1536,384]{1,0:T(8,128)(2,1)S(1)} %copy-done.7, ...), custom_call_target="tpu_custom_call" | custom-call | tf_op jit(solution)/shard_map/pallas_call | solution.py:78
  92.7 3.6 %all-to-all-start.1 = ((bf16[4,80,1536]{2,1,0:T(8,128)(2,1)}), bf16[4,80,1536]{2,1,0:T(8,128)(2,1)S(1)}, u32[]{:S(2)}, u32[]{:S(2)}) async-start(bf16[4,80,1536]{2,1,0:T(8,128)(2,1)} %bitcast.12), calls=%async_computation.1 | async-start | bytes 1966080 | tf_op jit(solution)/shard_map/all_to_all | solution.py:441
  101.9 4.1 %all-to-all-done.1 = bf16[4,80,1536]{2,1,0:T(8,128)(2,1)S(1)} async-done(((bf16[4,80,1536]{2,1,0:T(8,128)(2,1)}), bf16[4,80,1536]{2,1,0:T(8,128)(2,1)S(1)}, u32[]{:S(2)}, u32[]{:S(2)}) %all-to-all-start.1) | async-done | bytes 983072 | tf_op jit(solution)/shard_map/all_to_all | solution.py:441
  107.5 4.5 %collective-permute-start.14 = (bf16[128,1536]{1,0:T(8,128)(2,1)S(1)}, bf16[128,1536]{1,0:T(8,128)(2,1)S(1)}, u32[]{:S(2)}, u32[]{:S(2)}) collective-permute-start(bf16[128,1536]{1,0:T(8,128)(2,1)S(1)} %shard_map.80), channel_id=1, source_target_pairs={{0,8},{1,9},{2,10},{3,11},{4,12},{5,13},{6,14},{7,15},{16,24},{17,... | collective-permute-start | bytes 1179656 | tf_op jit(solution)/shard_map/ppermute | solution.py:56
  117.3 2.8 %collective-permute-done.9 = bf16[128,1536]{1,0:T(8,128)(2,1)S(1)} collective-permute-done((bf16[128,1536]{1,0:T(8,128)(2,1)S(1)}, bf16[128,1536]{1,0:T(8,128)(2,1)S(1)}, u32[]{:S(2)}, u32[]{:S(2)}) %collective-permute-start.9) | collective-permute-done | bytes 393248 | tf_op jit(solution)/shard_map/ppermute | solution.py:56
  120.2 2.5 %collective-permute-done.11 = bf16[128,1536]{1,0:T(8,128)(2,1)S(1)} collective-permute-done((bf16[128,1536]{1,0:T(8,128)(2,1)S(1)}, bf16[128,1536]{1,0:T(8,128)(2,1)S(1)}, u32[]{:S(2)}, u32[]{:S(2)}) %collective-permute-start.11) | collective-permute-done | bytes 393248 | tf_op jit(solution)/shard_map/ppermute | solution.py:56
  123.4 5.0 %collective-permute-start.15 = (bf16[64,1536]{1,0:T(8,128)(2,1)S(1)}, bf16[64,1536]{1,0:T(8,128)(2,1)S(1)}, u32[]{:S(2)}, u32[]{:S(2)}) collective-permute-start(bf16[64,1536]{1,0:T(8,128)(2,1)S(1)} %slice.35), channel_id=1, source_target_pairs={{0,8},{1,9},{2,10},{3,11},{4,12},{5,13},{6,14},{7,15},{16,24},{17,... | collective-permute-start | bytes 589832 | tf_op jit(solution)/shard_map/ppermute | solution.py:56
  128.4 5.0 %collective-permute-done.16 = bf16[128,1536]{1,0:T(8,128)(2,1)S(1)} collective-permute-done((bf16[128,1536]{1,0:T(8,128)(2,1)S(1)}, bf16[128,1536]{1,0:T(8,128)(2,1)S(1)}, u32[]{:S(2)}, u32[]{:S(2)}) %collective-permute-start.16) | collective-permute-done | bytes 393248 | tf_op jit(solution)/shard_map/ppermute | solution.py:56
  134.9 9.5 %collective-permute-start.21 = (bf16[256,1536]{1,0:T(8,128)(2,1)S(1)}, bf16[256,1536]{1,0:T(8,128)(2,1)S(1)}, u32[]{:S(2)}, u32[]{:S(2)}) collective-permute-start(bf16[256,1536]{1,0:T(8,128)(2,1)S(1)} %pad_maximum_fusion.refs_0_), channel_id=1, source_target_pairs={{0,1},{1,0},{2,3},{3,2},{4,5},{5,4},{6,7},{7,6},{16,17},{17,16},{1... | collective-permute-start | bytes 2359304 | tf_op jit(solution)/shard_map/ppermute | solution.py:56
  144.5 2.7 %collective-permute-start.20 = (bf16[256,1536]{1,0:T(8,128)(2,1)S(1)}, bf16[256,1536]{1,0:T(8,128)(2,1)S(1)}, u32[]{:S(2)}, u32[]{:S(2)}) collective-permute-start(bf16[256,1536]{1,0:T(8,128)(2,1)S(1)} %pad_maximum_fusion.1.refs_1_), channel_id=1, source_target_pairs={{0,6},{1,7},{2,4},{3,5},{4,2},{5,3},{6,0},{7,1},{16,22},{17,23},{1... | collective-permute-start | bytes 2359304 | tf_op jit(solution)/shard_map/ppermute | solution.py:56
  147.5 2.3 %shard_map.81.refs_9_ = bf16[8,64,384]{2,1,0:T(8,128)(2,1)S(1)} custom-call(s32[4]{0:T(128)S(1)} %pad_add_fusion.place_ref, bf16[256,1536]{1,0:T(8,128)(2,1)S(1)} %pad_maximum_fusion.refs_0_, bf16[256,1536]{1,0:T(8,128)(2,1)S(1)} %pad_maximum_fusion.1.refs_1_, bf16[256,1536]{1,0:T(8,128)(2,1)S(1)} %collective-permute-done.21.refs_2_.refs_4_, ...), custom_call_target="tpu_custom_call" | custom-call | tf_op jit(solution)/shard_map/pallas_call | solution.py:78
  149.8 13.4 %collective-permute-done.19.refs_2_ = bf16[256,1536]{1,0:T(8,128)(2,1)S(1)} collective-permute-done((bf16[256,1536]{1,0:T(8,128)(2,1)S(1)}, bf16[256,1536]{1,0:T(8,128)(2,1)S(1)}, u32[]{:S(2)}, u32[]{:S(2)}) %collective-permute-start.19) | collective-permute-done | bytes 786464 | tf_op jit(solution)/shard_map/ppermute | solution.py:56
  167.1 3.1 %collective-permute-start.25 = (bf16[160,1536]{1,0:T(8,128)(2,1)}, bf16[160,1536]{1,0:T(8,128)(2,1)}, u32[]{:S(2)}, u32[]{:S(2)}) collective-permute-start(bf16[160,1536]{1,0:T(8,128)(2,1)} %slice.37), channel_id=1, source_target_pairs={{0,8},{1,9},{2,10},{3,11},{4,12},{5,13},{6,14},{7,15},{16,24},{17,... | collective-permute-start | bytes 1474568 | tf_op jit(solution)/shard_map/ppermute | solution.py:56
  171.1 5.9 %shard_map.82 = (bf16[8,128,384]{2,1,0:T(8,128)(2,1)S(1)}, f32[384,3072]{1,0:T(8,128)}) custom-call(s32[4]{0:T(128)S(1)} %pad_add_fusion.place_ref, bf16[256,1536]{1,0:T(8,128)(2,1)S(1)} %pad_maximum_fusion.refs_0_, bf16[256,1536]{1,0:T(8,128)(2,1)S(1)} %pad_maximum_fusion.1.refs_1_, bf16[256,1536]{1,0:T(8,128)(2,1)S(1)} %collective-permute-done.19.refs_2_, ...), custom_call_target="tpu_custom_call" | custom-call | tf_op jit(solution)/shard_map/pallas_call | solution.py:78
  177.8 3.7 %all-to-all-start.3 = ((bf16[8,128,384]{2,1,0:T(8,128)(2,1)}), bf16[8,128,384]{2,1,0:T(8,128)(2,1)S(1)}, u32[]{:S(2)}, u32[]{:S(2)}) async-start(bf16[8,128,384]{2,1,0:T(8,128)(2,1)} %copy-done.18), calls=%async_computation.3 | async-start | bytes 1572864 | tf_op jit(solution)/shard_map/all_to_all | solution.py:478
  184.6 5.9 %shard_map.83 = f32[3072,384]{1,0:T(8,128)} custom-call(s32[4]{0:T(128)S(1)} %pad_add_fusion.place_ref, bf16[512,1536]{1,0:T(8,128)(2,1)S(1)} %constant_dynamic-update-slice_fusion.refs_0_, bf16[64,1536]{1,0:T(8,128)(2,1)S(1)} %collective-permute-done.15.refs_1_, bf16[288,1536]{1,0:T(8,128)(2,1)} %collective-permute-done.18.refs_2_, ...), custom_call_target="tpu_custom_call" | custom-call | tf_op jit(solution)/shard_map/pallas_call | solution.py:78
  190.6 3.4 %all-to-all-done.3.parts_ref = bf16[8,128,384]{2,1,0:T(8,128)(2,1)S(1)} async-done(((bf16[8,128,384]{2,1,0:T(8,128)(2,1)}), bf16[8,128,384]{2,1,0:T(8,128)(2,1)S(1)}, u32[]{:S(2)}, u32[]{:S(2)}) %all-to-all-start.3) | async-done | bytes 786464 | tf_op jit(solution)/shard_map/all_to_all | solution.py:478
  (127 shorter events, 53.5 us)
Async XLA Ops:
  3.1 10.2 %collective-permute-start.1 = (bf16[384,1536]{1,0:T(8,128)(2,1)}, bf16[384,1536]{1,0:T(8,128)(2,1)S(1)}, u32[]{:S(2)}, u32[]{:S(2)}) collective-permute-start(bf16[384,1536]{1,0:T(8,128)(2,1)} %constant_dynamic-slice_fusion), channel_id=1, source_target_pairs={{0,1},{1,0},{2,3},{3,2},{4,5},{5,4},{6,7},{7,6},{16,17},{17,16},{1... | collective-permute-start | bytes 3538952 | tf_op jit(solution)/shard_map/ppermute | solution.py:56
  6.4 29.2 %all-to-all-start = ((bf16[8,2,128,384]{3,2,1,0:T(8,128)(2,1)}), bf16[8,2,128,384]{3,2,1,0:T(8,128)(2,1)S(1)}, u32[]{:S(2)}, u32[]{:S(2)}) async-start(bf16[8,2,128,384]{3,2,1,0:T(8,128)(2,1)} %copy-done.15), calls=%async_computation | async-start | bytes 3145728 | tf_op jit(solution)/shard_map/all_to_all | solution.py:393
  12.9 2.9 %collective-permute-start = (bf16[1536,384]{1,0:T(8,128)(2,1)S(1)}, bf16[1536,384]{1,0:T(8,128)(2,1)S(1)}, u32[]{:S(2)}, u32[]{:S(2)}) collective-permute-start(bf16[1536,384]{1,0:T(8,128)(2,1)S(1)} %constant_dynamic-slice_fusion.1), channel_id=1, source_target_pairs={{0,1},{1,0},{2,3},{3,2},{4,5},{5,4},{6,7},{7,6},{16,17},{17,16},{1... | collective-permute-start | bytes 3538952 | tf_op jit(solution)/shard_map/ppermute | solution.py:56
  35.7 4.1 %collective-permute-start.2 = (bf16[8,2,128,384]{3,2,1,0:T(8,128)(2,1)S(1)}, bf16[8,2,128,384]{3,2,1,0:T(8,128)(2,1)S(1)}, u32[]{:S(2)}, u32[]{:S(2)}) collective-permute-start(bf16[8,2,128,384]{3,2,1,0:T(8,128)(2,1)S(1)} %all-to-all-done.l_ref.raw_ref), channel_id=1, source_target_pairs={{0,1},{1,0},{2,3},{3,2},{4,5},{5,4},{6,7},{7,6},{16,17},{17,16},{1... | collective-permute-start | bytes 4718600 | tf_op jit(solution)/shard_map/ppermute | solution.py:56
  44.1 19.2 %collective-permute-start.3 = (bf16[256,1536]{1,0:T(8,128)(2,1)S(1)}, bf16[256,1536]{1,0:T(8,128)(2,1)S(1)}, u32[]{:S(2)}, u32[]{:S(2)}) collective-permute-start(bf16[256,1536]{1,0:T(8,128)(2,1)S(1)} %shard_map.68), channel_id=1, source_target_pairs={{0,2},{1,3},{2,0},{3,1},{4,6},{5,7},{6,4},{7,5},{16,18},{17,19},{1... | collective-permute-start | bytes 2359304 | tf_op jit(solution)/shard_map/ppermute | solution.py:56
  47.1 21.8 %collective-permute-start.4 = (bf16[256,1536]{1,0:T(8,128)(2,1)S(1)}, bf16[256,1536]{1,0:T(8,128)(2,1)S(1)}, u32[]{:S(2)}, u32[]{:S(2)}) collective-permute-start(bf16[256,1536]{1,0:T(8,128)(2,1)S(1)} %shard_map.72), channel_id=1, source_target_pairs={{0,6},{1,7},{2,4},{3,5},{4,2},{5,3},{6,0},{7,1},{16,22},{17,23},{1... | collective-permute-start | bytes 2359304 | tf_op jit(solution)/shard_map/ppermute | solution.py:56
  51.0 19.9 %collective-permute-start.13 = (bf16[192,1536]{1,0:T(8,128)(2,1)S(1)}, bf16[192,1536]{1,0:T(8,128)(2,1)S(1)}, u32[]{:S(2)}, u32[]{:S(2)}) collective-permute-start(bf16[192,1536]{1,0:T(8,128)(2,1)S(1)} %shard_map.78), channel_id=1, source_target_pairs={{0,8},{1,9},{2,10},{3,11},{4,12},{5,13},{6,14},{7,15},{16,24},{17,... | collective-permute-start | bytes 1769480 | tf_op jit(solution)/shard_map/ppermute | solution.py:56
  56.1 31.7 %collective-permute-start.12 = (bf16[320,1536]{1,0:T(8,128)(2,1)}, bf16[320,1536]{1,0:T(8,128)(2,1)}, u32[]{:S(2)}, u32[]{:S(2)}) collective-permute-start(bf16[320,1536]{1,0:T(8,128)(2,1)} %shard_map.76), channel_id=1, source_target_pairs={{0,8},{1,9},{2,10},{3,11},{4,12},{5,13},{6,14},{7,15},{16,24},{17,... | collective-permute-start | bytes 2949128 | tf_op jit(solution)/shard_map/ppermute | solution.py:56
  65.4 12.0 %collective-permute-start.5 = (bf16[128,1536]{1,0:T(8,128)(2,1)}, bf16[128,1536]{1,0:T(8,128)(2,1)}, u32[]{:S(2)}, u32[]{:S(2)}) collective-permute-start(bf16[128,1536]{1,0:T(8,128)(2,1)} %get-tuple-element.35.refs_1_), channel_id=1, source_target_pairs={{0,6},{1,7},{2,4},{3,5},{4,2},{5,3},{6,0},{7,1},{16,22},{17,23},{1... | collective-permute-start | bytes 1179656 | tf_op jit(solution)/shard_map/ppermute | solution.py:56
  70.8 9.3 %collective-permute-start.6 = (bf16[128,1536]{1,0:T(8,128)(2,1)S(1)}, bf16[128,1536]{1,0:T(8,128)(2,1)}, u32[]{:S(2)}, u32[]{:S(2)}) collective-permute-start(bf16[128,1536]{1,0:T(8,128)(2,1)S(1)} %get-tuple-element.37.refs_1_), channel_id=1, source_target_pairs={{0,2},{1,3},{2,0},{3,1},{4,6},{5,7},{6,4},{7,5},{16,18},{17,19},{1... | collective-permute-start | bytes 1179656 | tf_op jit(solution)/shard_map/ppermute | solution.py:56
  73.2 19.5 %all-to-all-start.2 = ((bf16[4,48,1536]{2,1,0:T(8,128)(2,1)}), bf16[4,48,1536]{2,1,0:T(8,128)(2,1)}, u32[]{:S(2)}, u32[]{:S(2)}) async-start(bf16[4,48,1536]{2,1,0:T(8,128)(2,1)} %bitcast.13), calls=%async_computation.2 | async-start | bytes 1179648 | tf_op jit(solution)/shard_map/all_to_all | solution.py:441
  85.2 11.1 %collective-permute-start.7 = (bf16[128,1536]{1,0:T(8,128)(2,1)}, bf16[128,1536]{1,0:T(8,128)(2,1)}, u32[]{:S(2)}, u32[]{:S(2)}) collective-permute-start(bf16[128,1536]{1,0:T(8,128)(2,1)} %get-tuple-element.39), channel_id=1, source_target_pairs={{0,8},{1,9},{2,10},{3,11},{4,12},{5,13},{6,14},{7,15},{16,24},{17,... | collective-permute-start | bytes 1179656 | tf_op jit(solution)/shard_map/ppermute | solution.py:56
  92.7 13.4 %all-to-all-start.1 = ((bf16[4,80,1536]{2,1,0:T(8,128)(2,1)}), bf16[4,80,1536]{2,1,0:T(8,128)(2,1)S(1)}, u32[]{:S(2)}, u32[]{:S(2)}) async-start(bf16[4,80,1536]{2,1,0:T(8,128)(2,1)} %bitcast.12), calls=%async_computation.1 | async-start | bytes 1966080 | tf_op jit(solution)/shard_map/all_to_all | solution.py:441
  98.7 14.7 %collective-permute-start.10 = (bf16[64,1536]{1,0:T(8,128)(2,1)}, bf16[64,1536]{1,0:T(8,128)(2,1)S(1)}, u32[]{:S(2)}, u32[]{:S(2)}) collective-permute-start(bf16[64,1536]{1,0:T(8,128)(2,1)} %get-tuple-element.65), channel_id=1, source_target_pairs={{0,2},{1,3},{2,0},{3,1},{4,6},{5,7},{6,4},{7,5},{16,18},{17,19},{1... | collective-permute-start | bytes 589832 | tf_op jit(solution)/shard_map/ppermute | solution.py:56
  100.1 11.9 %collective-permute-start.8 = (bf16[64,1536]{1,0:T(8,128)(2,1)}, bf16[64,1536]{1,0:T(8,128)(2,1)}, u32[]{:S(2)}, u32[]{:S(2)}) collective-permute-start(bf16[64,1536]{1,0:T(8,128)(2,1)} %get-tuple-element.67), channel_id=1, source_target_pairs={{0,6},{1,7},{2,4},{3,5},{4,2},{5,3},{6,0},{7,1},{16,22},{17,23},{1... | collective-permute-start | bytes 589832 | tf_op jit(solution)/shard_map/ppermute | solution.py:56
  107.5 9.7 %collective-permute-start.14 = (bf16[128,1536]{1,0:T(8,128)(2,1)S(1)}, bf16[128,1536]{1,0:T(8,128)(2,1)S(1)}, u32[]{:S(2)}, u32[]{:S(2)}) collective-permute-start(bf16[128,1536]{1,0:T(8,128)(2,1)S(1)} %shard_map.80), channel_id=1, source_target_pairs={{0,8},{1,9},{2,10},{3,11},{4,12},{5,13},{6,14},{7,15},{16,24},{17,... | collective-permute-start | bytes 1179656 | tf_op jit(solution)/shard_map/ppermute | solution.py:56
  113.1 7.0 %collective-permute-start.9 = (bf16[128,1536]{1,0:T(8,128)(2,1)S(1)}, bf16[128,1536]{1,0:T(8,128)(2,1)S(1)}, u32[]{:S(2)}, u32[]{:S(2)}) collective-permute-start(bf16[128,1536]{1,0:T(8,128)(2,1)S(1)} %pad_maximum_fusion.2), channel_id=1, source_target_pairs={{0,2},{1,3},{2,0},{3,1},{4,6},{5,7},{6,4},{7,5},{16,18},{17,19},{1... | collective-permute-start | bytes 1179656 | tf_op jit(solution)/shard_map/ppermute | solution.py:56
  114.4 8.2 %collective-permute-start.11 = (bf16[128,1536]{1,0:T(8,128)(2,1)S(1)}, bf16[128,1536]{1,0:T(8,128)(2,1)S(1)}, u32[]{:S(2)}, u32[]{:S(2)}) collective-permute-start(bf16[128,1536]{1,0:T(8,128)(2,1)S(1)} %pad_maximum_fusion.3), channel_id=1, source_target_pairs={{0,6},{1,7},{2,4},{3,5},{4,2},{5,3},{6,0},{7,1},{16,22},{17,23},{1... | collective-permute-start | bytes 1179656 | tf_op jit(solution)/shard_map/ppermute | solution.py:56
  122.7 10.7 %collective-permute-start.16 = (bf16[128,1536]{1,0:T(8,128)(2,1)S(1)}, bf16[128,1536]{1,0:T(8,128)(2,1)S(1)}, u32[]{:S(2)}, u32[]{:S(2)}) collective-permute-start(bf16[128,1536]{1,0:T(8,128)(2,1)S(1)} %get-tuple-element.44), channel_id=1, source_target_pairs={{0,6},{1,7},{2,4},{3,5},{4,2},{5,3},{6,0},{7,1},{16,22},{17,23},{1... | collective-permute-start | bytes 1179656 | tf_op jit(solution)/shard_map/ppermute | solution.py:56
  123.4 10.0 %collective-permute-start.17 = (bf16[128,1536]{1,0:T(8,128)(2,1)S(1)}, bf16[128,1536]{1,0:T(8,128)(2,1)S(1)}, u32[]{:S(2)}, u32[]{:S(2)}) collective-permute-start(bf16[128,1536]{1,0:T(8,128)(2,1)S(1)} %get-tuple-element.45), channel_id=1, source_target_pairs={{0,2},{1,3},{2,0},{3,1},{4,6},{5,7},{6,4},{7,5},{16,18},{17,19},{1... | collective-permute-start | bytes 1179656 | tf_op jit(solution)/shard_map/ppermute | solution.py:56
  123.4 10.1 %collective-permute-start.15 = (bf16[64,1536]{1,0:T(8,128)(2,1)S(1)}, bf16[64,1536]{1,0:T(8,128)(2,1)S(1)}, u32[]{:S(2)}, u32[]{:S(2)}) collective-permute-start(bf16[64,1536]{1,0:T(8,128)(2,1)S(1)} %slice.35), channel_id=1, source_target_pairs={{0,8},{1,9},{2,10},{3,11},{4,12},{5,13},{6,14},{7,15},{16,24},{17,... | collective-permute-start | bytes 589832 | tf_op jit(solution)/shard_map/ppermute | solution.py:56
  133.6 30.7 %collective-permute-start.18 = (bf16[288,1536]{1,0:T(8,128)(2,1)S(1)}, bf16[288,1536]{1,0:T(8,128)(2,1)}, u32[]{:S(2)}, u32[]{:S(2)}) collective-permute-start(bf16[288,1536]{1,0:T(8,128)(2,1)S(1)} %slice.36), channel_id=1, source_target_pairs={{0,8},{1,9},{2,10},{3,11},{4,12},{5,13},{6,14},{7,15},{16,24},{17,... | collective-permute-start | bytes 2654216 | tf_op jit(solution)/shard_map/ppermute | solution.py:56
  134.9 12.3 %collective-permute-start.21 = (bf16[256,1536]{1,0:T(8,128)(2,1)S(1)}, bf16[256,1536]{1,0:T(8,128)(2,1)S(1)}, u32[]{:S(2)}, u32[]{:S(2)}) collective-permute-start(bf16[256,1536]{1,0:T(8,128)(2,1)S(1)} %pad_maximum_fusion.refs_0_), channel_id=1, source_target_pairs={{0,1},{1,0},{2,3},{3,2},{4,5},{5,4},{6,7},{7,6},{16,17},{17,16},{1... | collective-permute-start | bytes 2359304 | tf_op jit(solution)/shard_map/ppermute | solution.py:56
  144.4 3.0 %collective-permute-start.22 = (bf16[256,1536]{1,0:T(8,128)(2,1)S(1)}, bf16[256,1536]{1,0:T(8,128)(2,1)S(1)}, u32[]{:S(2)}, u32[]{:S(2)}) collective-permute-start(bf16[256,1536]{1,0:T(8,128)(2,1)S(1)} %pad_maximum_fusion.1.refs_1_), channel_id=1, source_target_pairs={{0,1},{1,0},{2,3},{3,2},{4,5},{5,4},{6,7},{7,6},{16,17},{17,16},{1... | collective-permute-start | bytes 2359304 | tf_op jit(solution)/shard_map/ppermute | solution.py:56
  144.5 18.7 %collective-permute-start.19 = (bf16[256,1536]{1,0:T(8,128)(2,1)S(1)}, bf16[256,1536]{1,0:T(8,128)(2,1)S(1)}, u32[]{:S(2)}, u32[]{:S(2)}) collective-permute-start(bf16[256,1536]{1,0:T(8,128)(2,1)S(1)} %pad_maximum_fusion.refs_0_), channel_id=1, source_target_pairs={{0,2},{1,3},{2,0},{3,1},{4,6},{5,7},{6,4},{7,5},{16,18},{17,19},{1... | collective-permute-start | bytes 2359304 | tf_op jit(solution)/shard_map/ppermute | solution.py:56
  144.5 19.7 %collective-permute-start.20 = (bf16[256,1536]{1,0:T(8,128)(2,1)S(1)}, bf16[256,1536]{1,0:T(8,128)(2,1)S(1)}, u32[]{:S(2)}, u32[]{:S(2)}) collective-permute-start(bf16[256,1536]{1,0:T(8,128)(2,1)S(1)} %pad_maximum_fusion.1.refs_1_), channel_id=1, source_target_pairs={{0,6},{1,7},{2,4},{3,5},{4,2},{5,3},{6,0},{7,1},{16,22},{17,23},{1... | collective-permute-start | bytes 2359304 | tf_op jit(solution)/shard_map/ppermute | solution.py:56
  164.2 20.4 %collective-permute-start.26 = (bf16[512,1536]{1,0:T(8,128)(2,1)S(1)}, bf16[512,1536]{1,0:T(8,128)(2,1)}, u32[]{:S(2)}, u32[]{:S(2)}) collective-permute-start(bf16[512,1536]{1,0:T(8,128)(2,1)S(1)} %constant_dynamic-update-slice_fusion.refs_0_), channel_id=1, source_target_pairs={{0,1},{1,0},{2,3},{3,2},{4,5},{5,4},{6,7},{7,6},{16,17},{17,16},{1... | collective-permute-start | bytes 4718600 | tf_op jit(solution)/shard_map/ppermute | solution.py:56
  165.8 4.7 %collective-permute-start.23 = (bf16[256,1536]{1,0:T(8,128)(2,1)S(1)}, bf16[256,1536]{1,0:T(8,128)(2,1)S(1)}, u32[]{:S(2)}, u32[]{:S(2)}) collective-permute-start(bf16[256,1536]{1,0:T(8,128)(2,1)S(1)} %collective-permute-done.19.refs_2_), channel_id=1, source_target_pairs={{0,1},{1,0},{2,3},{3,2},{4,5},{5,4},{6,7},{7,6},{16,17},{17,16},{1... | collective-permute-start | bytes 2359304 | tf_op jit(solution)/shard_map/ppermute | solution.py:56
  165.8 5.3 %collective-permute-start.24 = (bf16[256,1536]{1,0:T(8,128)(2,1)S(1)}, bf16[256,1536]{1,0:T(8,128)(2,1)S(1)}, u32[]{:S(2)}, u32[]{:S(2)}) collective-permute-start(bf16[256,1536]{1,0:T(8,128)(2,1)S(1)} %collective-permute-done.20.refs_3_), channel_id=1, source_target_pairs={{0,1},{1,0},{2,3},{3,2},{4,5},{5,4},{6,7},{7,6},{16,17},{17,16},{1... | collective-permute-start | bytes 2359304 | tf_op jit(solution)/shard_map/ppermute | solution.py:56
  167.1 14.9 %collective-permute-start.25 = (bf16[160,1536]{1,0:T(8,128)(2,1)}, bf16[160,1536]{1,0:T(8,128)(2,1)}, u32[]{:S(2)}, u32[]{:S(2)}) collective-permute-start(bf16[160,1536]{1,0:T(8,128)(2,1)} %slice.37), channel_id=1, source_target_pairs={{0,8},{1,9},{2,10},{3,11},{4,12},{5,13},{6,14},{7,15},{16,24},{17,... | collective-permute-start | bytes 1474568 | tf_op jit(solution)/shard_map/ppermute | solution.py:56
  170.2 14.1 %collective-permute-start.28 = (bf16[288,1536]{1,0:T(8,128)(2,1)}, bf16[288,1536]{1,0:T(8,128)(2,1)}, u32[]{:S(2)}, u32[]{:S(2)}) collective-permute-start(bf16[288,1536]{1,0:T(8,128)(2,1)} %collective-permute-done.18.refs_2_), channel_id=1, source_target_pairs={{0,1},{1,0},{2,3},{3,2},{4,5},{5,4},{6,7},{7,6},{16,17},{17,16},{1... | collective-permute-start | bytes 2654216 | tf_op jit(solution)/shard_map/ppermute | solution.py:56
  177.8 16.1 %all-to-all-start.3 = ((bf16[8,128,384]{2,1,0:T(8,128)(2,1)}), bf16[8,128,384]{2,1,0:T(8,128)(2,1)S(1)}, u32[]{:S(2)}, u32[]{:S(2)}) async-start(bf16[8,128,384]{2,1,0:T(8,128)(2,1)} %copy-done.18), calls=%async_computation.3 | async-start | bytes 1572864 | tf_op jit(solution)/shard_map/all_to_all | solution.py:478
  (29 other events, 142.4 us)

commit v3 on v2

--- a/solution.py
+++ b/solution.py
@@ -194,13 +194,13 @@
         step(pl.ds(pl.multiple_of(i * tile, tile), tile))
 
 
-def fold(place, held, second):
+def fold(place, held, second, earlier):
     count = len(held)
     rows, width = held[0].shape
     half = rows // 2
 
     def kernel(place_ref, *refs):
-        own_ref, send_ref = refs[2 * count :]
+        own_ref, send_ref = refs[-2:]
 
         def step(at):
             for i in range(count):
@@ -214,7 +214,7 @@
     return kernel_call(
         kernel,
         place,
-        (*held, *second),
+        (*held, *second, *earlier),
         [IN_VMEM, IN_VMEM],
         [jax.ShapeDtypeStruct(out, jnp.float32), jax.ShapeDtypeStruct(out, jnp.bfloat16)],
     )
@@ -439,7 +439,7 @@
         sums = partial_sums(place, raws, 0, near_half, w_out_both, 0, got, earlier=earlier)
         earlier = ()
         terms.append(lax.all_to_all(sums, "col", 0, 0, axis_index_groups=Z_GROUPS, tiled=True))
-    own_sums, to_send = fold(place, held, second)
+    own_sums, to_send = fold(place, held, second, [sums])
     far = swap(to_send, "y")
     q = quarter // 4
 
@@ -453,19 +453,17 @@
     far = swap(pre_share, "y")
     two = [jnp.concatenate([pre_share[i : i + q], far[i : i + q]]) for i in (0, q)]
 
-    gelu_keep, two = lax.optimization_barrier((gelu_keep, two))
-    cuts = (0, quarter // 4, 11 * quarter // 8)
-    gelu_far = [swap(gelu_keep[: cuts[1]], "y")]
     pre_keep = [jnp.concatenate([t, swap(t, order[1])]) for t, order in zip(two, TOKEN_ORDERS)]
 
-    gelu_far[0], pre_keep, gelu_keep = lax.optimization_barrier((gelu_far[0], pre_keep, gelu_keep))
-    gelu_far.append(swap(gelu_keep[cuts[1] : cuts[2]], "y"))
+    gelu_keep, pre_keep = together(gelu_keep, pre_keep)
+    cut = 21 * quarter // 16
+    gelu_far = [swap(gelu_keep[:cut], "y")]
     pre_first = [swap(k, order[0]) for k, order in zip(pre_keep, TOKEN_ORDERS)]
     pre_keep_other = [swap(k, "core") for k in pre_keep]
     kept = input_sums(place, pre_keep, pre_keep_other, w_in)
 
-    gelu_far[1], pre_first, kept, gelu_keep = lax.optimization_barrier((gelu_far[1], pre_first, kept, gelu_keep))
-    gelu_far.append(swap(gelu_keep[cuts[2] :], "y"))
+    gelu_far[0], pre_first, kept, gelu_keep = together(gelu_far[0], pre_first, kept, gelu_keep)
+    gelu_far.append(swap(gelu_keep[cut:], "y"))
     pre_first_other = [swap(f, "core") for f in pre_first]
     sums, w_in_grad = input_sums_and_grad(
         place,
@@ -476,7 +474,7 @@
         tok_features,
     )
     parts = lax.all_to_all(sums, "row", 0, 0, tiled=True)
-    w_in_grad, gelu_far[2] = together(w_in_grad, gelu_far[2])
+    w_in_grad, gelu_far[1] = together(w_in_grad, gelu_far[1])
     gelu_mine = (gelu_keep, *gelu_far)
     gelu_other = [swap(g, "core") for g in gelu_mine]
     w_out_grad = weight_grad(place, gelu_mine, gelu_other, grad_features)

time: 197 us -> 190 us (0.964)
  starting transfers between devices: 67 us -> 57.3 us
  waiting for transfers between devices: 67.7 us -> 70.7 us
    ppermute x30 -> x28, starting transfers between devices: 50.4 us -> 40.7 us  [swap(): return lax.ppermute(values, AXES, FLIPS[name])]
    ppermute x30 -> x28, waiting for transfers between devices: 41.5 us -> 43.8 us  [swap(): return lax.ppermute(values, AXES, FLIPS[name])]
    unnamed x58 -> x64, local copies, waits for them, and re-layouts: 14.4 us -> 15.4 us
  transfers between devices with their start and end apart: 34 -> 32, of which waited for: 19 -> 20; matrix products, arithmetic and copies ran while one was open for 3% -> 3% of each run, Pallas kernels for 18% -> 18%
where the time goes in v3:
time: 190 us
  waiting for transfers between devices  70.7 us (37%)
  starting transfers between devices  57.3 us (30%)
  Pallas kernels  37.2 us (20%)
  local copies, waits for them, and re-layouts  21 us (11%)
  other arithmetic  2.31 us (1%)
    ppermute x28, waiting for transfers between devices, swap(): return lax.ppermute(values, AXES, FLIPS[name])  43.8 us
    ppermute x28, starting transfers between devices, swap(): return lax.ppermute(values, AXES, FLIPS[name])  40.7 us
    pallas_call x18, Pallas kernels, kernel_call(): pl.pallas_call(kernel, in_specs=[pl.BlockSpec(memory_space=pltpu.SMEM)] +...  37.2 us
    all_to_all x1, waiting for transfers between devices, body(): raw = lax.all_to_all(copies, 'row', 0, 0, tiled=True)  18.8 us
    unnamed x64, local copies, waits for them, and re-layouts  15.4 us
    all_to_all x2, starting transfers between devices, body(): lax.all_to_all(sums, 'col', 0, 0, axis_index_groups=Z_GROUPS, tiled=True)  7.79 us
    all_to_all x1, starting transfers between devices, body(): raw = lax.all_to_all(copies, 'row', 0, 0, tiled=True)  5.12 us
    all_to_all x2, waiting for transfers between devices, body(): lax.all_to_all(sums, 'col', 0, 0, axis_index_groups=Z_GROUPS, tiled=True)  4.11 us
  transfers between devices with their start and end apart: 32, of which 20 were waited for; matrix products, arithmetic and copies ran while one was open for 3% of the time, Pallas kernels for 18%

profile of v3, /device:TPU:1, one launch (start us, length us, event | category | flops | bytes accessed | tf_op | source)
XLA Modules:
  0.0 189.6 jit_solution(12677261631202423569)
XLA Ops:
  0.7 2.4 %constant_dynamic-slice_fusion = bf16[384,1536]{1,0:T(8,128)(2,1)} fusion(bf16[384,3072]{1,0:T(8,128)(2,1)} %refs_8_.1, s32[]{:T(128)S(6)} %select_n.26), kind=kLoop, calls=%fused_computation.13 | loop fusion | bytes 2359300 | tf_op jit(solution)/shard_map/dynamic_slice | solution.py:396
  6.4 5.1 %all-to-all-start = ((bf16[8,2,128,384]{3,2,1,0:T(8,128)(2,1)}), bf16[8,2,128,384]{3,2,1,0:T(8,128)(2,1)S(1)}, u32[]{:S(2)}, u32[]{:S(2)}) async-start(bf16[8,2,128,384]{3,2,1,0:T(8,128)(2,1)} %copy-done.15), calls=%async_computation | async-start | bytes 3145728 | tf_op jit(solution)/shard_map/all_to_all | solution.py:393
  16.9 18.8 %all-to-all-done.l_ref.raw_ref = bf16[8,2,128,384]{3,2,1,0:T(8,128)(2,1)S(1)} async-done(((bf16[8,2,128,384]{3,2,1,0:T(8,128)(2,1)}), bf16[8,2,128,384]{3,2,1,0:T(8,128)(2,1)S(1)}, u32[]{:S(2)}, u32[]{:S(2)}) %all-to-all-start) | async-done | bytes 1572896 | tf_op jit(solution)/shard_map/all_to_all | solution.py:393
  36.8 3.0 %collective-permute-done.2.lo_ref = bf16[8,2,128,384]{3,2,1,0:T(8,128)(2,1)S(1)} collective-permute-done((bf16[8,2,128,384]{3,2,1,0:T(8,128)(2,1)S(1)}, bf16[8,2,128,384]{3,2,1,0:T(8,128)(2,1)S(1)}, u32[]{:S(2)}, u32[]{:S(2)}) %collective-permute-start.2) | collective-permute-done | bytes 1572896 | tf_op jit(solution)/shard_map/ppermute | solution.py:56
  47.1 2.3 %collective-permute-start.4 = (bf16[256,1536]{1,0:T(8,128)(2,1)S(1)}, bf16[256,1536]{1,0:T(8,128)(2,1)S(1)}, u32[]{:S(2)}, u32[]{:S(2)}) collective-permute-start(bf16[256,1536]{1,0:T(8,128)(2,1)S(1)} %shard_map.72), channel_id=1, source_target_pairs={{0,6},{1,7},{2,4},{3,5},{4,2},{5,3},{6,0},{7,1},{16,22},{17,23},{1... | collective-permute-start | bytes 2359304 | tf_op jit(solution)/shard_map/ppermute | solution.py:56
  51.0 2.7 %collective-permute-start.7 = (bf16[192,1536]{1,0:T(8,128)(2,1)S(1)}, bf16[192,1536]{1,0:T(8,128)(2,1)S(1)}, u32[]{:S(2)}, u32[]{:S(2)}) collective-permute-start(bf16[192,1536]{1,0:T(8,128)(2,1)S(1)} %shard_map.74), channel_id=1, source_target_pairs={{0,8},{1,9},{2,10},{3,11},{4,12},{5,13},{6,14},{7,15},{16,24},{17,... | collective-permute-start | bytes 1769480 | tf_op jit(solution)/shard_map/ppermute | solution.py:56
  53.7 2.5 %shard_map.78 = bf16[320,1536]{1,0:T(8,128)(2,1)} custom-call(s32[4]{0:T(128)S(1)} %pad_add_fusion.place_ref, bf16[8,2,128,384]{3,2,1,0:T(8,128)(2,1)S(1)} %all-to-all-done.l_ref.raw_ref, bf16[8,2,128,384]{3,2,1,0:T(8,128)(2,1)S(1)} %collective-permute-done.2.lo_ref, bf16[3072,384]{1,0:T(8,128)(2,1)S(1)} %copy-done.3, bf16[1536,384]{1,0:T(8,128)(2,1)S(1)} %copy-done.6), custom_call_target="tpu_custom_call" | custom-call | tf_op jit(solution)/shard_map/pallas_call | solution.py:78
  58.2 5.1 %collective-permute-done.3.refs_0_ = bf16[256,1536]{1,0:T(8,128)(2,1)S(1)} collective-permute-done((bf16[256,1536]{1,0:T(8,128)(2,1)S(1)}, bf16[256,1536]{1,0:T(8,128)(2,1)S(1)}, u32[]{:S(2)}, u32[]{:S(2)}) %collective-permute-start.3) | collective-permute-done | bytes 786464 | tf_op jit(solution)/shard_map/ppermute | solution.py:56
  63.3 2.1 %shard_map.71 = (bf16[128,1536]{1,0:T(8,128)(2,1)S(1)}, bf16[128,1536]{1,0:T(8,128)(2,1)}) custom-call(s32[4]{0:T(128)S(1)} %pad_add_fusion.place_ref, bf16[8,2,128,384]{3,2,1,0:T(8,128)(2,1)S(1)} %all-to-all-done.l_ref.raw_ref, bf16[8,2,128,384]{3,2,1,0:T(8,128)(2,1)S(1)} %collective-permute-done.2.lo_ref, bf16[384,3072]{1,0:T(8,128)(2,1)S(1)} %copy-done.1, ...), custom_call_target="tpu_custom_call" | custom-call | tf_op jit(solution)/shard_map/pallas_call | solution.py:78
  65.4 3.5 %collective-permute-start.5 = (bf16[128,1536]{1,0:T(8,128)(2,1)}, bf16[128,1536]{1,0:T(8,128)(2,1)}, u32[]{:S(2)}, u32[]{:S(2)}) collective-permute-start(bf16[128,1536]{1,0:T(8,128)(2,1)} %get-tuple-element.31.refs_1_), channel_id=1, source_target_pairs={{0,6},{1,7},{2,4},{3,5},{4,2},{5,3},{6,0},{7,1},{16,22},{17,23},{1... | collective-permute-start | bytes 1179656 | tf_op jit(solution)/shard_map/ppermute | solution.py:56
  68.9 1.8 shard_map.73
  73.2 4.1 %all-to-all-start.2 = ((bf16[4,48,1536]{2,1,0:T(8,128)(2,1)}), bf16[4,48,1536]{2,1,0:T(8,128)(2,1)}, u32[]{:S(2)}, u32[]{:S(2)}) async-start(bf16[4,48,1536]{2,1,0:T(8,128)(2,1)} %bitcast.11), calls=%async_computation.2 | async-start | bytes 1179648 | tf_op jit(solution)/shard_map/all_to_all | solution.py:441
  77.4 2.6 %collective-permute-done.6.refs_3_ = bf16[128,1536]{1,0:T(8,128)(2,1)} collective-permute-done((bf16[128,1536]{1,0:T(8,128)(2,1)S(1)}, bf16[128,1536]{1,0:T(8,128)(2,1)}, u32[]{:S(2)}, u32[]{:S(2)}) %collective-permute-start.6) | collective-permute-done | bytes 393248 | tf_op jit(solution)/shard_map/ppermute | solution.py:56
  83.1 2.2 %shard_map.76 = (f32[128,1536]{1,0:T(8,128)S(1)}, bf16[128,1536]{1,0:T(8,128)(2,1)}) custom-call(s32[4]{0:T(128)S(1)} %pad_add_fusion.place_ref, bf16[128,1536]{1,0:T(8,128)(2,1)S(1)} %copy-done.23, bf16[128,1536]{1,0:T(8,128)(2,1)S(1)} %copy-done.25, bf16[128,1536]{1,0:T(8,128)(2,1)} %collective-permute-done.5.refs_2_, ...), custom_call_target="tpu_custom_call" | custom-call | tf_op jit(solution)/shard_map/pallas_call | solution.py:78
  86.2 2.6 %collective-permute-start.8 = (bf16[128,1536]{1,0:T(8,128)(2,1)}, bf16[128,1536]{1,0:T(8,128)(2,1)}, u32[]{:S(2)}, u32[]{:S(2)}) collective-permute-start(bf16[128,1536]{1,0:T(8,128)(2,1)} %get-tuple-element.36), channel_id=1, source_target_pairs={{0,8},{1,9},{2,10},{3,11},{4,12},{5,13},{6,14},{7,15},{16,24},{17,... | collective-permute-start | bytes 1179656 | tf_op jit(solution)/shard_map/ppermute | solution.py:56
  90.5 2.2 %shard_map.79 = bf16[320,1536]{1,0:T(8,128)(2,1)S(1)} custom-call(s32[4]{0:T(128)S(1)} %pad_add_fusion.place_ref, bf16[8,2,128,384]{3,2,1,0:T(8,128)(2,1)S(1)} %all-to-all-done.l_ref.raw_ref, bf16[8,2,128,384]{3,2,1,0:T(8,128)(2,1)S(1)} %collective-permute-done.2.lo_ref, bf16[3072,384]{1,0:T(8,128)(2,1)S(1)} %copy-done.4, bf16[1536,384]{1,0:T(8,128)(2,1)S(1)} %copy-done.7, ...), custom_call_target="tpu_custom_call" | custom-call | tf_op jit(solution)/shard_map/pallas_call | solution.py:78
  93.6 3.6 %all-to-all-start.1 = ((bf16[4,80,1536]{2,1,0:T(8,128)(2,1)}), bf16[4,80,1536]{2,1,0:T(8,128)(2,1)S(1)}, u32[]{:S(2)}, u32[]{:S(2)}) async-start(bf16[4,80,1536]{2,1,0:T(8,128)(2,1)} %bitcast.13), calls=%async_computation.1 | async-start | bytes 1966080 | tf_op jit(solution)/shard_map/all_to_all | solution.py:441
  101.1 1.8 collective-permute-start.9
  102.9 4.1 %all-to-all-done.1 = bf16[4,80,1536]{2,1,0:T(8,128)(2,1)S(1)} async-done(((bf16[4,80,1536]{2,1,0:T(8,128)(2,1)}), bf16[4,80,1536]{2,1,0:T(8,128)(2,1)S(1)}, u32[]{:S(2)}, u32[]{:S(2)}) %all-to-all-start.1) | async-done | bytes 983072 | tf_op jit(solution)/shard_map/all_to_all | solution.py:441
  108.5 2.6 %collective-permute-start.14 = (bf16[128,1536]{1,0:T(8,128)(2,1)S(1)}, bf16[128,1536]{1,0:T(8,128)(2,1)S(1)}, u32[]{:S(2)}, u32[]{:S(2)}) collective-permute-start(bf16[128,1536]{1,0:T(8,128)(2,1)S(1)} %shard_map.80), channel_id=1, source_target_pairs={{0,8},{1,9},{2,10},{3,11},{4,12},{5,13},{6,14},{7,15},{16,24},{17,... | collective-permute-start | bytes 1179656 | tf_op jit(solution)/shard_map/ppermute | solution.py:56
  119.0 2.8 %collective-permute-done.12 = bf16[128,1536]{1,0:T(8,128)(2,1)S(1)} collective-permute-done((bf16[128,1536]{1,0:T(8,128)(2,1)S(1)}, bf16[128,1536]{1,0:T(8,128)(2,1)S(1)}, u32[]{:S(2)}, u32[]{:S(2)}) %collective-permute-start.12) | collective-permute-done | bytes 393248 | tf_op jit(solution)/shard_map/ppermute | solution.py:56
  121.8 4.8 %collective-permute-done.15 = bf16[128,1536]{1,0:T(8,128)(2,1)S(1)} collective-permute-done((bf16[128,1536]{1,0:T(8,128)(2,1)S(1)}, bf16[128,1536]{1,0:T(8,128)(2,1)S(1)}, u32[]{:S(2)}, u32[]{:S(2)}) %collective-permute-start.15) | collective-permute-done | bytes 393248 | tf_op jit(solution)/shard_map/ppermute | solution.py:56
  127.2 4.0 %collective-permute-start.17 = (bf16[336,1536]{1,0:T(8,128)(2,1)S(1)}, bf16[336,1536]{1,0:T(8,128)(2,1)}, u32[]{:S(2)}, u32[]{:S(2)}) collective-permute-start(bf16[336,1536]{1,0:T(8,128)(2,1)S(1)} %slice.32), channel_id=1, source_target_pairs={{0,8},{1,9},{2,10},{3,11},{4,12},{5,13},{6,14},{7,15},{16,24},{17,... | collective-permute-start | bytes 3096584 | tf_op jit(solution)/shard_map/ppermute | solution.py:56
  131.2 6.1 %collective-permute-start.20 = (bf16[256,1536]{1,0:T(8,128)(2,1)S(1)}, bf16[256,1536]{1,0:T(8,128)(2,1)S(1)}, u32[]{:S(2)}, u32[]{:S(2)}) collective-permute-start(bf16[256,1536]{1,0:T(8,128)(2,1)S(1)} %pad_maximum_fusion.refs_0_), channel_id=1, source_target_pairs={{0,1},{1,0},{2,3},{3,2},{4,5},{5,4},{6,7},{7,6},{16,17},{17,16},{1... | collective-permute-start | bytes 2359304 | tf_op jit(solution)/shard_map/ppermute | solution.py:56
  137.4 1.8 collective-permute-start.19
  140.4 2.3 %shard_map.81.refs_9_ = bf16[8,64,384]{2,1,0:T(8,128)(2,1)S(1)} custom-call(s32[4]{0:T(128)S(1)} %pad_add_fusion.place_ref, bf16[256,1536]{1,0:T(8,128)(2,1)S(1)} %pad_maximum_fusion.refs_0_, bf16[256,1536]{1,0:T(8,128)(2,1)S(1)} %pad_maximum_fusion.1.refs_1_, bf16[256,1536]{1,0:T(8,128)(2,1)S(1)} %collective-permute-done.20.refs_2_.refs_4_, ...), custom_call_target="tpu_custom_call" | custom-call | tf_op jit(solution)/shard_map/pallas_call | solution.py:78
  142.7 13.2 %collective-permute-done.18.refs_2_ = bf16[256,1536]{1,0:T(8,128)(2,1)S(1)} collective-permute-done((bf16[256,1536]{1,0:T(8,128)(2,1)S(1)}, bf16[256,1536]{1,0:T(8,128)(2,1)S(1)}, u32[]{:S(2)}, u32[]{:S(2)}) %collective-permute-start.18) | collective-permute-done | bytes 786464 | tf_op jit(solution)/shard_map/ppermute | solution.py:56
  162.6 2.2 %collective-permute-done.23.refs_7_ = bf16[256,1536]{1,0:T(8,128)(2,1)S(1)} collective-permute-done((bf16[256,1536]{1,0:T(8,128)(2,1)S(1)}, bf16[256,1536]{1,0:T(8,128)(2,1)S(1)}, u32[]{:S(2)}, u32[]{:S(2)}) %collective-permute-start.23) | collective-permute-done | bytes 786464 | tf_op jit(solution)/shard_map/ppermute | solution.py:56
  164.9 5.8 %shard_map.82 = (bf16[8,128,384]{2,1,0:T(8,128)(2,1)S(1)}, f32[384,3072]{1,0:T(8,128)}) custom-call(s32[4]{0:T(128)S(1)} %pad_add_fusion.place_ref, bf16[256,1536]{1,0:T(8,128)(2,1)S(1)} %pad_maximum_fusion.refs_0_, bf16[256,1536]{1,0:T(8,128)(2,1)S(1)} %pad_maximum_fusion.1.refs_1_, bf16[256,1536]{1,0:T(8,128)(2,1)S(1)} %collective-permute-done.18.refs_2_, ...), custom_call_target="tpu_custom_call" | custom-call | tf_op jit(solution)/shard_map/pallas_call | solution.py:78
  171.6 3.7 %all-to-all-start.3 = ((bf16[8,128,384]{2,1,0:T(8,128)(2,1)}), bf16[8,128,384]{2,1,0:T(8,128)(2,1)S(1)}, u32[]{:S(2)}, u32[]{:S(2)}) async-start(bf16[8,128,384]{2,1,0:T(8,128)(2,1)} %copy-done.19), calls=%async_computation.3 | async-start | bytes 1572864 | tf_op jit(solution)/shard_map/all_to_all | solution.py:476
  178.2 6.1 %shard_map.83 = f32[3072,384]{1,0:T(8,128)} custom-call(s32[4]{0:T(128)S(1)} %pad_add_fusion.place_ref, bf16[512,1536]{1,0:T(8,128)(2,1)S(1)} %constant_dynamic-update-slice_fusion.refs_0_, bf16[336,1536]{1,0:T(8,128)(2,1)} %collective-permute-done.17.refs_1_, bf16[176,1536]{1,0:T(8,128)(2,1)} %collective-permute-done.24.refs_2_, ...), custom_call_target="tpu_custom_call" | custom-call | tf_op jit(solution)/shard_map/pallas_call | solution.py:78
  184.3 4.0 %all-to-all-done.3.parts_ref = bf16[8,128,384]{2,1,0:T(8,128)(2,1)S(1)} async-done(((bf16[8,128,384]{2,1,0:T(8,128)(2,1)}), bf16[8,128,384]{2,1,0:T(8,128)(2,1)S(1)}, u32[]{:S(2)}, u32[]{:S(2)}) %all-to-all-start.3) | async-done | bytes 786464 | tf_op jit(solution)/shard_map/all_to_all | solution.py:476
  (129 shorter events, 56.3 us)
Async XLA Ops:
  3.1 10.2 %collective-permute-start.1 = (bf16[384,1536]{1,0:T(8,128)(2,1)}, bf16[384,1536]{1,0:T(8,128)(2,1)S(1)}, u32[]{:S(2)}, u32[]{:S(2)}) collective-permute-start(bf16[384,1536]{1,0:T(8,128)(2,1)} %constant_dynamic-slice_fusion), channel_id=1, source_target_pairs={{0,1},{1,0},{2,3},{3,2},{4,5},{5,4},{6,7},{7,6},{16,17},{17,16},{1... | collective-permute-start | bytes 3538952 | tf_op jit(solution)/shard_map/ppermute | solution.py:56
  6.4 29.2 %all-to-all-start = ((bf16[8,2,128,384]{3,2,1,0:T(8,128)(2,1)}), bf16[8,2,128,384]{3,2,1,0:T(8,128)(2,1)S(1)}, u32[]{:S(2)}, u32[]{:S(2)}) async-start(bf16[8,2,128,384]{3,2,1,0:T(8,128)(2,1)} %copy-done.15), calls=%async_computation | async-start | bytes 3145728 | tf_op jit(solution)/shard_map/all_to_all | solution.py:393
  12.9 2.9 %collective-permute-start = (bf16[1536,384]{1,0:T(8,128)(2,1)S(1)}, bf16[1536,384]{1,0:T(8,128)(2,1)S(1)}, u32[]{:S(2)}, u32[]{:S(2)}) collective-permute-start(bf16[1536,384]{1,0:T(8,128)(2,1)S(1)} %constant_dynamic-slice_fusion.1), channel_id=1, source_target_pairs={{0,1},{1,0},{2,3},{3,2},{4,5},{5,4},{6,7},{7,6},{16,17},{17,16},{1... | collective-permute-start | bytes 3538952 | tf_op jit(solution)/shard_map/ppermute | solution.py:56
  35.7 4.1 %collective-permute-start.2 = (bf16[8,2,128,384]{3,2,1,0:T(8,128)(2,1)S(1)}, bf16[8,2,128,384]{3,2,1,0:T(8,128)(2,1)S(1)}, u32[]{:S(2)}, u32[]{:S(2)}) collective-permute-start(bf16[8,2,128,384]{3,2,1,0:T(8,128)(2,1)S(1)} %all-to-all-done.l_ref.raw_ref), channel_id=1, source_target_pairs={{0,1},{1,0},{2,3},{3,2},{4,5},{5,4},{6,7},{7,6},{16,17},{17,16},{1... | collective-permute-start | bytes 4718600 | tf_op jit(solution)/shard_map/ppermute | solution.py:56
  44.1 19.2 %collective-permute-start.3 = (bf16[256,1536]{1,0:T(8,128)(2,1)S(1)}, bf16[256,1536]{1,0:T(8,128)(2,1)S(1)}, u32[]{:S(2)}, u32[]{:S(2)}) collective-permute-start(bf16[256,1536]{1,0:T(8,128)(2,1)S(1)} %shard_map.68), channel_id=1, source_target_pairs={{0,2},{1,3},{2,0},{3,1},{4,6},{5,7},{6,4},{7,5},{16,18},{17,19},{1... | collective-permute-start | bytes 2359304 | tf_op jit(solution)/shard_map/ppermute | solution.py:56
  47.1 21.7 %collective-permute-start.4 = (bf16[256,1536]{1,0:T(8,128)(2,1)S(1)}, bf16[256,1536]{1,0:T(8,128)(2,1)S(1)}, u32[]{:S(2)}, u32[]{:S(2)}) collective-permute-start(bf16[256,1536]{1,0:T(8,128)(2,1)S(1)} %shard_map.72), channel_id=1, source_target_pairs={{0,6},{1,7},{2,4},{3,5},{4,2},{5,3},{6,0},{7,1},{16,22},{17,23},{1... | collective-permute-start | bytes 2359304 | tf_op jit(solution)/shard_map/ppermute | solution.py:56
  51.0 19.9 %collective-permute-start.7 = (bf16[192,1536]{1,0:T(8,128)(2,1)S(1)}, bf16[192,1536]{1,0:T(8,128)(2,1)S(1)}, u32[]{:S(2)}, u32[]{:S(2)}) collective-permute-start(bf16[192,1536]{1,0:T(8,128)(2,1)S(1)} %shard_map.74), channel_id=1, source_target_pairs={{0,8},{1,9},{2,10},{3,11},{4,12},{5,13},{6,14},{7,15},{16,24},{17,... | collective-permute-start | bytes 1769480 | tf_op jit(solution)/shard_map/ppermute | solution.py:56
  56.1 32.7 %collective-permute-start.13 = (bf16[320,1536]{1,0:T(8,128)(2,1)}, bf16[320,1536]{1,0:T(8,128)(2,1)}, u32[]{:S(2)}, u32[]{:S(2)}) collective-permute-start(bf16[320,1536]{1,0:T(8,128)(2,1)} %shard_map.78), channel_id=1, source_target_pairs={{0,8},{1,9},{2,10},{3,11},{4,12},{5,13},{6,14},{7,15},{16,24},{17,... | collective-permute-start | bytes 2949128 | tf_op jit(solution)/shard_map/ppermute | solution.py:56
  65.4 12.0 %collective-permute-start.5 = (bf16[128,1536]{1,0:T(8,128)(2,1)}, bf16[128,1536]{1,0:T(8,128)(2,1)}, u32[]{:S(2)}, u32[]{:S(2)}) collective-permute-start(bf16[128,1536]{1,0:T(8,128)(2,1)} %get-tuple-element.31.refs_1_), channel_id=1, source_target_pairs={{0,6},{1,7},{2,4},{3,5},{4,2},{5,3},{6,0},{7,1},{16,22},{17,23},{1... | collective-permute-start | bytes 1179656 | tf_op jit(solution)/shard_map/ppermute | solution.py:56
  70.8 9.3 %collective-permute-start.6 = (bf16[128,1536]{1,0:T(8,128)(2,1)S(1)}, bf16[128,1536]{1,0:T(8,128)(2,1)}, u32[]{:S(2)}, u32[]{:S(2)}) collective-permute-start(bf16[128,1536]{1,0:T(8,128)(2,1)S(1)} %get-tuple-element.33.refs_1_), channel_id=1, source_target_pairs={{0,2},{1,3},{2,0},{3,1},{4,6},{5,7},{6,4},{7,5},{16,18},{17,19},{1... | collective-permute-start | bytes 1179656 | tf_op jit(solution)/shard_map/ppermute | solution.py:56
  73.2 20.5 %all-to-all-start.2 = ((bf16[4,48,1536]{2,1,0:T(8,128)(2,1)}), bf16[4,48,1536]{2,1,0:T(8,128)(2,1)}, u32[]{:S(2)}, u32[]{:S(2)}) async-start(bf16[4,48,1536]{2,1,0:T(8,128)(2,1)} %bitcast.11), calls=%async_computation.2 | async-start | bytes 1179648 | tf_op jit(solution)/shard_map/all_to_all | solution.py:441
  86.2 11.1 %collective-permute-start.8 = (bf16[128,1536]{1,0:T(8,128)(2,1)}, bf16[128,1536]{1,0:T(8,128)(2,1)}, u32[]{:S(2)}, u32[]{:S(2)}) collective-permute-start(bf16[128,1536]{1,0:T(8,128)(2,1)} %get-tuple-element.36), channel_id=1, source_target_pairs={{0,8},{1,9},{2,10},{3,11},{4,12},{5,13},{6,14},{7,15},{16,24},{17,... | collective-permute-start | bytes 1179656 | tf_op jit(solution)/shard_map/ppermute | solution.py:56
  93.6 13.4 %all-to-all-start.1 = ((bf16[4,80,1536]{2,1,0:T(8,128)(2,1)}), bf16[4,80,1536]{2,1,0:T(8,128)(2,1)S(1)}, u32[]{:S(2)}, u32[]{:S(2)}) async-start(bf16[4,80,1536]{2,1,0:T(8,128)(2,1)} %bitcast.13), calls=%async_computation.1 | async-start | bytes 1966080 | tf_op jit(solution)/shard_map/all_to_all | solution.py:441
  99.7 12.8 %collective-permute-start.11 = (bf16[64,1536]{1,0:T(8,128)(2,1)}, bf16[64,1536]{1,0:T(8,128)(2,1)S(1)}, u32[]{:S(2)}, u32[]{:S(2)}) collective-permute-start(bf16[64,1536]{1,0:T(8,128)(2,1)} %get-tuple-element.57), channel_id=1, source_target_pairs={{0,2},{1,3},{2,0},{3,1},{4,6},{5,7},{6,4},{7,5},{16,18},{17,19},{1... | collective-permute-start | bytes 589832 | tf_op jit(solution)/shard_map/ppermute | solution.py:56
  101.1 10.0 %collective-permute-start.9 = (bf16[64,1536]{1,0:T(8,128)(2,1)}, bf16[64,1536]{1,0:T(8,128)(2,1)}, u32[]{:S(2)}, u32[]{:S(2)}) collective-permute-start(bf16[64,1536]{1,0:T(8,128)(2,1)} %get-tuple-element.59), channel_id=1, source_target_pairs={{0,6},{1,7},{2,4},{3,5},{4,2},{5,3},{6,0},{7,1},{16,22},{17,23},{1... | collective-permute-start | bytes 589832 | tf_op jit(solution)/shard_map/ppermute | solution.py:56
  108.5 8.2 %collective-permute-start.14 = (bf16[128,1536]{1,0:T(8,128)(2,1)S(1)}, bf16[128,1536]{1,0:T(8,128)(2,1)S(1)}, u32[]{:S(2)}, u32[]{:S(2)}) collective-permute-start(bf16[128,1536]{1,0:T(8,128)(2,1)S(1)} %shard_map.80), channel_id=1, source_target_pairs={{0,8},{1,9},{2,10},{3,11},{4,12},{5,13},{6,14},{7,15},{16,24},{17,... | collective-permute-start | bytes 1179656 | tf_op jit(solution)/shard_map/ppermute | solution.py:56
  112.1 6.8 %collective-permute-start.10 = (bf16[128,1536]{1,0:T(8,128)(2,1)S(1)}, bf16[128,1536]{1,0:T(8,128)(2,1)S(1)}, u32[]{:S(2)}, u32[]{:S(2)}) collective-permute-start(bf16[128,1536]{1,0:T(8,128)(2,1)S(1)} %pad_maximum_fusion.2), channel_id=1, source_target_pairs={{0,2},{1,3},{2,0},{3,1},{4,6},{5,7},{6,4},{7,5},{16,18},{17,19},{1... | collective-permute-start | bytes 1179656 | tf_op jit(solution)/shard_map/ppermute | solution.py:56
  113.5 8.2 %collective-permute-start.12 = (bf16[128,1536]{1,0:T(8,128)(2,1)S(1)}, bf16[128,1536]{1,0:T(8,128)(2,1)S(1)}, u32[]{:S(2)}, u32[]{:S(2)}) collective-permute-start(bf16[128,1536]{1,0:T(8,128)(2,1)S(1)} %pad_maximum_fusion.3), channel_id=1, source_target_pairs={{0,6},{1,7},{2,4},{3,5},{4,2},{5,3},{6,0},{7,1},{16,22},{17,23},{1... | collective-permute-start | bytes 1179656 | tf_op jit(solution)/shard_map/ppermute | solution.py:56
  116.7 9.8 %collective-permute-start.15 = (bf16[128,1536]{1,0:T(8,128)(2,1)S(1)}, bf16[128,1536]{1,0:T(8,128)(2,1)S(1)}, u32[]{:S(2)}, u32[]{:S(2)}) collective-permute-start(bf16[128,1536]{1,0:T(8,128)(2,1)S(1)} %pad_maximum_fusion.4), channel_id=1, source_target_pairs={{0,6},{1,7},{2,4},{3,5},{4,2},{5,3},{6,0},{7,1},{16,22},{17,23},{1... | collective-permute-start | bytes 1179656 | tf_op jit(solution)/shard_map/ppermute | solution.py:56
  117.7 9.3 %collective-permute-start.16 = (bf16[128,1536]{1,0:T(8,128)(2,1)S(1)}, bf16[128,1536]{1,0:T(8,128)(2,1)S(1)}, u32[]{:S(2)}, u32[]{:S(2)}) collective-permute-start(bf16[128,1536]{1,0:T(8,128)(2,1)S(1)} %pad_maximum_fusion.5), channel_id=1, source_target_pairs={{0,2},{1,3},{2,0},{3,1},{4,6},{5,7},{6,4},{7,5},{16,18},{17,19},{1... | collective-permute-start | bytes 1179656 | tf_op jit(solution)/shard_map/ppermute | solution.py:56
  127.2 29.7 %collective-permute-start.17 = (bf16[336,1536]{1,0:T(8,128)(2,1)S(1)}, bf16[336,1536]{1,0:T(8,128)(2,1)}, u32[]{:S(2)}, u32[]{:S(2)}) collective-permute-start(bf16[336,1536]{1,0:T(8,128)(2,1)S(1)} %slice.32), channel_id=1, source_target_pairs={{0,8},{1,9},{2,10},{3,11},{4,12},{5,13},{6,14},{7,15},{16,24},{17,... | collective-permute-start | bytes 3096584 | tf_op jit(solution)/shard_map/ppermute | solution.py:56
  131.2 8.0 %collective-permute-start.20 = (bf16[256,1536]{1,0:T(8,128)(2,1)S(1)}, bf16[256,1536]{1,0:T(8,128)(2,1)S(1)}, u32[]{:S(2)}, u32[]{:S(2)}) collective-permute-start(bf16[256,1536]{1,0:T(8,128)(2,1)S(1)} %pad_maximum_fusion.refs_0_), channel_id=1, source_target_pairs={{0,1},{1,0},{2,3},{3,2},{4,5},{5,4},{6,7},{7,6},{16,17},{17,16},{1... | collective-permute-start | bytes 2359304 | tf_op jit(solution)/shard_map/ppermute | solution.py:56
  137.3 3.0 %collective-permute-start.21 = (bf16[256,1536]{1,0:T(8,128)(2,1)S(1)}, bf16[256,1536]{1,0:T(8,128)(2,1)S(1)}, u32[]{:S(2)}, u32[]{:S(2)}) collective-permute-start(bf16[256,1536]{1,0:T(8,128)(2,1)S(1)} %pad_maximum_fusion.1.refs_1_), channel_id=1, source_target_pairs={{0,1},{1,0},{2,3},{3,2},{4,5},{5,4},{6,7},{7,6},{16,17},{17,16},{1... | collective-permute-start | bytes 2359304 | tf_op jit(solution)/shard_map/ppermute | solution.py:56
  137.3 18.6 %collective-permute-start.18 = (bf16[256,1536]{1,0:T(8,128)(2,1)S(1)}, bf16[256,1536]{1,0:T(8,128)(2,1)S(1)}, u32[]{:S(2)}, u32[]{:S(2)}) collective-permute-start(bf16[256,1536]{1,0:T(8,128)(2,1)S(1)} %pad_maximum_fusion.refs_0_), channel_id=1, source_target_pairs={{0,2},{1,3},{2,0},{3,1},{4,6},{5,7},{6,4},{7,5},{16,18},{17,19},{1... | collective-permute-start | bytes 2359304 | tf_op jit(solution)/shard_map/ppermute | solution.py:56
  137.4 19.5 %collective-permute-start.19 = (bf16[256,1536]{1,0:T(8,128)(2,1)S(1)}, bf16[256,1536]{1,0:T(8,128)(2,1)S(1)}, u32[]{:S(2)}, u32[]{:S(2)}) collective-permute-start(bf16[256,1536]{1,0:T(8,128)(2,1)S(1)} %pad_maximum_fusion.1.refs_1_), channel_id=1, source_target_pairs={{0,6},{1,7},{2,4},{3,5},{4,2},{5,3},{6,0},{7,1},{16,22},{17,23},{1... | collective-permute-start | bytes 2359304 | tf_op jit(solution)/shard_map/ppermute | solution.py:56
  156.9 21.3 %collective-permute-start.25 = (bf16[512,1536]{1,0:T(8,128)(2,1)S(1)}, bf16[512,1536]{1,0:T(8,128)(2,1)}, u32[]{:S(2)}, u32[]{:S(2)}) collective-permute-start(bf16[512,1536]{1,0:T(8,128)(2,1)S(1)} %constant_dynamic-update-slice_fusion.refs_0_), channel_id=1, source_target_pairs={{0,1},{1,0},{2,3},{3,2},{4,5},{5,4},{6,7},{7,6},{16,17},{17,16},{1... | collective-permute-start | bytes 4718600 | tf_op jit(solution)/shard_map/ppermute | solution.py:56
  158.6 4.0 %collective-permute-start.22 = (bf16[256,1536]{1,0:T(8,128)(2,1)S(1)}, bf16[256,1536]{1,0:T(8,128)(2,1)S(1)}, u32[]{:S(2)}, u32[]{:S(2)}) collective-permute-start(bf16[256,1536]{1,0:T(8,128)(2,1)S(1)} %collective-permute-done.18.refs_2_), channel_id=1, source_target_pairs={{0,1},{1,0},{2,3},{3,2},{4,5},{5,4},{6,7},{7,6},{16,17},{17,16},{1... | collective-permute-start | bytes 2359304 | tf_op jit(solution)/shard_map/ppermute | solution.py:56
  158.6 6.3 %collective-permute-start.23 = (bf16[256,1536]{1,0:T(8,128)(2,1)S(1)}, bf16[256,1536]{1,0:T(8,128)(2,1)S(1)}, u32[]{:S(2)}, u32[]{:S(2)}) collective-permute-start(bf16[256,1536]{1,0:T(8,128)(2,1)S(1)} %collective-permute-done.19.refs_3_), channel_id=1, source_target_pairs={{0,1},{1,0},{2,3},{3,2},{4,5},{5,4},{6,7},{7,6},{16,17},{17,16},{1... | collective-permute-start | bytes 2359304 | tf_op jit(solution)/shard_map/ppermute | solution.py:56
  159.9 15.7 %collective-permute-start.24 = (bf16[176,1536]{1,0:T(8,128)(2,1)}, bf16[176,1536]{1,0:T(8,128)(2,1)}, u32[]{:S(2)}, u32[]{:S(2)}) collective-permute-start(bf16[176,1536]{1,0:T(8,128)(2,1)} %slice.33), channel_id=1, source_target_pairs={{0,8},{1,9},{2,10},{3,11},{4,12},{5,13},{6,14},{7,15},{16,24},{17,... | collective-permute-start | bytes 1622024 | tf_op jit(solution)/shard_map/ppermute | solution.py:56
  161.0 15.4 %collective-permute-start.26 = (bf16[336,1536]{1,0:T(8,128)(2,1)}, bf16[336,1536]{1,0:T(8,128)(2,1)}, u32[]{:S(2)}, u32[]{:S(2)}) collective-permute-start(bf16[336,1536]{1,0:T(8,128)(2,1)} %collective-permute-done.17.refs_1_), channel_id=1, source_target_pairs={{0,1},{1,0},{2,3},{3,2},{4,5},{5,4},{6,7},{7,6},{16,17},{17,16},{1... | collective-permute-start | bytes 3096584 | tf_op jit(solution)/shard_map/ppermute | solution.py:56
  171.6 16.7 %all-to-all-start.3 = ((bf16[8,128,384]{2,1,0:T(8,128)(2,1)}), bf16[8,128,384]{2,1,0:T(8,128)(2,1)S(1)}, u32[]{:S(2)}, u32[]{:S(2)}) async-start(bf16[8,128,384]{2,1,0:T(8,128)(2,1)} %copy-done.19), calls=%async_computation.3 | async-start | bytes 1572864 | tf_op jit(solution)/shard_map/all_to_all | solution.py:476
  175.6 2.6 %collective-permute-start.27 = (bf16[176,1536]{1,0:T(8,128)(2,1)}, bf16[176,1536]{1,0:T(8,128)(2,1)S(1)}, u32[]{:S(2)}, u32[]{:S(2)}) collective-permute-start(bf16[176,1536]{1,0:T(8,128)(2,1)} %collective-permute-done.24.refs_2_), channel_id=1, source_target_pairs={{0,1},{1,0},{2,3},{3,2},{4,5},{5,4},{6,7},{7,6},{16,17},{17,16},{1... | collective-permute-start | bytes 1622024 | tf_op jit(solution)/shard_map/ppermute | solution.py:56
  (30 other events, 129.3 us)

commit v4 on v3

--- a/solution.py
+++ b/solution.py
@@ -456,7 +456,7 @@
     pre_keep = [jnp.concatenate([t, swap(t, order[1])]) for t, order in zip(two, TOKEN_ORDERS)]
 
     gelu_keep, pre_keep = together(gelu_keep, pre_keep)
-    cut = 21 * quarter // 16
+    cut = 11 * quarter // 8
     gelu_far = [swap(gelu_keep[:cut], "y")]
     pre_first = [swap(k, order[0]) for k, order in zip(pre_keep, TOKEN_ORDERS)]
     pre_keep_other = [swap(k, "core") for k in pre_keep]

time: 190 us -> 191 us (level)
  transfers between devices with their start and end apart: 32 -> 32, of which waited for: 20 -> 21; matrix products, arithmetic and copies ran while one was open for 3% -> 3% of each run, Pallas kernels for 18% -> 18%
where the time goes in v4:
time: 191 us; the launch traced here: 190 us
  waiting for transfers between devices  72 us (38%)
  starting transfers between devices  56.2 us (29%)
  Pallas kernels  37.2 us (19%)
  local copies, waits for them, and re-layouts  21 us (11%)
  other arithmetic  2.31 us (1%)
    ppermute x28, waiting for transfers between devices, swap(): return lax.ppermute(values, AXES, FLIPS[name])  44.4 us
    ppermute x28, starting transfers between devices, swap(): return lax.ppermute(values, AXES, FLIPS[name])  39.6 us
    pallas_call x18, Pallas kernels, kernel_call(): pl.pallas_call(kernel, in_specs=[pl.BlockSpec(memory_space=pltpu.SMEM)] +...  37.2 us
    all_to_all x1, waiting for transfers between devices, body(): raw = lax.all_to_all(copies, 'row', 0, 0, tiled=True)  18.8 us
    unnamed x64, local copies, waits for them, and re-layouts  15.5 us
    all_to_all x2, starting transfers between devices, body(): lax.all_to_all(sums, 'col', 0, 0, axis_index_groups=Z_GROUPS, tiled=True)  7.8 us
    all_to_all x1, starting transfers between devices, body(): raw = lax.all_to_all(copies, 'row', 0, 0, tiled=True)  5.12 us
    all_to_all x1, waiting for transfers between devices, body(): parts = lax.all_to_all(sums, 'row', 0, 0, tiled=True)  4.76 us
  transfers between devices with their start and end apart: 32, of which 21 were waited for; matrix products, arithmetic and copies ran while one was open for 3% of the time, Pallas kernels for 18%

profile of v4, /device:TPU:1, one launch (start us, length us, event | category | flops | bytes accessed | tf_op | source)
XLA Modules:
  0.0 189.9 jit_solution(13507619155781178224)
XLA Ops:
  0.7 2.4 %constant_dynamic-slice_fusion = bf16[384,1536]{1,0:T(8,128)(2,1)} fusion(bf16[384,3072]{1,0:T(8,128)(2,1)} %refs_8_.1, s32[]{:T(128)S(6)} %select_n.26), kind=kLoop, calls=%fused_computation.13 | loop fusion | bytes 2359300 | tf_op jit(solution)/shard_map/dynamic_slice | solution.py:396
  6.4 5.1 %all-to-all-start = ((bf16[8,2,128,384]{3,2,1,0:T(8,128)(2,1)}), bf16[8,2,128,384]{3,2,1,0:T(8,128)(2,1)S(1)}, u32[]{:S(2)}, u32[]{:S(2)}) async-start(bf16[8,2,128,384]{3,2,1,0:T(8,128)(2,1)} %copy-done.15), calls=%async_computation | async-start | bytes 3145728 | tf_op jit(solution)/shard_map/all_to_all | solution.py:393
  16.9 18.8 %all-to-all-done.l_ref.raw_ref = bf16[8,2,128,384]{3,2,1,0:T(8,128)(2,1)S(1)} async-done(((bf16[8,2,128,384]{3,2,1,0:T(8,128)(2,1)}), bf16[8,2,128,384]{3,2,1,0:T(8,128)(2,1)S(1)}, u32[]{:S(2)}, u32[]{:S(2)}) %all-to-all-start) | async-done | bytes 1572896 | tf_op jit(solution)/shard_map/all_to_all | solution.py:393
  36.8 3.0 %collective-permute-done.2.lo_ref = bf16[8,2,128,384]{3,2,1,0:T(8,128)(2,1)S(1)} collective-permute-done((bf16[8,2,128,384]{3,2,1,0:T(8,128)(2,1)S(1)}, bf16[8,2,128,384]{3,2,1,0:T(8,128)(2,1)S(1)}, u32[]{:S(2)}, u32[]{:S(2)}) %collective-permute-start.2) | collective-permute-done | bytes 1572896 | tf_op jit(solution)/shard_map/ppermute | solution.py:56
  47.1 2.3 %collective-permute-start.4 = (bf16[256,1536]{1,0:T(8,128)(2,1)S(1)}, bf16[256,1536]{1,0:T(8,128)(2,1)S(1)}, u32[]{:S(2)}, u32[]{:S(2)}) collective-permute-start(bf16[256,1536]{1,0:T(8,128)(2,1)S(1)} %shard_map.72), channel_id=1, source_target_pairs={{0,6},{1,7},{2,4},{3,5},{4,2},{5,3},{6,0},{7,1},{16,22},{17,23},{1... | collective-permute-start | bytes 2359304 | tf_op jit(solution)/shard_map/ppermute | solution.py:56
  51.0 2.7 %collective-permute-start.7 = (bf16[192,1536]{1,0:T(8,128)(2,1)S(1)}, bf16[192,1536]{1,0:T(8,128)(2,1)S(1)}, u32[]{:S(2)}, u32[]{:S(2)}) collective-permute-start(bf16[192,1536]{1,0:T(8,128)(2,1)S(1)} %shard_map.74), channel_id=1, source_target_pairs={{0,8},{1,9},{2,10},{3,11},{4,12},{5,13},{6,14},{7,15},{16,24},{17,... | collective-permute-start | bytes 1769480 | tf_op jit(solution)/shard_map/ppermute | solution.py:56
  53.7 2.5 %shard_map.78 = bf16[320,1536]{1,0:T(8,128)(2,1)} custom-call(s32[4]{0:T(128)S(1)} %pad_add_fusion.place_ref, bf16[8,2,128,384]{3,2,1,0:T(8,128)(2,1)S(1)} %all-to-all-done.l_ref.raw_ref, bf16[8,2,128,384]{3,2,1,0:T(8,128)(2,1)S(1)} %collective-permute-done.2.lo_ref, bf16[3072,384]{1,0:T(8,128)(2,1)S(1)} %copy-done.3, bf16[1536,384]{1,0:T(8,128)(2,1)S(1)} %copy-done.6), custom_call_target="tpu_custom_call" | custom-call | tf_op jit(solution)/shard_map/pallas_call | solution.py:78
  58.2 5.1 %collective-permute-done.3.refs_0_ = bf16[256,1536]{1,0:T(8,128)(2,1)S(1)} collective-permute-done((bf16[256,1536]{1,0:T(8,128)(2,1)S(1)}, bf16[256,1536]{1,0:T(8,128)(2,1)S(1)}, u32[]{:S(2)}, u32[]{:S(2)}) %collective-permute-start.3) | collective-permute-done | bytes 786464 | tf_op jit(solution)/shard_map/ppermute | solution.py:56
  63.3 2.1 %shard_map.71 = (bf16[128,1536]{1,0:T(8,128)(2,1)S(1)}, bf16[128,1536]{1,0:T(8,128)(2,1)}) custom-call(s32[4]{0:T(128)S(1)} %pad_add_fusion.place_ref, bf16[8,2,128,384]{3,2,1,0:T(8,128)(2,1)S(1)} %all-to-all-done.l_ref.raw_ref, bf16[8,2,128,384]{3,2,1,0:T(8,128)(2,1)S(1)} %collective-permute-done.2.lo_ref, bf16[384,3072]{1,0:T(8,128)(2,1)S(1)} %copy-done.1, ...), custom_call_target="tpu_custom_call" | custom-call | tf_op jit(solution)/shard_map/pallas_call | solution.py:78
  65.4 3.5 %collective-permute-start.5 = (bf16[128,1536]{1,0:T(8,128)(2,1)}, bf16[128,1536]{1,0:T(8,128)(2,1)}, u32[]{:S(2)}, u32[]{:S(2)}) collective-permute-start(bf16[128,1536]{1,0:T(8,128)(2,1)} %get-tuple-element.31.refs_1_), channel_id=1, source_target_pairs={{0,6},{1,7},{2,4},{3,5},{4,2},{5,3},{6,0},{7,1},{16,22},{17,23},{1... | collective-permute-start | bytes 1179656 | tf_op jit(solution)/shard_map/ppermute | solution.py:56
  68.9 1.8 shard_map.73
  73.2 4.2 %all-to-all-start.2 = ((bf16[4,48,1536]{2,1,0:T(8,128)(2,1)}), bf16[4,48,1536]{2,1,0:T(8,128)(2,1)}, u32[]{:S(2)}, u32[]{:S(2)}) async-start(bf16[4,48,1536]{2,1,0:T(8,128)(2,1)} %bitcast.11), calls=%async_computation.2 | async-start | bytes 1179648 | tf_op jit(solution)/shard_map/all_to_all | solution.py:441
  77.4 2.6 %collective-permute-done.6.refs_3_ = bf16[128,1536]{1,0:T(8,128)(2,1)} collective-permute-done((bf16[128,1536]{1,0:T(8,128)(2,1)S(1)}, bf16[128,1536]{1,0:T(8,128)(2,1)}, u32[]{:S(2)}, u32[]{:S(2)}) %collective-permute-start.6) | collective-permute-done | bytes 393248 | tf_op jit(solution)/shard_map/ppermute | solution.py:56
  83.1 2.2 %shard_map.76 = (f32[128,1536]{1,0:T(8,128)S(1)}, bf16[128,1536]{1,0:T(8,128)(2,1)}) custom-call(s32[4]{0:T(128)S(1)} %pad_add_fusion.place_ref, bf16[128,1536]{1,0:T(8,128)(2,1)S(1)} %copy-done.23, bf16[128,1536]{1,0:T(8,128)(2,1)S(1)} %copy-done.25, bf16[128,1536]{1,0:T(8,128)(2,1)} %collective-permute-done.5.refs_2_, ...), custom_call_target="tpu_custom_call" | custom-call | tf_op jit(solution)/shard_map/pallas_call | solution.py:78
  86.2 2.6 %collective-permute-start.8 = (bf16[128,1536]{1,0:T(8,128)(2,1)}, bf16[128,1536]{1,0:T(8,128)(2,1)}, u32[]{:S(2)}, u32[]{:S(2)}) collective-permute-start(bf16[128,1536]{1,0:T(8,128)(2,1)} %get-tuple-element.36), channel_id=1, source_target_pairs={{0,8},{1,9},{2,10},{3,11},{4,12},{5,13},{6,14},{7,15},{16,24},{17,... | collective-permute-start | bytes 1179656 | tf_op jit(solution)/shard_map/ppermute | solution.py:56
  90.5 2.2 %shard_map.79 = bf16[320,1536]{1,0:T(8,128)(2,1)S(1)} custom-call(s32[4]{0:T(128)S(1)} %pad_add_fusion.place_ref, bf16[8,2,128,384]{3,2,1,0:T(8,128)(2,1)S(1)} %all-to-all-done.l_ref.raw_ref, bf16[8,2,128,384]{3,2,1,0:T(8,128)(2,1)S(1)} %collective-permute-done.2.lo_ref, bf16[3072,384]{1,0:T(8,128)(2,1)S(1)} %copy-done.4, bf16[1536,384]{1,0:T(8,128)(2,1)S(1)} %copy-done.7, ...), custom_call_target="tpu_custom_call" | custom-call | tf_op jit(solution)/shard_map/pallas_call | solution.py:78
  93.7 3.6 %all-to-all-start.1 = ((bf16[4,80,1536]{2,1,0:T(8,128)(2,1)}), bf16[4,80,1536]{2,1,0:T(8,128)(2,1)S(1)}, u32[]{:S(2)}, u32[]{:S(2)}) async-start(bf16[4,80,1536]{2,1,0:T(8,128)(2,1)} %bitcast.13), calls=%async_computation.1 | async-start | bytes 1966080 | tf_op jit(solution)/shard_map/all_to_all | solution.py:441
  101.2 1.8 collective-permute-start.9
  103.0 4.1 %all-to-all-done.1 = bf16[4,80,1536]{2,1,0:T(8,128)(2,1)S(1)} async-done(((bf16[4,80,1536]{2,1,0:T(8,128)(2,1)}), bf16[4,80,1536]{2,1,0:T(8,128)(2,1)S(1)}, u32[]{:S(2)}, u32[]{:S(2)}) %all-to-all-start.1) | async-done | bytes 983072 | tf_op jit(solution)/shard_map/all_to_all | solution.py:441
  108.5 2.5 %collective-permute-start.14 = (bf16[128,1536]{1,0:T(8,128)(2,1)S(1)}, bf16[128,1536]{1,0:T(8,128)(2,1)S(1)}, u32[]{:S(2)}, u32[]{:S(2)}) collective-permute-start(bf16[128,1536]{1,0:T(8,128)(2,1)S(1)} %shard_map.80), channel_id=1, source_target_pairs={{0,8},{1,9},{2,10},{3,11},{4,12},{5,13},{6,14},{7,15},{16,24},{17,... | collective-permute-start | bytes 1179656 | tf_op jit(solution)/shard_map/ppermute | solution.py:56
  119.0 2.8 %collective-permute-done.12 = bf16[128,1536]{1,0:T(8,128)(2,1)S(1)} collective-permute-done((bf16[128,1536]{1,0:T(8,128)(2,1)S(1)}, bf16[128,1536]{1,0:T(8,128)(2,1)S(1)}, u32[]{:S(2)}, u32[]{:S(2)}) %collective-permute-start.12) | collective-permute-done | bytes 393248 | tf_op jit(solution)/shard_map/ppermute | solution.py:56
  121.8 4.8 %collective-permute-done.15 = bf16[128,1536]{1,0:T(8,128)(2,1)S(1)} collective-permute-done((bf16[128,1536]{1,0:T(8,128)(2,1)S(1)}, bf16[128,1536]{1,0:T(8,128)(2,1)S(1)}, u32[]{:S(2)}, u32[]{:S(2)}) %collective-permute-start.15) | collective-permute-done | bytes 393248 | tf_op jit(solution)/shard_map/ppermute | solution.py:56
  127.3 3.7 %collective-permute-start.17 = (bf16[352,1536]{1,0:T(8,128)(2,1)S(1)}, bf16[352,1536]{1,0:T(8,128)(2,1)}, u32[]{:S(2)}, u32[]{:S(2)}) collective-permute-start(bf16[352,1536]{1,0:T(8,128)(2,1)S(1)} %slice.32), channel_id=1, source_target_pairs={{0,8},{1,9},{2,10},{3,11},{4,12},{5,13},{6,14},{7,15},{16,24},{17,... | collective-permute-start | bytes 3244040 | tf_op jit(solution)/shard_map/ppermute | solution.py:56
  131.1 6.2 %collective-permute-start.20 = (bf16[256,1536]{1,0:T(8,128)(2,1)S(1)}, bf16[256,1536]{1,0:T(8,128)(2,1)S(1)}, u32[]{:S(2)}, u32[]{:S(2)}) collective-permute-start(bf16[256,1536]{1,0:T(8,128)(2,1)S(1)} %pad_maximum_fusion.refs_0_), channel_id=1, source_target_pairs={{0,1},{1,0},{2,3},{3,2},{4,5},{5,4},{6,7},{7,6},{16,17},{17,16},{1... | collective-permute-start | bytes 2359304 | tf_op jit(solution)/shard_map/ppermute | solution.py:56
  140.3 2.3 %shard_map.81.refs_9_ = bf16[8,64,384]{2,1,0:T(8,128)(2,1)S(1)} custom-call(s32[4]{0:T(128)S(1)} %pad_add_fusion.place_ref, bf16[256,1536]{1,0:T(8,128)(2,1)S(1)} %pad_maximum_fusion.refs_0_, bf16[256,1536]{1,0:T(8,128)(2,1)S(1)} %pad_maximum_fusion.1.refs_1_, bf16[256,1536]{1,0:T(8,128)(2,1)S(1)} %collective-permute-done.20.refs_2_.refs_4_, ...), custom_call_target="tpu_custom_call" | custom-call | tf_op jit(solution)/shard_map/pallas_call | solution.py:78
  142.7 13.2 %collective-permute-done.18.refs_2_ = bf16[256,1536]{1,0:T(8,128)(2,1)S(1)} collective-permute-done((bf16[256,1536]{1,0:T(8,128)(2,1)S(1)}, bf16[256,1536]{1,0:T(8,128)(2,1)S(1)}, u32[]{:S(2)}, u32[]{:S(2)}) %collective-permute-start.18) | collective-permute-done | bytes 786464 | tf_op jit(solution)/shard_map/ppermute | solution.py:56
  161.1 2.6 %collective-permute-done.22.refs_6_ = bf16[256,1536]{1,0:T(8,128)(2,1)S(1)} collective-permute-done((bf16[256,1536]{1,0:T(8,128)(2,1)S(1)}, bf16[256,1536]{1,0:T(8,128)(2,1)S(1)}, u32[]{:S(2)}, u32[]{:S(2)}) %collective-permute-start.22) | collective-permute-done | bytes 786464 | tf_op jit(solution)/shard_map/ppermute | solution.py:56
  165.2 5.8 %shard_map.82 = (bf16[8,128,384]{2,1,0:T(8,128)(2,1)S(1)}, f32[384,3072]{1,0:T(8,128)}) custom-call(s32[4]{0:T(128)S(1)} %pad_add_fusion.place_ref, bf16[256,1536]{1,0:T(8,128)(2,1)S(1)} %pad_maximum_fusion.refs_0_, bf16[256,1536]{1,0:T(8,128)(2,1)S(1)} %pad_maximum_fusion.1.refs_1_, bf16[256,1536]{1,0:T(8,128)(2,1)S(1)} %collective-permute-done.18.refs_2_, ...), custom_call_target="tpu_custom_call" | custom-call | tf_op jit(solution)/shard_map/pallas_call | solution.py:78
  171.9 3.7 %all-to-all-start.3 = ((bf16[8,128,384]{2,1,0:T(8,128)(2,1)}), bf16[8,128,384]{2,1,0:T(8,128)(2,1)S(1)}, u32[]{:S(2)}, u32[]{:S(2)}) async-start(bf16[8,128,384]{2,1,0:T(8,128)(2,1)} %copy-done.19), calls=%async_computation.3 | async-start | bytes 1572864 | tf_op jit(solution)/shard_map/all_to_all | solution.py:476
  175.8 1.9 %collective-permute-done.27.refs_5_ = bf16[160,1536]{1,0:T(8,128)(2,1)S(1)} collective-permute-done((bf16[160,1536]{1,0:T(8,128)(2,1)}, bf16[160,1536]{1,0:T(8,128)(2,1)S(1)}, u32[]{:S(2)}, u32[]{:S(2)}) %collective-permute-start.27) | collective-permute-done | bytes 491552 | tf_op jit(solution)/shard_map/ppermute | solution.py:56
  177.8 6.1 %shard_map.83 = f32[3072,384]{1,0:T(8,128)} custom-call(s32[4]{0:T(128)S(1)} %pad_add_fusion.place_ref, bf16[512,1536]{1,0:T(8,128)(2,1)S(1)} %constant_dynamic-update-slice_fusion.refs_0_, bf16[352,1536]{1,0:T(8,128)(2,1)} %collective-permute-done.17.refs_1_, bf16[160,1536]{1,0:T(8,128)(2,1)} %collective-permute-done.24.refs_2_, ...), custom_call_target="tpu_custom_call" | custom-call | tf_op jit(solution)/shard_map/pallas_call | solution.py:78
  183.8 4.8 %all-to-all-done.3.parts_ref = bf16[8,128,384]{2,1,0:T(8,128)(2,1)S(1)} async-done(((bf16[8,128,384]{2,1,0:T(8,128)(2,1)}), bf16[8,128,384]{2,1,0:T(8,128)(2,1)S(1)}, u32[]{:S(2)}, u32[]{:S(2)}) %all-to-all-start.3) | async-done | bytes 786464 | tf_op jit(solution)/shard_map/all_to_all | solution.py:476
  (129 shorter events, 55.6 us)
Async XLA Ops:
  3.1 10.2 %collective-permute-start.1 = (bf16[384,1536]{1,0:T(8,128)(2,1)}, bf16[384,1536]{1,0:T(8,128)(2,1)S(1)}, u32[]{:S(2)}, u32[]{:S(2)}) collective-permute-start(bf16[384,1536]{1,0:T(8,128)(2,1)} %constant_dynamic-slice_fusion), channel_id=1, source_target_pairs={{0,1},{1,0},{2,3},{3,2},{4,5},{5,4},{6,7},{7,6},{16,17},{17,16},{1... | collective-permute-start | bytes 3538952 | tf_op jit(solution)/shard_map/ppermute | solution.py:56
  6.4 29.2 %all-to-all-start = ((bf16[8,2,128,384]{3,2,1,0:T(8,128)(2,1)}), bf16[8,2,128,384]{3,2,1,0:T(8,128)(2,1)S(1)}, u32[]{:S(2)}, u32[]{:S(2)}) async-start(bf16[8,2,128,384]{3,2,1,0:T(8,128)(2,1)} %copy-done.15), calls=%async_computation | async-start | bytes 3145728 | tf_op jit(solution)/shard_map/all_to_all | solution.py:393
  12.9 2.9 %collective-permute-start = (bf16[1536,384]{1,0:T(8,128)(2,1)S(1)}, bf16[1536,384]{1,0:T(8,128)(2,1)S(1)}, u32[]{:S(2)}, u32[]{:S(2)}) collective-permute-start(bf16[1536,384]{1,0:T(8,128)(2,1)S(1)} %constant_dynamic-slice_fusion.1), channel_id=1, source_target_pairs={{0,1},{1,0},{2,3},{3,2},{4,5},{5,4},{6,7},{7,6},{16,17},{17,16},{1... | collective-permute-start | bytes 3538952 | tf_op jit(solution)/shard_map/ppermute | solution.py:56
  35.7 4.1 %collective-permute-start.2 = (bf16[8,2,128,384]{3,2,1,0:T(8,128)(2,1)S(1)}, bf16[8,2,128,384]{3,2,1,0:T(8,128)(2,1)S(1)}, u32[]{:S(2)}, u32[]{:S(2)}) collective-permute-start(bf16[8,2,128,384]{3,2,1,0:T(8,128)(2,1)S(1)} %all-to-all-done.l_ref.raw_ref), channel_id=1, source_target_pairs={{0,1},{1,0},{2,3},{3,2},{4,5},{5,4},{6,7},{7,6},{16,17},{17,16},{1... | collective-permute-start | bytes 4718600 | tf_op jit(solution)/shard_map/ppermute | solution.py:56
  44.1 19.2 %collective-permute-start.3 = (bf16[256,1536]{1,0:T(8,128)(2,1)S(1)}, bf16[256,1536]{1,0:T(8,128)(2,1)S(1)}, u32[]{:S(2)}, u32[]{:S(2)}) collective-permute-start(bf16[256,1536]{1,0:T(8,128)(2,1)S(1)} %shard_map.68), channel_id=1, source_target_pairs={{0,2},{1,3},{2,0},{3,1},{4,6},{5,7},{6,4},{7,5},{16,18},{17,19},{1... | collective-permute-start | bytes 2359304 | tf_op jit(solution)/shard_map/ppermute | solution.py:56
  47.1 21.7 %collective-permute-start.4 = (bf16[256,1536]{1,0:T(8,128)(2,1)S(1)}, bf16[256,1536]{1,0:T(8,128)(2,1)S(1)}, u32[]{:S(2)}, u32[]{:S(2)}) collective-permute-start(bf16[256,1536]{1,0:T(8,128)(2,1)S(1)} %shard_map.72), channel_id=1, source_target_pairs={{0,6},{1,7},{2,4},{3,5},{4,2},{5,3},{6,0},{7,1},{16,22},{17,23},{1... | collective-permute-start | bytes 2359304 | tf_op jit(solution)/shard_map/ppermute | solution.py:56
  51.0 19.9 %collective-permute-start.7 = (bf16[192,1536]{1,0:T(8,128)(2,1)S(1)}, bf16[192,1536]{1,0:T(8,128)(2,1)S(1)}, u32[]{:S(2)}, u32[]{:S(2)}) collective-permute-start(bf16[192,1536]{1,0:T(8,128)(2,1)S(1)} %shard_map.74), channel_id=1, source_target_pairs={{0,8},{1,9},{2,10},{3,11},{4,12},{5,13},{6,14},{7,15},{16,24},{17,... | collective-permute-start | bytes 1769480 | tf_op jit(solution)/shard_map/ppermute | solution.py:56
  56.1 32.7 %collective-permute-start.13 = (bf16[320,1536]{1,0:T(8,128)(2,1)}, bf16[320,1536]{1,0:T(8,128)(2,1)}, u32[]{:S(2)}, u32[]{:S(2)}) collective-permute-start(bf16[320,1536]{1,0:T(8,128)(2,1)} %shard_map.78), channel_id=1, source_target_pairs={{0,8},{1,9},{2,10},{3,11},{4,12},{5,13},{6,14},{7,15},{16,24},{17,... | collective-permute-start | bytes 2949128 | tf_op jit(solution)/shard_map/ppermute | solution.py:56
  65.4 12.0 %collective-permute-start.5 = (bf16[128,1536]{1,0:T(8,128)(2,1)}, bf16[128,1536]{1,0:T(8,128)(2,1)}, u32[]{:S(2)}, u32[]{:S(2)}) collective-permute-start(bf16[128,1536]{1,0:T(8,128)(2,1)} %get-tuple-element.31.refs_1_), channel_id=1, source_target_pairs={{0,6},{1,7},{2,4},{3,5},{4,2},{5,3},{6,0},{7,1},{16,22},{17,23},{1... | collective-permute-start | bytes 1179656 | tf_op jit(solution)/shard_map/ppermute | solution.py:56
  70.7 9.3 %collective-permute-start.6 = (bf16[128,1536]{1,0:T(8,128)(2,1)S(1)}, bf16[128,1536]{1,0:T(8,128)(2,1)}, u32[]{:S(2)}, u32[]{:S(2)}) collective-permute-start(bf16[128,1536]{1,0:T(8,128)(2,1)S(1)} %get-tuple-element.33.refs_1_), channel_id=1, source_target_pairs={{0,2},{1,3},{2,0},{3,1},{4,6},{5,7},{6,4},{7,5},{16,18},{17,19},{1... | collective-permute-start | bytes 1179656 | tf_op jit(solution)/shard_map/ppermute | solution.py:56
  73.2 20.6 %all-to-all-start.2 = ((bf16[4,48,1536]{2,1,0:T(8,128)(2,1)}), bf16[4,48,1536]{2,1,0:T(8,128)(2,1)}, u32[]{:S(2)}, u32[]{:S(2)}) async-start(bf16[4,48,1536]{2,1,0:T(8,128)(2,1)} %bitcast.11), calls=%async_computation.2 | async-start | bytes 1179648 | tf_op jit(solution)/shard_map/all_to_all | solution.py:441
  86.2 11.1 %collective-permute-start.8 = (bf16[128,1536]{1,0:T(8,128)(2,1)}, bf16[128,1536]{1,0:T(8,128)(2,1)}, u32[]{:S(2)}, u32[]{:S(2)}) collective-permute-start(bf16[128,1536]{1,0:T(8,128)(2,1)} %get-tuple-element.36), channel_id=1, source_target_pairs={{0,8},{1,9},{2,10},{3,11},{4,12},{5,13},{6,14},{7,15},{16,24},{17,... | collective-permute-start | bytes 1179656 | tf_op jit(solution)/shard_map/ppermute | solution.py:56
  93.7 13.4 %all-to-all-start.1 = ((bf16[4,80,1536]{2,1,0:T(8,128)(2,1)}), bf16[4,80,1536]{2,1,0:T(8,128)(2,1)S(1)}, u32[]{:S(2)}, u32[]{:S(2)}) async-start(bf16[4,80,1536]{2,1,0:T(8,128)(2,1)} %bitcast.13), calls=%async_computation.1 | async-start | bytes 1966080 | tf_op jit(solution)/shard_map/all_to_all | solution.py:441
  99.8 12.8 %collective-permute-start.11 = (bf16[64,1536]{1,0:T(8,128)(2,1)}, bf16[64,1536]{1,0:T(8,128)(2,1)S(1)}, u32[]{:S(2)}, u32[]{:S(2)}) collective-permute-start(bf16[64,1536]{1,0:T(8,128)(2,1)} %get-tuple-element.57), channel_id=1, source_target_pairs={{0,2},{1,3},{2,0},{3,1},{4,6},{5,7},{6,4},{7,5},{16,18},{17,19},{1... | collective-permute-start | bytes 589832 | tf_op jit(solution)/shard_map/ppermute | solution.py:56
  101.2 10.0 %collective-permute-start.9 = (bf16[64,1536]{1,0:T(8,128)(2,1)}, bf16[64,1536]{1,0:T(8,128)(2,1)}, u32[]{:S(2)}, u32[]{:S(2)}) collective-permute-start(bf16[64,1536]{1,0:T(8,128)(2,1)} %get-tuple-element.59), channel_id=1, source_target_pairs={{0,6},{1,7},{2,4},{3,5},{4,2},{5,3},{6,0},{7,1},{16,22},{17,23},{1... | collective-permute-start | bytes 589832 | tf_op jit(solution)/shard_map/ppermute | solution.py:56
  108.5 8.2 %collective-permute-start.14 = (bf16[128,1536]{1,0:T(8,128)(2,1)S(1)}, bf16[128,1536]{1,0:T(8,128)(2,1)S(1)}, u32[]{:S(2)}, u32[]{:S(2)}) collective-permute-start(bf16[128,1536]{1,0:T(8,128)(2,1)S(1)} %shard_map.80), channel_id=1, source_target_pairs={{0,8},{1,9},{2,10},{3,11},{4,12},{5,13},{6,14},{7,15},{16,24},{17,... | collective-permute-start | bytes 1179656 | tf_op jit(solution)/shard_map/ppermute | solution.py:56
  112.2 6.8 %collective-permute-start.10 = (bf16[128,1536]{1,0:T(8,128)(2,1)S(1)}, bf16[128,1536]{1,0:T(8,128)(2,1)S(1)}, u32[]{:S(2)}, u32[]{:S(2)}) collective-permute-start(bf16[128,1536]{1,0:T(8,128)(2,1)S(1)} %pad_maximum_fusion.2), channel_id=1, source_target_pairs={{0,2},{1,3},{2,0},{3,1},{4,6},{5,7},{6,4},{7,5},{16,18},{17,19},{1... | collective-permute-start | bytes 1179656 | tf_op jit(solution)/shard_map/ppermute | solution.py:56
  113.6 8.2 %collective-permute-start.12 = (bf16[128,1536]{1,0:T(8,128)(2,1)S(1)}, bf16[128,1536]{1,0:T(8,128)(2,1)S(1)}, u32[]{:S(2)}, u32[]{:S(2)}) collective-permute-start(bf16[128,1536]{1,0:T(8,128)(2,1)S(1)} %pad_maximum_fusion.3), channel_id=1, source_target_pairs={{0,6},{1,7},{2,4},{3,5},{4,2},{5,3},{6,0},{7,1},{16,22},{17,23},{1... | collective-permute-start | bytes 1179656 | tf_op jit(solution)/shard_map/ppermute | solution.py:56
  116.8 9.8 %collective-permute-start.15 = (bf16[128,1536]{1,0:T(8,128)(2,1)S(1)}, bf16[128,1536]{1,0:T(8,128)(2,1)S(1)}, u32[]{:S(2)}, u32[]{:S(2)}) collective-permute-start(bf16[128,1536]{1,0:T(8,128)(2,1)S(1)} %pad_maximum_fusion.4), channel_id=1, source_target_pairs={{0,6},{1,7},{2,4},{3,5},{4,2},{5,3},{6,0},{7,1},{16,22},{17,23},{1... | collective-permute-start | bytes 1179656 | tf_op jit(solution)/shard_map/ppermute | solution.py:56
  117.8 9.4 %collective-permute-start.16 = (bf16[128,1536]{1,0:T(8,128)(2,1)S(1)}, bf16[128,1536]{1,0:T(8,128)(2,1)S(1)}, u32[]{:S(2)}, u32[]{:S(2)}) collective-permute-start(bf16[128,1536]{1,0:T(8,128)(2,1)S(1)} %pad_maximum_fusion.5), channel_id=1, source_target_pairs={{0,2},{1,3},{2,0},{3,1},{4,6},{5,7},{6,4},{7,5},{16,18},{17,19},{1... | collective-permute-start | bytes 1179656 | tf_op jit(solution)/shard_map/ppermute | solution.py:56
  127.3 29.5 %collective-permute-start.17 = (bf16[352,1536]{1,0:T(8,128)(2,1)S(1)}, bf16[352,1536]{1,0:T(8,128)(2,1)}, u32[]{:S(2)}, u32[]{:S(2)}) collective-permute-start(bf16[352,1536]{1,0:T(8,128)(2,1)S(1)} %slice.32), channel_id=1, source_target_pairs={{0,8},{1,9},{2,10},{3,11},{4,12},{5,13},{6,14},{7,15},{16,24},{17,... | collective-permute-start | bytes 3244040 | tf_op jit(solution)/shard_map/ppermute | solution.py:56
  131.1 8.1 %collective-permute-start.20 = (bf16[256,1536]{1,0:T(8,128)(2,1)S(1)}, bf16[256,1536]{1,0:T(8,128)(2,1)S(1)}, u32[]{:S(2)}, u32[]{:S(2)}) collective-permute-start(bf16[256,1536]{1,0:T(8,128)(2,1)S(1)} %pad_maximum_fusion.refs_0_), channel_id=1, source_target_pairs={{0,1},{1,0},{2,3},{3,2},{4,5},{5,4},{6,7},{7,6},{16,17},{17,16},{1... | collective-permute-start | bytes 2359304 | tf_op jit(solution)/shard_map/ppermute | solution.py:56
  137.3 3.0 %collective-permute-start.21 = (bf16[256,1536]{1,0:T(8,128)(2,1)S(1)}, bf16[256,1536]{1,0:T(8,128)(2,1)S(1)}, u32[]{:S(2)}, u32[]{:S(2)}) collective-permute-start(bf16[256,1536]{1,0:T(8,128)(2,1)S(1)} %pad_maximum_fusion.1.refs_1_), channel_id=1, source_target_pairs={{0,1},{1,0},{2,3},{3,2},{4,5},{5,4},{6,7},{7,6},{16,17},{17,16},{1... | collective-permute-start | bytes 2359304 | tf_op jit(solution)/shard_map/ppermute | solution.py:56
  137.3 18.6 %collective-permute-start.18 = (bf16[256,1536]{1,0:T(8,128)(2,1)S(1)}, bf16[256,1536]{1,0:T(8,128)(2,1)S(1)}, u32[]{:S(2)}, u32[]{:S(2)}) collective-permute-start(bf16[256,1536]{1,0:T(8,128)(2,1)S(1)} %pad_maximum_fusion.refs_0_), channel_id=1, source_target_pairs={{0,2},{1,3},{2,0},{3,1},{4,6},{5,7},{6,4},{7,5},{16,18},{17,19},{1... | collective-permute-start | bytes 2359304 | tf_op jit(solution)/shard_map/ppermute | solution.py:56
  137.4 19.5 %collective-permute-start.19 = (bf16[256,1536]{1,0:T(8,128)(2,1)S(1)}, bf16[256,1536]{1,0:T(8,128)(2,1)S(1)}, u32[]{:S(2)}, u32[]{:S(2)}) collective-permute-start(bf16[256,1536]{1,0:T(8,128)(2,1)S(1)} %pad_maximum_fusion.1.refs_1_), channel_id=1, source_target_pairs={{0,6},{1,7},{2,4},{3,5},{4,2},{5,3},{6,0},{7,1},{16,22},{17,23},{1... | collective-permute-start | bytes 2359304 | tf_op jit(solution)/shard_map/ppermute | solution.py:56
  156.9 20.9 %collective-permute-start.25 = (bf16[512,1536]{1,0:T(8,128)(2,1)S(1)}, bf16[512,1536]{1,0:T(8,128)(2,1)}, u32[]{:S(2)}, u32[]{:S(2)}) collective-permute-start(bf16[512,1536]{1,0:T(8,128)(2,1)S(1)} %constant_dynamic-update-slice_fusion.refs_0_), channel_id=1, source_target_pairs={{0,1},{1,0},{2,3},{3,2},{4,5},{5,4},{6,7},{7,6},{16,17},{17,16},{1... | collective-permute-start | bytes 4718600 | tf_op jit(solution)/shard_map/ppermute | solution.py:56
  158.5 5.2 %collective-permute-start.22 = (bf16[256,1536]{1,0:T(8,128)(2,1)S(1)}, bf16[256,1536]{1,0:T(8,128)(2,1)S(1)}, u32[]{:S(2)}, u32[]{:S(2)}) collective-permute-start(bf16[256,1536]{1,0:T(8,128)(2,1)S(1)} %collective-permute-done.18.refs_2_), channel_id=1, source_target_pairs={{0,1},{1,0},{2,3},{3,2},{4,5},{5,4},{6,7},{7,6},{16,17},{17,16},{1... | collective-permute-start | bytes 2359304 | tf_op jit(solution)/shard_map/ppermute | solution.py:56
  158.5 6.7 %collective-permute-start.23 = (bf16[256,1536]{1,0:T(8,128)(2,1)S(1)}, bf16[256,1536]{1,0:T(8,128)(2,1)S(1)}, u32[]{:S(2)}, u32[]{:S(2)}) collective-permute-start(bf16[256,1536]{1,0:T(8,128)(2,1)S(1)} %collective-permute-done.19.refs_3_), channel_id=1, source_target_pairs={{0,1},{1,0},{2,3},{3,2},{4,5},{5,4},{6,7},{7,6},{16,17},{17,16},{1... | collective-permute-start | bytes 2359304 | tf_op jit(solution)/shard_map/ppermute | solution.py:56
  159.0 16.8 %collective-permute-start.26 = (bf16[352,1536]{1,0:T(8,128)(2,1)}, bf16[352,1536]{1,0:T(8,128)(2,1)}, u32[]{:S(2)}, u32[]{:S(2)}) collective-permute-start(bf16[352,1536]{1,0:T(8,128)(2,1)} %collective-permute-done.17.refs_1_), channel_id=1, source_target_pairs={{0,1},{1,0},{2,3},{3,2},{4,5},{5,4},{6,7},{7,6},{16,17},{17,16},{1... | collective-permute-start | bytes 3244040 | tf_op jit(solution)/shard_map/ppermute | solution.py:56
  159.9 15.7 %collective-permute-start.24 = (bf16[160,1536]{1,0:T(8,128)(2,1)}, bf16[160,1536]{1,0:T(8,128)(2,1)}, u32[]{:S(2)}, u32[]{:S(2)}) collective-permute-start(bf16[160,1536]{1,0:T(8,128)(2,1)} %slice.33), channel_id=1, source_target_pairs={{0,8},{1,9},{2,10},{3,11},{4,12},{5,13},{6,14},{7,15},{16,24},{17,... | collective-permute-start | bytes 1474568 | tf_op jit(solution)/shard_map/ppermute | solution.py:56
  171.9 16.7 %all-to-all-start.3 = ((bf16[8,128,384]{2,1,0:T(8,128)(2,1)}), bf16[8,128,384]{2,1,0:T(8,128)(2,1)S(1)}, u32[]{:S(2)}, u32[]{:S(2)}) async-start(bf16[8,128,384]{2,1,0:T(8,128)(2,1)} %copy-done.19), calls=%async_computation.3 | async-start | bytes 1572864 | tf_op jit(solution)/shard_map/all_to_all | solution.py:476
  175.6 2.2 %collective-permute-start.27 = (bf16[160,1536]{1,0:T(8,128)(2,1)}, bf16[160,1536]{1,0:T(8,128)(2,1)S(1)}, u32[]{:S(2)}, u32[]{:S(2)}) collective-permute-start(bf16[160,1536]{1,0:T(8,128)(2,1)} %collective-permute-done.24.refs_2_), channel_id=1, source_target_pairs={{0,1},{1,0},{2,3},{3,2},{4,5},{5,4},{6,7},{7,6},{16,17},{17,16},{1... | collective-permute-start | bytes 1474568 | tf_op jit(solution)/shard_map/ppermute | solution.py:56
  (30 other events, 144.2 us)
